TPU v7x, 32 devices: a whole 2x2x4 slice. The times are simulated.
32 devices in a mesh: cells: 8 (over z, y), states: 4 (over x, core).
Axes of the slice: x: 2, y: 2, z: 4, core: 2. Of those that a mesh axis runs over, the one named last changes fastest.
Arguments:
- filter_input: bfloat16 [5096, 512], P('cells', 'states'), may hold values from -4 to 4, as said below
- cell_table: bfloat16 [8, 343, 343], replicated, may hold values from -0.5 to 3.5, as said below
- cell_type: int32 [16], P('cells'), may hold values from 0 to 7
- atom_center: int32 [32], P('cells'), may hold values from 0 to 1, as said below
- proj_values: bfloat16 [32, 3, 16, 343], P('cells'), may hold values from -0.3125 to 0.3125
- coupling: float32 [16, 16], replicated, may hold values from -1.5 to 1.5
- occupation: float32 [512], P('states'), may hold values from 0.25 to 4
Outputs:
- filtered: float32 [5096, 512], P('cells', 'states')
- density: float32 [5096], P('cells')
Inputs may be any that keep to these rules, and one draw needn't show every extreme that they name: `filter_input`: rows that stand for the same node on two blocks hold the same values. `cell_table`: each of the 8 matrices is symmetric. `atom_center`: in each block of 4 atoms of one owner, at least one atom sits on cell 0 and at least one on cell 1.
All inputs are finite; a program needn't handle non-finite values.
Results may differ from a plain program's by a relative error of at most 0.0027.
Values may be sent and summed in bfloat16 or wider, within the bound.
No kernel may reach another device: no remote copies, remote signals or barrier semaphores. Data moves between devices by JAX's collectives and lax.ppermute only.
A program may use at most 64 MiB of HBM per device.

v0:
```python
import jax
import jax.numpy as jnp
from jax import lax
from jax.sharding import PartitionSpec as P

PROJECTORS = 16
STEPS = 3
FACE = 49
CELL_NODES = 343
STRIDE = 294


lower_edge = 4.0
upper_edge = 12.0
ground_edge = -2.0


def with_halo(shard, sides, width):
    for axis, dim in sides:
        peers, length = (lax.axis_size(axis), shard.shape[dim])
        up = [(i, (i + 1) % peers) for i in range(peers)]
        down = [(j, i) for i, j in up]
        last = lax.slice_in_dim(shard, length - width, length, axis=dim)
        initial = lax.slice_in_dim(shard, 0, width, axis=dim)
        before = lax.ppermute(last, axis, up)
        after = lax.ppermute(initial, axis, down)
        shard = jnp.concatenate([before, shard, after], axis=dim)
    return shard


def split_cells(node_block):
    tile_count = (node_block.shape[0] - FACE) // STRIDE
    columns = node_block.shape[1]
    head_rows = node_block[: tile_count * STRIDE].reshape(tile_count, STRIDE, columns)
    padded = jnp.pad(node_block, ((0, STRIDE - FACE), (0, 0)))
    face_rows = padded[STRIDE : STRIDE + tile_count * STRIDE].reshape(tile_count, STRIDE, columns)[
        :, :FACE
    ]
    return jnp.concatenate([head_rows, face_rows], axis=1)


def join_cells(cell_tiles):
    tile_count = cell_tiles.shape[0]
    columns = cell_tiles.shape[2]
    head_rows = cell_tiles[:, :STRIDE].reshape(tile_count * STRIDE, columns)
    tail_rows = jnp.pad(cell_tiles[:, STRIDE:], ((0, 0), (0, STRIDE - FACE), (0, 0))).reshape(
        tile_count * STRIDE, columns
    )
    return (
        jnp.pad(head_rows, ((0, FACE), (0, 0)))
        + jnp.pad(tail_rows, ((STRIDE, 0), (0, 0)))[: tile_count * STRIDE + FACE]
    )


def body(filter_input, cell_table, cell_type, atom_center, proj_values, coupling, occupation):
    cell_count = cell_type.shape[0]
    atom_count = atom_center.shape[0]
    states_local = filter_input.shape[1]
    node_rows = filter_input.shape[0]
    coef_rows = atom_count * PROJECTORS
    matrices = jnp.take(cell_table, cell_type, axis=0)
    picks = atom_center[:, None] + jnp.arange(3, dtype=jnp.int32)[None, :]
    onehot = (
        picks[:, :, None] == jnp.arange(cell_count + 2, dtype=jnp.int32)[None, None, :]
    ).astype(jnp.float32)
    beta_cells = jnp.einsum(
        "ajk,ajpr->kapr", onehot, proj_values.astype(jnp.float32), precision=lax.Precision.HIGHEST
    )
    beta_cells = beta_cells.reshape(cell_count + 2, coef_rows, CELL_NODES).astype(jnp.bfloat16)

    def apply_h(current):
        rounded = current.astype(jnp.bfloat16)
        x_rims = with_halo(rounded[FACE:-FACE], (("cells", 0),), STRIDE)
        extended = jnp.concatenate([x_rims[:STRIDE], rounded, x_rims[-STRIDE:]], axis=0)
        ext_tiles = split_cells(extended)
        cell_terms = jnp.einsum(
            "cij,cjs->cis", matrices, ext_tiles[1:-1], preferred_element_type=jnp.float32
        )
        coeffs = jnp.einsum(
            "kqr,krs->qs", beta_cells, ext_tiles, preferred_element_type=jnp.float32
        )
        weighted = jnp.einsum(
            "pq,aqs->aps",
            coupling,
            coeffs.reshape(atom_count, PROJECTORS, states_local),
            precision=lax.Precision.HIGHEST,
        )
        flat_weighted = weighted.astype(jnp.bfloat16).reshape(coef_rows, states_local)
        spread = jnp.einsum(
            "kqr,qs->krs", beta_cells, flat_weighted, preferred_element_type=jnp.float32
        )
        summed = join_cells(spread + jnp.pad(cell_terms, ((1, 1), (0, 0), (0, 0))))
        outer_rows = with_halo(summed, (("cells", 0),), CELL_NODES)
        mine_rows = summed[STRIDE : STRIDE + node_rows]
        lower_part = jnp.pad(outer_rows[:CELL_NODES], ((0, node_rows - CELL_NODES), (0, 0)))
        upper_part = jnp.pad(outer_rows[-CELL_NODES:], ((node_rows - CELL_NODES, 0), (0, 0)))
        return mine_rows + lower_part + upper_part

    half_width = (upper_edge - lower_edge) / 2.0
    centre = (upper_edge + lower_edge) / 2.0
    scale_now = half_width / (ground_edge - centre)
    twice_inverse = 2.0 / scale_now
    previous = filter_input.astype(jnp.float32)
    current = (apply_h(previous) - centre * previous) * (scale_now / half_width)
    for repeat in range(STEPS - 1):
        scale_next = 1.0 / (twice_inverse - scale_now)
        image = apply_h(current)
        upcoming = (image - centre * current) * (
            2.0 * scale_next / half_width
        ) - scale_now * scale_next * previous
        previous, current = (current, upcoming)
        scale_now = scale_next
    squares = jnp.sum(current * current * occupation[None, :], axis=1) / (
        states_local * lax.axis_size("states")
    )
    density = lax.psum(squares, "states")
    return (current, density)


def solution(mesh):
    in_specs = (
        P("cells", "states"),
        P(),
        P("cells"),
        P("cells"),
        P("cells", None, None, None),
        P(),
        P("states"),
    )
    out_specs = (P("cells", "states"), P("cells"))
    return jax.shard_map(body, mesh=mesh, in_specs=in_specs, out_specs=out_specs, check_vma=False)
```

profile of v0, /device:TPU:0, one launch (start us, length us, event | category | flops | bytes accessed | tf_op | source)
XLA Modules:
  0.0 109.0 jit_solution(10207504196476106833)
XLA Ops:
  0.6 1.1 %fusion.70 = (bf16[294,128]{1,0:T(8,128)(2,1)S(1)}, bf16[294,128]{1,0:T(8,128)(2,1)S(1)}) fusion(bf16[637,128]{1,0:T(8,128)(2,1)} %param.7), kind=kLoop, calls=%fused_computation.101 | loop fusion | bytes 301056 | tf_op jit(solution)/shard_map/slice | solution.py:24
  1.8 6.1 %collective-permute-start.1 = (bf16[294,128]{1,0:T(8,128)(2,1)S(1)}, bf16[294,128]{1,0:T(8,128)(2,1)S(1)}, u32[]{:S(2)}, u32[]{:S(2)}) collective-permute-start(bf16[294,128]{1,0:T(8,128)(2,1)S(1)} %get-tuple-element.22), channel_id=1, source_target_pairs={{4,0},{8,4},{12,8},{16,12},{20,16},{24,20},{28,24},{0,28},{5,1},{9... | collective-permute-start | bytes 225800 | tf_op jit(solution)/shard_map/ppermute | solution.py:26
  7.8 0.7 compare_and_fusion
  8.5 0.7 compare_select_fusion
  9.1 0.7 iota_add_fusion
  9.9 4.6 %gather_fusion = bf16[2,343,343]{2,0,1:T(2,128)(2,1)S(1)} fusion(bf16[8,343,343]{2,0,1:T(8,128)(2,1)S(1)} %copy-done, s32[1024]{0:T(1024)S(1)} %pad_clamp_fusion), kind=kCustom, calls=%fused_computation | custom fusion | bytes 941200 | tf_op jit(solution)/shard_map/jit(_take)/gather | solution.py:61
  14.6 1.4 %broadcast_select_fusion = bf16[2,343,343]{2,0,1:T(2,128)(2,1)} fusion(bf16[2,343,343]{2,0,1:T(2,128)(2,1)S(1)} %gather_fusion, pred[2]{0:T(512)(128)(4,1)S(1)} %compare_and_fusion), kind=kLoop, calls=%fused_computation.17 | loop fusion | flops 235298 | bytes 941194 | tf_op jit(solution)/shard_map/jit(_take)/select_n | solution.py:61
  16.0 0.9 convolution_convert_fusion
  16.9 1.0 concatenate.18
  17.9 0.1 fusion.67
  18.0 0.1 reshape.81
  18.1 0.1 reshape.82
  18.2 1.2 %convolution_bitcast_fusion.5 = f32[4,16,128]{2,1,0:T(8,128)S(1)} fusion(bf16[4,49,128]{2,1,0:T(8,128)(2,1)S(1)} %slice.156, bf16[4,294,128]{2,1,0:T(8,128)(2,1)S(1)} %reshape.81, bf16[4,16,4,343]{3,2,1,0:T(4,128)(2,1)} %bitcast.70), kind=kOutput, calls=%fused_computation.10 | convolution fusion | flops 23181312 | bytes 559616 | tf_op jit(solution)/shard_map/kqr,krs->qs/dot_general | solution.py:79
  19.4 1.4 %fusion.13 = f32[2,343,128]{2,1,0:T(8,128)S(1)} fusion(bf16[2,343,343]{2,0,1:T(2,128)(2,1)} %broadcast_select_fusion, bf16[4,294,128]{2,1,0:T(8,128)(2,1)S(1)} %reshape.81, bf16[4,49,128]{2,1,0:T(8,128)(2,1)S(1)} %slice.156), kind=kOutput, calls=%fused_computation.36 | convolution fusion | flops 60587520 | bytes 1173060 | tf_op jit(solution)/shard_map/cij,cjs->cis/dot_general | solution.py:76
  20.8 0.2 fusion.3
  20.9 1.3 %fusion = f32[4,343,128]{2,1,0:T(8,128)S(1)} fusion(bf16[4,16,128,1]{2,1,0,3:T(8,128)(2,1)S(1)} %fusion.3, f32[2,343,128]{2,1,0:T(8,128)S(1)} %fusion.13, bf16[4,4,16,343]{3,0,2,1:T(4,128)(2,1)} %bitcast.71), kind=kOutput, calls=%fused_computation.4 | convolution fusion | flops 22654464 | bytes 1245696 | tf_op jit(solution)/shard_map/kqr,qs->krs/dot_general | solution.py:89
  22.3 0.9 reshape.83
  23.2 0.9 reshape.84
  24.1 1.3 %fusion.6 = f32[1225,128]{1,0:T(8,128)S(1)} fusion(f32[1176,128]{1,0:T(8,128)} %reshape.84, f32[1176,128]{1,0:T(8,128)} %reshape.83), kind=kLoop, calls=%fused_computation.21 | loop fusion | flops 156800 | bytes 1831424 | tf_op jit(solution)/shard_map/add | solution.py:50
  25.4 0.1 collective-permute-start.2
  25.5 4.8 %collective-permute-start.3 = (f32[343,128]{1,0:T(8,128)S(1)}, f32[343,128]{1,0:T(8,128)S(1)}, u32[]{:S(2)}, u32[]{:S(2)}) collective-permute-start(f32[343,128]{1,0:T(8,128)S(1)} %get-tuple-element.11), channel_id=1, source_target_pairs={{4,0},{8,4},{12,8},{16,12},{20,16},{24,20},{28,24},{0,28},{5,1},{9... | collective-permute-start | bytes 526856 | tf_op jit(solution)/shard_map/ppermute | solution.py:26
  30.3 3.9 %collective-permute-done.2 = f32[343,128]{1,0:T(8,128)S(1)} collective-permute-done((f32[343,128]{1,0:T(8,128)S(1)}, f32[343,128]{1,0:T(8,128)S(1)}, u32[]{:S(2)}, u32[]{:S(2)}) %collective-permute-start.2) | collective-permute-done | bytes 175648 | tf_op jit(solution)/shard_map/ppermute | solution.py:25
  34.2 1.0 collective-permute-done.3
  35.2 0.1 multiply_convert_fusion
  35.4 4.4 %collective-permute-start.5 = (bf16[294,128]{1,0:T(8,128)(2,1)S(1)}, bf16[294,128]{1,0:T(8,128)(2,1)S(1)}, u32[]{:S(2)}, u32[]{:S(2)}) collective-permute-start(bf16[294,128]{1,0:T(8,128)(2,1)S(1)} %get-tuple-element.20), channel_id=1, source_target_pairs={{4,0},{8,4},{12,8},{16,12},{20,16},{24,20},{28,24},{0,28},{5,1},{9... | collective-permute-start | bytes 225800 | tf_op jit(solution)/shard_map/ppermute | solution.py:26
  39.8 2.0 %collective-permute-done.5 = bf16[294,128]{1,0:T(8,128)(2,1)S(1)} collective-permute-done((bf16[294,128]{1,0:T(8,128)(2,1)S(1)}, bf16[294,128]{1,0:T(8,128)(2,1)S(1)}, u32[]{:S(2)}, u32[]{:S(2)}) %collective-permute-start.5) | collective-permute-done | bytes 75296 | tf_op jit(solution)/shard_map/ppermute | solution.py:26
  41.8 5.1 %collective-permute-done.4 = bf16[294,128]{1,0:T(8,128)(2,1)S(1)} collective-permute-done((bf16[294,128]{1,0:T(8,128)(2,1)S(1)}, bf16[294,128]{1,0:T(8,128)(2,1)S(1)}, u32[]{:S(2)}, u32[]{:S(2)}) %collective-permute-start.4) | collective-permute-done | bytes 75296 | tf_op jit(solution)/shard_map/ppermute | solution.py:25
  46.9 1.0 concatenate.20
  47.9 0.1 fusion.66
  48.0 0.8 reshape.85
  48.8 0.1 reshape.86
  48.9 1.3 %convolution_bitcast_fusion.4 = f32[4,16,128]{2,1,0:T(8,128)S(1)} fusion(bf16[4,49,128]{2,1,0:T(8,128)(2,1)S(1)} %slice.167, bf16[4,294,128]{2,1,0:T(8,128)(2,1)} %reshape.85, bf16[4,16,4,343]{3,2,1,0:T(4,128)(2,1)} %bitcast.72), kind=kOutput, calls=%fused_computation.9 | convolution fusion | flops 23181312 | bytes 559616 | tf_op jit(solution)/shard_map/kqr,krs->qs/dot_general | solution.py:79
  50.2 1.4 %fusion.11 = f32[2,343,128]{2,1,0:T(8,128)S(1)} fusion(bf16[2,343,343]{2,0,1:T(2,128)(2,1)} %broadcast_select_fusion, bf16[4,294,128]{2,1,0:T(8,128)(2,1)} %reshape.85, bf16[4,49,128]{2,1,0:T(8,128)(2,1)S(1)} %slice.167), kind=kOutput, calls=%fused_computation.34 | convolution fusion | flops 60587520 | bytes 1173060 | tf_op jit(solution)/shard_map/cij,cjs->cis/dot_general | solution.py:76
  51.6 0.2 fusion.4
  51.8 1.3 %fusion.1 = f32[4,343,128]{2,1,0:T(8,128)S(1)} fusion(bf16[4,16,128,1]{2,1,0,3:T(8,128)(2,1)S(1)} %fusion.4, f32[2,343,128]{2,1,0:T(8,128)S(1)} %fusion.11, bf16[4,4,16,343]{3,0,2,1:T(4,128)(2,1)} %bitcast.73), kind=kOutput, calls=%fused_computation.5 | convolution fusion | flops 22654464 | bytes 1245696 | tf_op jit(solution)/shard_map/kqr,qs->krs/dot_general | solution.py:89
  53.2 0.9 reshape.87
  54.1 0.9 reshape.88
  55.0 1.3 %fusion.7 = f32[1225,128]{1,0:T(8,128)S(1)} fusion(f32[1176,128]{1,0:T(8,128)} %reshape.88, f32[1176,128]{1,0:T(8,128)} %reshape.87), kind=kLoop, calls=%fused_computation.22 | loop fusion | flops 156800 | bytes 1831424 | tf_op jit(solution)/shard_map/add | solution.py:50
  56.3 0.1 collective-permute-start.6
  56.3 4.7 %collective-permute-start.7 = (f32[343,128]{1,0:T(8,128)S(1)}, f32[343,128]{1,0:T(8,128)S(1)}, u32[]{:S(2)}, u32[]{:S(2)}) collective-permute-start(f32[343,128]{1,0:T(8,128)S(1)} %get-tuple-element.9), channel_id=1, source_target_pairs={{4,0},{8,4},{12,8},{16,12},{20,16},{24,20},{28,24},{0,28},{5,1},{9... | collective-permute-start | bytes 526856 | tf_op jit(solution)/shard_map/ppermute | solution.py:26
  61.0 3.5 %collective-permute-done.6 = f32[343,128]{1,0:T(8,128)S(1)} collective-permute-done((f32[343,128]{1,0:T(8,128)S(1)}, f32[343,128]{1,0:T(8,128)S(1)}, u32[]{:S(2)}, u32[]{:S(2)}) %collective-permute-start.6) | collective-permute-done | bytes 175648 | tf_op jit(solution)/shard_map/ppermute | solution.py:25
  64.6 0.1 fusion.59
  64.8 4.7 %collective-permute-start.9 = (bf16[294,128]{1,0:T(8,128)(2,1)S(1)}, bf16[294,128]{1,0:T(8,128)(2,1)S(1)}, u32[]{:S(2)}, u32[]{:S(2)}) collective-permute-start(bf16[294,128]{1,0:T(8,128)(2,1)S(1)} %get-tuple-element.18), channel_id=1, source_target_pairs={{4,0},{8,4},{12,8},{16,12},{20,16},{24,20},{28,24},{0,28},{5,1},{9... | collective-permute-start | bytes 225800 | tf_op jit(solution)/shard_map/ppermute | solution.py:26
  69.5 2.0 %collective-permute-done.9 = bf16[294,128]{1,0:T(8,128)(2,1)S(1)} collective-permute-done((bf16[294,128]{1,0:T(8,128)(2,1)S(1)}, bf16[294,128]{1,0:T(8,128)(2,1)S(1)}, u32[]{:S(2)}, u32[]{:S(2)}) %collective-permute-start.9) | collective-permute-done | bytes 75296 | tf_op jit(solution)/shard_map/ppermute | solution.py:26
  71.5 0.6 copy-done.7
  72.2 4.5 %collective-permute-done.8 = bf16[294,128]{1,0:T(8,128)(2,1)} collective-permute-done((bf16[294,128]{1,0:T(8,128)(2,1)S(1)}, bf16[294,128]{1,0:T(8,128)(2,1)}, u32[]{:S(2)}, u32[]{:S(2)}) %collective-permute-start.8) | collective-permute-done | bytes 75296 | tf_op jit(solution)/shard_map/ppermute | solution.py:25
  76.7 2.9 %concatenate.22 = bf16[1225,128]{1,0:T(8,128)(2,1)S(1)} concatenate(bf16[294,128]{1,0:T(8,128)(2,1)} %collective-permute-done.8, bf16[637,128]{1,0:T(8,128)(2,1)} %copy-done.2, bf16[294,128]{1,0:T(8,128)(2,1)} %copy-done.7), dimensions={0} | concatenate | bytes 627200 | tf_op jit(solution)/shard_map/concatenate | solution.py:74
  79.6 0.9 fusion.65
  80.5 1.8 %reshape.89 = bf16[4,294,128]{2,1,0:T(8,128)(2,1)} reshape(bf16[1176,128]{1,0:T(8,128)(2,1)} %get-tuple-element.12) | data formatting | bytes 602112 | tf_op jit(solution)/shard_map/reshape | solution.py:34
  82.2 1.0 reshape.90
  83.3 1.4 %fusion.9 = f32[2,343,128]{2,1,0:T(8,128)S(1)} fusion(bf16[2,343,343]{2,0,1:T(2,128)(2,1)} %broadcast_select_fusion, bf16[4,294,128]{2,1,0:T(8,128)(2,1)} %reshape.89, bf16[4,49,128]{2,1,0:T(8,128)(2,1)S(1)} %slice.178), kind=kOutput, calls=%fused_computation.32 | convolution fusion | flops 60587520 | bytes 1173060 | tf_op jit(solution)/shard_map/cij,cjs->cis/dot_general | solution.py:76
  84.7 1.3 %convolution_bitcast_fusion.3 = f32[4,16,128]{2,1,0:T(8,128)S(1)} fusion(bf16[4,49,128]{2,1,0:T(8,128)(2,1)S(1)} %slice.178, bf16[4,294,128]{2,1,0:T(8,128)(2,1)} %reshape.89, bf16[4,16,4,343]{3,2,1,0:T(4,128)(2,1)} %bitcast.74), kind=kOutput, calls=%fused_computation.8 | convolution fusion | flops 23181312 | bytes 559616 | tf_op jit(solution)/shard_map/kqr,krs->qs/dot_general | solution.py:79
  86.1 0.2 fusion.5
  86.2 0.4 fusion.2
  86.6 0.9 slice.181
  87.5 1.9 %reshape.91 = f32[1176,128]{1,0:T(8,128)} reshape(f32[4,294,128]{2,1,0:T(8,128)} %slice.181) | data formatting | bytes 1204224 | tf_op jit(solution)/shard_map/reshape | solution.py:45
  89.5 0.9 pad.87
  90.3 1.9 %reshape.92 = f32[1176,128]{1,0:T(8,128)} reshape(f32[4,294,128]{2,1,0:T(8,128)} %pad.87) | data formatting | bytes 1204224 | tf_op jit(solution)/shard_map/reshape | solution.py:46
  92.2 1.3 %fusion.8 = f32[1225,128]{1,0:T(8,128)S(1)} fusion(f32[1176,128]{1,0:T(8,128)} %reshape.92, f32[1176,128]{1,0:T(8,128)} %reshape.91), kind=kLoop, calls=%fused_computation.23 | loop fusion | flops 156800 | bytes 1831424 | tf_op jit(solution)/shard_map/add | solution.py:50
  93.6 0.1 collective-permute-start.10
  93.7 4.7 %collective-permute-start.11 = (f32[343,128]{1,0:T(8,128)S(1)}, f32[343,128]{1,0:T(8,128)S(1)}, u32[]{:S(2)}, u32[]{:S(2)}) collective-permute-start(f32[343,128]{1,0:T(8,128)S(1)} %get-tuple-element.7), channel_id=1, source_target_pairs={{4,0},{8,4},{12,8},{16,12},{20,16},{24,20},{28,24},{0,28},{5,1},{9... | collective-permute-start | bytes 526856 | tf_op jit(solution)/shard_map/ppermute | solution.py:26
  98.4 3.4 %collective-permute-done.10 = f32[343,128]{1,0:T(8,128)S(1)} collective-permute-done((f32[343,128]{1,0:T(8,128)S(1)}, f32[343,128]{1,0:T(8,128)S(1)}, u32[]{:S(2)}, u32[]{:S(2)}) %collective-permute-start.10) | collective-permute-done | bytes 175648 | tf_op jit(solution)/shard_map/ppermute | solution.py:25
  101.8 1.0 multiply_reduce_fusion
  102.8 6.2 %psum.7 = f32[637]{0:T(1024)} all-reduce(f32[637]{0:T(1024)S(1)} %broadcast_multiply_fusion), channel_id=1, replica_groups=mesh['cells'=8,'states'=4] {'states'}, use_global_device_ids=true, to_apply=%region_1.2 | all-reduce | flops 637 | bytes 5096 | tf_op jit(solution)/shard_map/psum | solution.py:116
  (47 shorter events, 0.5 us)
Async XLA Ops:
  0.6 9.2 %copy-start = (bf16[8,343,343]{2,0,1:T(8,128)(2,1)S(1)}, bf16[8,343,343]{2,0,1:T(8,128)(2,1)}, u32[]{:S(2)}) copy-start(bf16[8,343,343]{2,0,1:T(8,128)(2,1)} %param.8) | copy-start | bytes 5647156
  1.8 15.1 %collective-permute-start.1 = (bf16[294,128]{1,0:T(8,128)(2,1)S(1)}, bf16[294,128]{1,0:T(8,128)(2,1)S(1)}, u32[]{:S(2)}, u32[]{:S(2)}) collective-permute-start(bf16[294,128]{1,0:T(8,128)(2,1)S(1)} %get-tuple-element.22), channel_id=1, source_target_pairs={{4,0},{8,4},{12,8},{16,12},{20,16},{24,20},{28,24},{0,28},{5,1},{9... | collective-permute-start | bytes 225800 | tf_op jit(solution)/shard_map/ppermute | solution.py:26
  7.8 9.1 %collective-permute-start = (bf16[294,128]{1,0:T(8,128)(2,1)S(1)}, bf16[294,128]{1,0:T(8,128)(2,1)S(1)}, u32[]{:S(2)}, u32[]{:S(2)}) collective-permute-start(bf16[294,128]{1,0:T(8,128)(2,1)S(1)} %get-tuple-element.23), channel_id=1, source_target_pairs={{0,4},{4,8},{8,12},{12,16},{16,20},{20,24},{24,28},{28,0},{1,5},{5... | collective-permute-start | bytes 225800 | tf_op jit(solution)/shard_map/ppermute | solution.py:25
  9.9 6.1 %copy-start.10 = (bf16[4,3,16,343]{3,2,1,0:T(8,128)(2,1)S(1)}, bf16[4,3,16,343]{3,2,1,0:T(8,128)(2,1)}, u32[]{:S(2)}) copy-start(bf16[4,3,16,343]{3,2,1,0:T(8,128)(2,1)} %param.11) | copy-start | bytes 395140
  9.9 7.0 %copy-start.1 = (bf16[637,128]{1,0:T(8,128)(2,1)S(1)}, bf16[637,128]{1,0:T(8,128)(2,1)}, u32[]{:S(2)}) copy-start(bf16[637,128]{1,0:T(8,128)(2,1)} %param.7) | copy-start | bytes 489220
  17.9 2.9 %copy-start.8 = (f32[16,16]{1,0:T(8,128)S(1)}, f32[16,16]{1,0:T(8,128)}, u32[]{:S(2)}) copy-start(f32[16,16]{1,0:T(8,128)} %param.12) | copy-start | bytes 3076
  25.4 8.8 %collective-permute-start.2 = (f32[343,128]{1,0:T(8,128)S(1)}, f32[343,128]{1,0:T(8,128)S(1)}, u32[]{:S(2)}, u32[]{:S(2)}) collective-permute-start(f32[343,128]{1,0:T(8,128)S(1)} %get-tuple-element.10), channel_id=1, source_target_pairs={{0,4},{4,8},{8,12},{12,16},{16,20},{20,24},{24,28},{28,0},{1,5},{5... | collective-permute-start | bytes 526856 | tf_op jit(solution)/shard_map/ppermute | solution.py:25
  25.5 9.7 %collective-permute-start.3 = (f32[343,128]{1,0:T(8,128)S(1)}, f32[343,128]{1,0:T(8,128)S(1)}, u32[]{:S(2)}, u32[]{:S(2)}) collective-permute-start(f32[343,128]{1,0:T(8,128)S(1)} %get-tuple-element.11), channel_id=1, source_target_pairs={{4,0},{8,4},{12,8},{16,12},{20,16},{24,20},{28,24},{0,28},{5,1},{9... | collective-permute-start | bytes 526856 | tf_op jit(solution)/shard_map/ppermute | solution.py:26
  35.4 6.4 %collective-permute-start.5 = (bf16[294,128]{1,0:T(8,128)(2,1)S(1)}, bf16[294,128]{1,0:T(8,128)(2,1)S(1)}, u32[]{:S(2)}, u32[]{:S(2)}) collective-permute-start(bf16[294,128]{1,0:T(8,128)(2,1)S(1)} %get-tuple-element.20), channel_id=1, source_target_pairs={{4,0},{8,4},{12,8},{16,12},{20,16},{24,20},{28,24},{0,28},{5,1},{9... | collective-permute-start | bytes 225800 | tf_op jit(solution)/shard_map/ppermute | solution.py:26
  39.8 7.1 %collective-permute-start.4 = (bf16[294,128]{1,0:T(8,128)(2,1)S(1)}, bf16[294,128]{1,0:T(8,128)(2,1)S(1)}, u32[]{:S(2)}, u32[]{:S(2)}) collective-permute-start(bf16[294,128]{1,0:T(8,128)(2,1)S(1)} %get-tuple-element.21), channel_id=1, source_target_pairs={{0,4},{4,8},{8,12},{12,16},{16,20},{20,24},{24,28},{28,0},{1,5},{5... | collective-permute-start | bytes 225800 | tf_op jit(solution)/shard_map/ppermute | solution.py:25
  56.3 8.3 %collective-permute-start.6 = (f32[343,128]{1,0:T(8,128)S(1)}, f32[343,128]{1,0:T(8,128)S(1)}, u32[]{:S(2)}, u32[]{:S(2)}) collective-permute-start(f32[343,128]{1,0:T(8,128)S(1)} %get-tuple-element.8), channel_id=1, source_target_pairs={{0,4},{4,8},{8,12},{12,16},{16,20},{20,24},{24,28},{28,0},{1,5},{5... | collective-permute-start | bytes 526856 | tf_op jit(solution)/shard_map/ppermute | solution.py:25
  56.3 8.2 %collective-permute-start.7 = (f32[343,128]{1,0:T(8,128)S(1)}, f32[343,128]{1,0:T(8,128)S(1)}, u32[]{:S(2)}, u32[]{:S(2)}) collective-permute-start(f32[343,128]{1,0:T(8,128)S(1)} %get-tuple-element.9), channel_id=1, source_target_pairs={{4,0},{8,4},{12,8},{16,12},{20,16},{24,20},{28,24},{0,28},{5,1},{9... | collective-permute-start | bytes 526856 | tf_op jit(solution)/shard_map/ppermute | solution.py:26
  64.6 6.9 %copy-start.3 = (f32[343,128]{1,0:T(8,128)}, f32[343,128]{1,0:T(8,128)S(1)}, u32[]{:S(2)}) copy-start(f32[343,128]{1,0:T(8,128)S(1)} %collective-permute-done.6) | copy-start | bytes 526852
  64.6 6.9 %copy-start.5 = (f32[343,128]{1,0:T(8,128)}, f32[343,128]{1,0:T(8,128)S(1)}, u32[]{:S(2)}) copy-start(f32[343,128]{1,0:T(8,128)S(1)} %collective-permute-done.7) | copy-start | bytes 526852
  64.7 6.8 %copy-start.2 = (bf16[637,128]{1,0:T(8,128)(2,1)}, bf16[637,128]{1,0:T(8,128)(2,1)S(1)}, u32[]{:S(2)}) copy-start(bf16[637,128]{1,0:T(8,128)(2,1)S(1)} %fusion.59) | copy-start | bytes 489220
  64.8 6.7 %collective-permute-start.9 = (bf16[294,128]{1,0:T(8,128)(2,1)S(1)}, bf16[294,128]{1,0:T(8,128)(2,1)S(1)}, u32[]{:S(2)}, u32[]{:S(2)}) collective-permute-start(bf16[294,128]{1,0:T(8,128)(2,1)S(1)} %get-tuple-element.18), channel_id=1, source_target_pairs={{4,0},{8,4},{12,8},{16,12},{20,16},{24,20},{28,24},{0,28},{5,1},{9... | collective-permute-start | bytes 225800 | tf_op jit(solution)/shard_map/ppermute | solution.py:26
  69.5 7.2 %collective-permute-start.8 = (bf16[294,128]{1,0:T(8,128)(2,1)S(1)}, bf16[294,128]{1,0:T(8,128)(2,1)}, u32[]{:S(2)}, u32[]{:S(2)}) collective-permute-start(bf16[294,128]{1,0:T(8,128)(2,1)S(1)} %get-tuple-element.19), channel_id=1, source_target_pairs={{0,4},{4,8},{8,12},{12,16},{16,20},{20,24},{24,28},{28,0},{1,5},{5... | collective-permute-start | bytes 225800 | tf_op jit(solution)/shard_map/ppermute | solution.py:25
  71.5 0.6 copy-start.7
  83.3 3.0 %copy-start.11 = (bf16[4,4,16,343]{3,1,2,0:T(4,128)(2,1)S(1)}, bf16[4,4,16,343]{3,1,2,0:T(4,128)(2,1)}, u32[]{:S(2)}) copy-start(bf16[4,4,16,343]{3,1,2,0:T(4,128)(2,1)} %convolution_convert_fusion) | copy-start | bytes 526852
  89.5 12.3 %copy-start.4 = (f32[343,128]{1,0:T(8,128)S(1)}, f32[343,128]{1,0:T(8,128)}, u32[]{:S(2)}) copy-start(f32[343,128]{1,0:T(8,128)} %copy-done.3) | copy-start | bytes 526852
  89.5 12.4 %copy-start.9 = (f32[128]{0:T(128)S(1)}, f32[128]{0:T(128)}, u32[]{:S(2)}) copy-start(f32[128]{0:T(128)} %param.13) | copy-start | bytes 1540
  92.2 9.6 %copy-start.6 = (f32[343,128]{1,0:T(8,128)S(1)}, f32[343,128]{1,0:T(8,128)}, u32[]{:S(2)}) copy-start(f32[343,128]{1,0:T(8,128)} %copy-done.5) | copy-start | bytes 526852
  93.6 8.2 %collective-permute-start.10 = (f32[343,128]{1,0:T(8,128)S(1)}, f32[343,128]{1,0:T(8,128)S(1)}, u32[]{:S(2)}, u32[]{:S(2)}) collective-permute-start(f32[343,128]{1,0:T(8,128)S(1)} %get-tuple-element.6), channel_id=1, source_target_pairs={{0,4},{4,8},{8,12},{12,16},{16,20},{20,24},{24,28},{28,0},{1,5},{5... | collective-permute-start | bytes 526856 | tf_op jit(solution)/shard_map/ppermute | solution.py:25
  93.7 8.1 %collective-permute-start.11 = (f32[343,128]{1,0:T(8,128)S(1)}, f32[343,128]{1,0:T(8,128)S(1)}, u32[]{:S(2)}, u32[]{:S(2)}) collective-permute-start(f32[343,128]{1,0:T(8,128)S(1)} %get-tuple-element.7), channel_id=1, source_target_pairs={{4,0},{8,4},{12,8},{16,12},{20,16},{24,20},{28,24},{0,28},{5,1},{9... | collective-permute-start | bytes 526856 | tf_op jit(solution)/shard_map/ppermute | solution.py:26
where the time goes:
time: 110 us; the launch traced here: 109 us
  starting transfers between devices  29.6 us (27%)
  local copies, waits for them, and re-layouts  25.7 us (23%)
  waiting for transfers between devices  25.5 us (23%)
  matrix products  12.4 us (11%)
  other arithmetic  8.51 us (8%)
  blocking collectives  6.22 us (6%)
    ppermute x6, starting transfers between devices, with_halo(): after = lax.ppermute(initial, axis, down)  29.4 us
    ppermute x6, waiting for transfers between devices, with_halo(): before = lax.ppermute(last, axis, up)  20.5 us
    psum x1, blocking collectives, body(): density = lax.psum(squares, 'states')  6.22 us
    ppermute x6, waiting for transfers between devices, with_halo(): after = lax.ppermute(initial, axis, down)  5.04 us
    concatenate x3, local copies, waits for them, and re-layouts, apply_h(): jnp.concatenate([x_rims[:STRIDE], rounded, x_rims[-STRIDE:]], axis=0)  4.85 us
    gather x1, local copies, waits for them, and re-layouts, body(): matrices = jnp.take(cell_table, cell_type, axis=0)  4.65 us
    dot_general x3, matrix products, apply_h(): jnp.einsum('cij,cjs->cis', matrices, ext_tiles[1:-1], preferred_element_t...  4.23 us
    add x3, other arithmetic, join_cells(): jnp.pad(head_rows, ((0, FACE), (0, 0)))  3.86 us
  transfers between devices with their start and end apart: 12, of which 8 were waited for; matrix products, arithmetic and copies ran while one was open for 8% of the time, Pallas kernels for 0%

commit v1 on v0

v1 whole, which is shorter than its diff:
```python
import functools

import jax
import jax.numpy as jnp
from jax import lax
from jax.experimental import pallas as pl
from jax.experimental.pallas import tpu as pltpu
from jax.sharding import PartitionSpec as P

STEPS = 3
LANES = 128
ROWS16 = 16

lower_edge = 4.0
upper_edge = 12.0
ground_edge = -2.0

F32 = jnp.float32
BF16 = jnp.bfloat16


def up16(n):
    return -(-n // ROWS16) * ROWS16


def down16(n):
    return n // ROWS16 * ROWS16


class Sizes:
    def __init__(self, node_rows, cells, cell_nodes, atoms, projectors):
        self.rows = node_rows
        self.nodes = cell_nodes
        self.stride = (node_rows - cell_nodes) // (cells - 1)
        self.face = cell_nodes - self.stride
        self.last = node_rows - cell_nodes
        self.end = node_rows - self.face
        self.atoms = atoms
        self.proj = projectors
        self.coef = atoms * projectors
        self.chunks = -(-cell_nodes // LANES)
        self.tail = cell_nodes - (self.chunks - 1) * LANES
        self.shift = self.stride - (self.chunks - 1) * LANES
        self.m_face = self.chunks * self.coef
        self.m_coef = self.m_face + self.coef
        self.m_rows = self.m_coef + self.coef
        self.right_lo, self.right_hi = down16(self.last), up16(self.end)
        self.left_lo, self.left_hi = down16(self.face), up16(cell_nodes)
        self.halo = max(self.right_hi - self.right_lo, self.left_hi - self.left_lo)
        self.first = self.m_rows + self.halo
        self.pad_face = up16(self.face)
        self.l_face = 2 * self.coef
        self.l_term = self.l_face + self.pad_face
        self.later = self.l_term + self.pad_face


def dot(a, b):
    return jnp.dot(a, b, preferred_element_type=F32)


def exact_dot(a, b):
    return jnp.dot(a, b, preferred_element_type=F32, precision=lax.Precision.HIGHEST)


def pack_kernel(z, center, x0, proj, right, left, own0, own1, xs):
    xs[...] = x0[...].astype(F32)
    right[...] = jnp.zeros_like(right)
    left[...] = jnp.zeros_like(left)
    for a in range(z.atoms):
        low = center[a] == 0
        before, here, after = proj[a, 0], proj[a, 1], proj[a, 2]
        none = jnp.zeros_like(before)
        at = slice(a * z.proj, (a + 1) * z.proj)
        on0 = jnp.where(low, here, before)
        on1 = jnp.where(low, after, here)
        own0[at, :] = on0
        own1[at, :] = on1
        reach_left = jnp.where(low, before, none)
        reach_right = jnp.where(low, none, after)
        for k in range(z.chunks):
            width = LANES if k < z.chunks - 1 else z.tail
            cols = slice(k * LANES, k * LANES + width)
            rows = slice(k * z.coef + a * z.proj, k * z.coef + (a + 1) * z.proj)
            right[rows, :width] = reach_right[:, cols]
            left[rows, :width] = reach_left[:, cols]
        rows = slice(z.m_face + a * z.proj, z.m_face + (a + 1) * z.proj)
        right[rows, : z.tail] = on1[:, (z.chunks - 1) * LANES :]
        left[rows, :] = on0[:, :LANES]
    coeffs = dot(own0[...], x0[: z.nodes, :]) + dot(own1[...], xs[z.last :, :].astype(BF16))
    sent = coeffs.astype(BF16)
    right[z.m_coef : z.m_rows, :] = sent
    left[z.m_coef : z.m_rows, :] = sent
    n = z.right_hi - z.right_lo
    right[z.m_rows : z.m_rows + n, :] = x0[z.right_lo : z.right_hi, :]
    n = z.left_hi - z.left_lo
    left[z.m_rows : z.m_rows + n, :] = x0[z.left_lo : z.left_hi, :]


def local_terms(z, cell0, cell1, spread0, spread1, x_ref, weighted, out):
    c = z.coef
    before, own, after = (weighted[i * c : (i + 1) * c] for i in range(3))
    w0 = jnp.concatenate([own, before], axis=0)
    w1 = jnp.concatenate([own, after], axis=0)
    out[: z.nodes, :] = dot(cell0[...], x_ref[: z.nodes, :].astype(BF16)) + dot(spread0[...], w0)
    term1 = dot(cell1[...], x_ref[z.last :, :].astype(BF16)) + dot(spread1[...], w1)
    out[z.last : z.nodes, :] += term1[: z.nodes - z.last]
    out[z.nodes :, :] = term1[z.nodes - z.last :]


def face_scale(z):
    row = lax.broadcasted_iota(jnp.int32, (z.rows, 1), 0)
    return jnp.where((row < z.face) | (row >= z.end), 0.5, 1.0).astype(F32)


def part_coeffs(z, rows0, rows1, face0, face1, part, pad):
    c = z.coef
    pad[0] = jnp.zeros(pad.shape[1:], F32)
    pad[1] = jnp.zeros(pad.shape[1:], F32)
    pad[0, z.shift : z.shift + z.face, :] = part[: z.face, :]
    pad[1, : z.face, :] = part[z.end :, :]
    s0 = dot(rows0[...], part[: z.nodes, :].astype(BF16)) + dot(face0[...], pad[0].astype(BF16))
    s1 = dot(rows1[...], part[z.last :, :].astype(BF16)) + dot(face1[...], pad[1].astype(BF16))
    return s0[c:], s0[:c] + s1[:c], s1[c:]


def fill_messages(z, coeffs, part, right, left, far_right, far_left):
    before, own, after = (s.astype(BF16) for s in coeffs)
    right[: z.coef, :] = own
    left[: z.coef, :] = own
    right[z.coef : 2 * z.coef, :] = after
    left[z.coef : 2 * z.coef, :] = before
    far_right[...] = after
    far_left[...] = before
    right[z.l_face :, :] = jnp.zeros((z.later - z.l_face, right.shape[1]), BF16)
    left[z.l_face :, :] = jnp.zeros((z.later - z.l_face, left.shape[1]), BF16)
    right[z.l_face : z.l_face + z.face, :] = part[z.end :, :].astype(BF16)
    left[z.l_face : z.l_face + z.face, :] = part[: z.face, :].astype(BF16)


def whole_coeffs(z, own_ref, from_left, from_right, far_left, far_right, mix):
    c = z.coef
    l0, l1 = from_left[:c, :].astype(F32), from_left[c : 2 * c, :].astype(F32)
    r0, r1 = from_right[:c, :].astype(F32), from_right[c : 2 * c, :].astype(F32)
    before = own_ref[:c, :] + l0 + far_left[...].astype(F32)
    own = own_ref[c : 2 * c, :] + l1 + r1
    after = own_ref[2 * c :, :] + r0 + far_right[...].astype(F32)
    return exact_dot(mix[...], jnp.concatenate([before, own, after], axis=0)).astype(BF16)


def whole_field(z, part, from_left, from_right, out):
    out[...] = part[...]
    out[: z.face, :] += from_left[z.l_face : z.l_face + z.face, :].astype(F32)
    out[z.end :, :] += from_right[z.l_face : z.l_face + z.face, :].astype(F32)


def first_kernel(
    z, gain,
    x0, own0, own1, mine_right, mine_left, from_left, from_right, cell0, cell1, mix,
    part, coeffs, right, left, far_right, far_left,
    rows0, rows1, spread0, spread1, face0, face1,
    xs, ext, terms, pad,
):
    c, k_last = z.coef, (z.chunks - 1) * LANES
    xs[...] = x0[...].astype(F32)
    rows0[:c, :] = own0[...]
    rows1[:c, :] = own1[...]
    for k in range(z.chunks):
        width = LANES if k < z.chunks - 1 else z.tail
        cols = slice(k * LANES, k * LANES + width)
        rows0[c:, cols] = from_left[k * c : (k + 1) * c, :width]
        rows1[c:, cols] = from_right[k * c : (k + 1) * c, :width]
    spread0[...] = rows0[...].T
    spread1[...] = rows1[...].T
    face0[:c, :] = mine_left[(z.chunks - 1) * c : z.chunks * c, :]
    face0[c:, :] = from_left[z.m_face : z.m_coef, :]
    face1[:c, :] = mine_right[:c, :]
    face1[c:, :] = from_right[z.m_face : z.m_coef, :]
    ext[...] = jnp.zeros_like(ext)
    halo = from_left[z.m_rows :, :].astype(F32)
    skip = z.last - z.right_lo
    ext[0, : z.stride, :] = halo[skip : skip + z.stride]
    ext[0, z.stride : z.nodes, :] = xs[: z.face, :]
    halo = from_right[z.m_rows :, :].astype(F32)
    skip = z.face - z.left_lo
    ext[1, : z.face, :] = xs[z.end :, :]
    ext[1, z.face : z.nodes, :] = halo[skip : skip + z.stride]
    s0 = dot(rows0[...], x0[: z.nodes, :])
    s1 = dot(rows1[...], xs[z.last :, :].astype(BF16))
    own = s0[:c] + s1[:c]
    for k in range(z.chunks):
        cols = slice(k * LANES, (k + 1) * LANES)
        own += dot(mine_left[k * c : (k + 1) * c, :], ext[0, cols, :].astype(BF16))
        own += dot(mine_right[k * c : (k + 1) * c, :], ext[1, cols, :].astype(BF16))
    before = s0[c:] + from_left[z.m_coef : z.m_rows, :].astype(F32)
    after = s1[c:] + from_right[z.m_coef : z.m_rows, :].astype(F32)
    weighted = exact_dot(mix[...], jnp.concatenate([before, own, after], axis=0)).astype(BF16)
    local_terms(z, cell0, cell1, spread0, spread1, xs, weighted, terms)
    centre = (upper_edge + lower_edge) / 2.0
    part[...] = (terms[...] - centre * (face_scale(z) * xs[...])) * gain
    s = part_coeffs(z, rows0, rows1, face0, face1, part, pad)
    for i in range(3):
        coeffs[i * c : (i + 1) * c, :] = s[i]
    fill_messages(z, s, part, right, left, far_right, far_left)
    right[z.l_term : z.l_term + z.face, : z.tail] = (
        cell1[...].astype(F32)[z.stride :, k_last:].astype(BF16)
    )
    left[z.l_term : z.l_term + z.face, :] = cell0[...].astype(F32)[: z.face, :LANES].astype(BF16)


def second_kernel(
    z, gain, back,
    x0, own_part, own_coeffs, from_left, from_right, from_far_left, from_far_right,
    cell0, cell1, mix, rows0, rows1, spread0, spread1, face0, face1,
    part, coeffs, whole, right, left, far_right, far_left,
    terms, pad,
):
    c = z.coef
    weighted = whole_coeffs(
        z, own_coeffs, from_left, from_right, from_far_left, from_far_right, mix
    )
    whole_field(z, own_part, from_left, from_right, whole)
    local_terms(z, cell0, cell1, spread0, spread1, whole, weighted, terms)
    centre = (upper_edge + lower_edge) / 2.0
    scale = face_scale(z)
    part[...] = (terms[...] - centre * (scale * whole[...])) * gain - back * (
        scale * x0[...].astype(F32)
    )
    s = part_coeffs(z, rows0, rows1, face0, face1, part, pad)
    for i in range(3):
        coeffs[i * c : (i + 1) * c, :] = s[i]
    fill_messages(z, s, part, right, left, far_right, far_left)
    last = dot(cell1[...], part[z.last :, :].astype(BF16))
    first = dot(cell0[...], part[: z.nodes, :].astype(BF16))
    right[z.l_term : z.l_term + z.face, :] = last[z.stride :].astype(BF16)
    left[z.l_term : z.l_term + z.face, :] = first[: z.face].astype(BF16)


def third_kernel(
    z, gain, back, share,
    previous, own_part, own_coeffs, from_left, from_right, from_far_left, from_far_right,
    block_left, block_right, cell0, cell1, mix, spread0, spread1, face0, face1, occupation,
    out, density,
    whole, terms, pad,
):
    c = z.coef
    weighted = whole_coeffs(
        z, own_coeffs, from_left, from_right, from_far_left, from_far_right, mix
    )
    whole_field(z, own_part, from_left, from_right, whole)
    local_terms(z, cell0, cell1, spread0, spread1, whole, weighted, terms)
    before, own, after = (weighted[i * c : (i + 1) * c] for i in range(3))
    pad[...] = jnp.zeros_like(pad)
    pad[0, z.shift : z.shift + z.face, :] = own_part[: z.face, :]
    pad[1, : z.face, :] = own_part[z.end :, :]
    faces = slice(z.l_term, z.l_term + z.face)
    term = from_left[faces, :].astype(F32)
    term += dot(block_left[z.l_term :, :], pad[0].astype(BF16))[: z.face]
    term += dot(face0[...].T, jnp.concatenate([own, before], axis=0))[
        z.shift : z.shift + z.face
    ]
    terms[: z.face, :] += term
    term = from_right[faces, :].astype(F32)
    term += dot(block_right[z.l_term :, :], pad[1].astype(BF16))[: z.face]
    term += dot(face1[...].T, jnp.concatenate([own, after], axis=0))[: z.face]
    terms[z.end :, :] += term
    centre = (upper_edge + lower_edge) / 2.0
    result = (terms[...] - centre * whole[...]) * gain - back * previous[...]
    out[...] = result
    density[...] = lax.dot_general(
        occupation[...] * share,
        result * result,
        (((1,), (1,)), ((), ())),
        preferred_element_type=F32,
        precision=lax.Precision.HIGHEST,
    )


def call(kernel, outs, scratch, *args, scalars=0):
    vmem = pl.BlockSpec(memory_space=pltpu.VMEM)
    smem = pl.BlockSpec(memory_space=pltpu.SMEM)
    return pl.pallas_call(
        kernel,
        out_shape=[jax.ShapeDtypeStruct(s, t) for s, t in outs],
        in_specs=[smem] * scalars + [vmem] * (len(args) - scalars),
        out_specs=[vmem] * len(outs),
        scratch_shapes=[pltpu.VMEM(s, t) for s, t in scratch],
        compiler_params=pltpu.CompilerParams(vmem_limit_bytes=32 * 1024 * 1024),
    )(*args)


def body(filter_input, cell_table, cell_type, atom_center, proj_values, coupling, occupation):
    cells = cell_type.shape[0]
    atoms, projectors = proj_values.shape[0], proj_values.shape[2]
    rows, states = filter_input.shape
    z = Sizes(rows, cells, cell_table.shape[1], atoms, projectors)
    c, n = z.coef, z.nodes
    devices = lax.axis_size("cells")
    states_all = states * lax.axis_size("states")

    def shifted(array, by):
        return lax.ppermute(array, "cells", [(i, (i + by) % devices) for i in range(devices)])

    half_width = (upper_edge - lower_edge) / 2.0
    centre = (upper_edge + lower_edge) / 2.0
    scale = half_width / (ground_edge - centre)
    twice_inverse = 2.0 / scale
    gains, backs = [scale / half_width], [0.0]
    for _ in range(STEPS - 1):
        scale_next = 1.0 / (twice_inverse - scale)
        gains.append(2.0 * scale_next / half_width)
        backs.append(scale * scale_next)
        scale = scale_next

    right, left, own0, own1 = call(
        functools.partial(pack_kernel, z),
        [((z.first, states), BF16)] * 2 + [((c, n), BF16)] * 2,
        [((rows, states), F32)],
        atom_center, filter_input, proj_values,
        scalars=1,
    )
    from_left, from_right = shifted(right, 1), shifted(left, -1)

    onehot = (cell_type[:, None] == jnp.arange(cell_table.shape[0])[None, :]).astype(BF16)
    matrices = jnp.einsum("ct,tij->cij", onehot, cell_table, preferred_element_type=F32)
    matrices = matrices.astype(BF16)
    cell0, cell1 = matrices[0], matrices[-1]
    group = jnp.arange(3 * c) // projectors
    mix = jnp.where(
        group[:, None] == group[None, :], jnp.tile(coupling, (3 * atoms, 3 * atoms)), 0.0
    )

    block, field = (rows, states), ((rows, states), F32)
    messages = [((z.later, states), BF16)] * 2 + [((c, states), BF16)] * 2
    pad = ((2, LANES, states), F32)
    part, coeffs, right, left, far_right, far_left, rows0, rows1, spread0, spread1, face0, face1 = (
        call(
            functools.partial(first_kernel, z, gains[0]),
            [field, ((3 * c, states), F32)]
            + messages
            + [((2 * c, n), BF16)] * 2
            + [((n, 2 * c), BF16)] * 2
            + [((2 * c, LANES), BF16)] * 2,
            [field, ((2, z.chunks * LANES, states), F32), field, pad],
            filter_input, own0, own1, right, left, from_left, from_right, cell0, cell1, mix,
        )
    )
    block_left, block_right = shifted(right, 1), shifted(left, -1)
    from_far_left, from_far_right = shifted(far_right, 2), shifted(far_left, -2)
    part, coeffs, whole, right, left, far_right, far_left = call(
        functools.partial(second_kernel, z, gains[1], backs[1]),
        [field, ((3 * c, states), F32), field] + messages,
        [field, pad],
        filter_input, part, coeffs, block_left, block_right, from_far_left, from_far_right,
        cell0, cell1, mix, rows0, rows1, spread0, spread1, face0, face1,
    )
    from_left, from_right = shifted(right, 1), shifted(left, -1)
    from_far_left, from_far_right = shifted(far_right, 2), shifted(far_left, -2)
    filtered, density = call(
        functools.partial(third_kernel, z, gains[2], backs[2], 1.0 / states_all),
        [field, ((1, rows), F32)],
        [field, field, pad],
        whole, part, coeffs, from_left, from_right, from_far_left, from_far_right,
        block_left, block_right, cell0, cell1, mix, spread0, spread1, face0, face1,
        occupation[None, :],
    )
    return filtered, lax.psum(density[0], "states")


def solution(mesh):
    in_specs = (
        P("cells", "states"),
        P(),
        P("cells"),
        P("cells"),
        P("cells", None, None, None),
        P(),
        P("states"),
    )
    out_specs = (P("cells", "states"), P("cells"))
    return jax.shard_map(body, mesh=mesh, in_specs=in_specs, out_specs=out_specs, check_vma=False)
```

time: 110 us -> 48.2 us (0.44)
  waiting for transfers between devices: 25.5 us -> 3.45 us
  local copies, waits for them, and re-layouts: 25.7 us -> 6.64 us
  matrix products: 12.4 us -> 1.43 us
  other arithmetic: 8.51 us -> 1.05 us
  starting transfers between devices: 29.6 us -> 23.3 us
  Pallas kernels: 0 us -> 5.05 us
    ppermute x12 -> x10, waiting for transfers between devices: 25.5 us -> 3.45 us  [shifted(): lax.ppermute(array, 'cells', [(i, (i + by) % devices) for i in range(devi...]
    reshape x12 -> x0, local copies, waits for them, and re-layouts: 11.2 us -> none  [the longest x3 3.7 us: join_cells(): head_rows = cell_tiles[:, :STRIDE].reshape(tile_count * STRIDE, columns)]
    dot_general x13 -> x1, matrix products: 12.4 us -> 1.43 us  [body(): jnp.einsum('ct,tij->cij', onehot, cell_table, preferred_element_type=F32)]
    ppermute x12 -> x10, starting transfers between devices: 29.6 us -> 23.3 us  [shifted(): lax.ppermute(array, 'cells', [(i, (i + by) % devices) for i in range(devi...]
    pallas_call x0 -> x4, Pallas kernels: none -> 5.05 us  [call(): pl.pallas_call(kernel, out_shape=[jax.ShapeDtypeStruct(s, t) for s, t in...]
    concatenate x3 -> x0, local copies, waits for them, and re-layouts: 4.85 us -> none  [apply_h(): jnp.concatenate([x_rims[:STRIDE], rounded, x_rims[-STRIDE:]], axis=0)]
    gather x1 -> x0, local copies, waits for them, and re-layouts: 4.65 us -> none  [body(): matrices = jnp.take(cell_table, cell_type, axis=0)]
    add x4 -> x0, other arithmetic: 4.59 us -> none  [the longest x3 3.86 us: join_cells(): jnp.pad(head_rows, ((0, FACE), (0, 0)))]
  transfers between devices with their start and end apart: 12 -> 10, of which waited for: 8 -> 2; matrix products, arithmetic and copies ran while one was open for 8% -> 13% of each run, Pallas kernels for 0% -> 0%
where the time goes in v1:
time: 48.2 us; the launch traced here: 48 us
  starting transfers between devices  23.3 us (48%)
  local copies, waits for them, and re-layouts  6.64 us (14%)
  blocking collectives  6.26 us (13%)
  Pallas kernels  5.05 us (10%)
  waiting for transfers between devices  3.45 us (7%)
  matrix products  1.43 us (3%)
  other arithmetic  1.05 us (2%)
  between operations  0.79 us (2%)
    ppermute x10, starting transfers between devices, shifted(): lax.ppermute(array, 'cells', [(i, (i + by) % devices) for i in range(devi...  23.3 us
    psum x1, blocking collectives, body(): return (filtered, lax.psum(density[0], 'states'))  6.26 us
    pallas_call x4, Pallas kernels, call(): pl.pallas_call(kernel, out_shape=[jax.ShapeDtypeStruct(s, t) for s, t in...  5.05 us
    another operation x2, local copies, waits for them, and re-layouts, body(): jnp.tile(coupling, (3 * atoms, 3 * atoms))  3.87 us
    ppermute x10, waiting for transfers between devices, shifted(): lax.ppermute(array, 'cells', [(i, (i + by) % devices) for i in range(devi...  3.45 us
    unnamed x14, local copies, waits for them, and re-layouts  2.65 us
    dot_general x1, matrix products, body(): jnp.einsum('ct,tij->cij', onehot, cell_table, preferred_element_type=F32)  1.43 us
    select_n x1, other arithmetic, body(): jnp.where(group[:, None] == group[None, :], jnp.tile(coupling, (3 * atoms...  1.03 us
  transfers between devices with their start and end apart: 10, of which 2 were waited for; matrix products, arithmetic and copies ran while one was open for 13% of the time, Pallas kernels for 0%

profile of v1, /device:TPU:0, one launch (start us, length us, event | category | flops | bytes accessed | tf_op | source)
XLA Modules:
  0.0 48.0 jit_solution(16211668774733644485)
XLA Ops:
  0.6 0.0 copy-start
  0.6 0.0 copy-start.1
  0.7 1.1 %copy-done.1 = bf16[637,128]{1,0:T(8,128)(2,1)S(1)} copy-done((bf16[637,128]{1,0:T(8,128)(2,1)S(1)}, bf16[637,128]{1,0:T(8,128)(2,1)}, u32[]{:S(2)}) %copy-start.1) | copy-done | bytes 163096
  1.7 0.0 copy-start.3
  1.7 0.9 %copy-done.3 = bf16[4,3,16,343]{3,2,1,0:T(8,128)(2,1)S(1)} copy-done((bf16[4,3,16,343]{3,2,1,0:T(8,128)(2,1)S(1)}, bf16[4,3,16,343]{3,2,1,0:T(8,128)(2,1)}, u32[]{:S(2)}) %copy-start.3) | copy-done | bytes 131736
  2.6 0.0 copy-start.4
  2.6 0.7 %copy-done.4 = s32[4]{0:T(128)S(1)} copy-done((s32[4]{0:T(128)S(1)}, s32[4]{0:T(128)}, u32[]{:S(2)}) %copy-start.4) | copy-done | bytes 40
  3.3 0.8 %shard_map.86 = (bf16[624,128]{1,0:T(8,128)(2,1)S(1)}, bf16[624,128]{1,0:T(8,128)(2,1)S(1)}, bf16[64,343]{1,0:T(8,128)(2,1)S(1)}, bf16[64,343]{1,0:T(8,128)(2,1)S(1)}) custom-call(s32[4]{0:T(128)S(1)} %copy-done.4, bf16[637,128]{1,0:T(8,128)(2,1)S(1)} %copy-done.1, bf16[4,3,16,343]{3,2,1,0:T(8,128)(2,1)S(1)} %copy-done.3), custom_call_target="tpu_custom_call" | custom-call | tf_op jit(solution)/shard_map/pallas_call | solution.py:281
  4.1 3.0 %collective-permute-start = (bf16[624,128]{1,0:T(8,128)(2,1)S(1)}, bf16[624,128]{1,0:T(8,128)(2,1)S(1)}, u32[]{:S(2)}, u32[]{:S(2)}) collective-permute-start(bf16[624,128]{1,0:T(8,128)(2,1)S(1)} %get-tuple-element.29.mine_right), channel_id=1, source_target_pairs={{0,4},{4,8},{8,12},{12,16},{16,20},{20,24},{24,28},{28,0},{1,5},{5... | collective-permute-start | bytes 479240 | tf_op jit(solution)/shard_map/ppermute | solution.py:301
  7.1 3.1 %collective-permute-start.1 = (bf16[624,128]{1,0:T(8,128)(2,1)S(1)}, bf16[624,128]{1,0:T(8,128)(2,1)S(1)}, u32[]{:S(2)}, u32[]{:S(2)}) collective-permute-start(bf16[624,128]{1,0:T(8,128)(2,1)S(1)} %get-tuple-element.30.mine_left), channel_id=1, source_target_pairs={{0,28},{4,0},{8,4},{12,8},{16,12},{20,16},{24,20},{28,24},{1,29},{... | collective-permute-start | bytes 479240 | tf_op jit(solution)/shard_map/ppermute | solution.py:301
  10.2 0.0 copy-done
  10.2 0.0 copy-start.6
  10.2 1.4 %fusion = bf16[2,343,343]{2,0,1:T(2,128)(2,1)S(1)} fusion(bf16[8,343,343]{2,0,1:T(8,128)(2,1)S(1)} %copy-done, s32[2]{0:T(128)} %param.9), kind=kOutput, calls=%fused_computation.7 | convolution fusion | flops 3764784 | bytes 2352988 | tf_op jit(solution)/shard_map/ct,tij->cij/dot_general | solution.py:324
  11.6 0.1 copy.12
  11.7 0.1 slice_bitcast_fusion
  11.8 0.0 copy-done.6
  11.8 0.0 copy-start.2
  11.8 1.3 %tile.4 = f32[12,16,12,16]{3,2,1,0:T(8,128)} broadcast(f32[16,16]{1,0:T(8,128)S(1)} %copy-done.6), dimensions={1,3} | broadcast | bytes 148480 | tf_op jit(solution)/shard_map/tile | solution.py:329
  13.1 2.6 %tile.10 = f32[192,192]{1,0:T(8,128)} reshape(f32[12,16,12,16]{3,2,1,0:T(8,128)} %tile.4) | data formatting | bytes 294912 | tf_op jit(solution)/shard_map/tile | solution.py:329
  15.6 0.0 copy-start.5
  15.7 1.0 %compare_select_fusion.mix = f32[192,192]{1,0:T(8,128)S(1)} fusion(f32[192,192]{1,0:T(8,128)} %tile.10, s32[192]{0:T(256)S(1)} %and_select_fusion), kind=kLoop, calls=%fused_computation.3 | loop fusion | flops 73728 | bytes 295680 | tf_op jit(solution)/shard_map/jit(_where)/select_n | solution.py:328
  16.7 0.0 collective-permute-done.from_left
  16.7 0.0 collective-permute-done.1.from_right
  16.7 0.0 copy-done.2
  16.7 1.4 %shard_map.87 = (f32[637,128]{1,0:T(8,128)S(1)}, f32[192,128]{1,0:T(8,128)S(1)}, bf16[256,128]{1,0:T(8,128)(2,1)S(1)}, bf16[256,128]{1,0:T(8,128)(2,1)S(1)}, bf1...) custom-call(bf16[637,128]{1,0:T(8,128)(2,1)S(1)} %copy-done.2, ...), custom_call_target="tpu_custom_call" | custom-call | tf_op jit(solution)/shard_map/pallas_call | solution.py:281
  18.1 0.1 collective-permute-start.2
  18.2 4.7 %collective-permute-start.3 = (bf16[256,128]{1,0:T(8,128)(2,1)S(1)}, bf16[256,128]{1,0:T(8,128)(2,1)S(1)}, u32[]{:S(2)}, u32[]{:S(2)}) collective-permute-start(bf16[256,128]{1,0:T(8,128)(2,1)S(1)} %get-tuple-element.34), channel_id=1, source_target_pairs={{0,28},{4,0},{8,4},{12,8},{16,12},{20,16},{24,20},{28,24},{1,29},{... | collective-permute-start | bytes 196616 | tf_op jit(solution)/shard_map/ppermute | solution.py:301
  22.9 0.0 collective-permute-start.4
  22.9 3.8 %collective-permute-start.5 = (bf16[64,128]{1,0:T(8,128)(2,1)S(1)}, bf16[64,128]{1,0:T(8,128)(2,1)S(1)}, u32[]{:S(2)}, u32[]{:S(2)}) collective-permute-start(bf16[64,128]{1,0:T(8,128)(2,1)S(1)} %get-tuple-element.36), channel_id=1, source_target_pairs={{0,24},{4,28},{8,0},{12,4},{16,8},{20,12},{24,16},{28,20},{1,25},{... | collective-permute-start | bytes 49160 | tf_op jit(solution)/shard_map/ppermute | solution.py:301
  26.7 1.7 %collective-permute-done.4.from_far_left = bf16[64,128]{1,0:T(8,128)(2,1)S(1)} collective-permute-done((bf16[64,128]{1,0:T(8,128)(2,1)S(1)}, bf16[64,128]{1,0:T(8,128)(2,1)S(1)}, u32[]{:S(2)}, u32[]{:S(2)}) %collective-permute-start.4) | collective-permute-done | bytes 16416 | tf_op jit(solution)/shard_map/ppermute | solution.py:301
  28.4 0.0 collective-permute-done.5.from_far_right
  28.4 0.0 collective-permute-done.2.from_left.block_left
  28.4 0.0 collective-permute-done.3.from_right.block_right
  28.4 1.2 %shard_map.88 = (f32[637,128]{1,0:T(8,128)S(1)}, f32[192,128]{1,0:T(8,128)S(1)}, f32[637,128]{1,0:T(8,128)S(1)}, bf16[256,128]{1,0:T(8,128)(2,1)S(1)}, bf16[256,...) custom-call(bf16[637,128]{1,0:T(8,128)(2,1)S(1)} %copy-done.2, ...), custom_call_target="tpu_custom_call" | custom-call | tf_op jit(solution)/shard_map/pallas_call | solution.py:281
  29.7 0.1 collective-permute-start.6
  29.8 4.7 %collective-permute-start.7 = (bf16[256,128]{1,0:T(8,128)(2,1)S(1)}, bf16[256,128]{1,0:T(8,128)(2,1)S(1)}, u32[]{:S(2)}, u32[]{:S(2)}) collective-permute-start(bf16[256,128]{1,0:T(8,128)(2,1)S(1)} %get-tuple-element.47), channel_id=1, source_target_pairs={{0,28},{4,0},{8,4},{12,8},{16,12},{20,16},{24,20},{28,24},{1,29},{... | collective-permute-start | bytes 196616 | tf_op jit(solution)/shard_map/ppermute | solution.py:301
  34.5 0.0 collective-permute-start.8
  34.5 3.8 %collective-permute-start.9 = (bf16[64,128]{1,0:T(8,128)(2,1)S(1)}, bf16[64,128]{1,0:T(8,128)(2,1)S(1)}, u32[]{:S(2)}, u32[]{:S(2)}) collective-permute-start(bf16[64,128]{1,0:T(8,128)(2,1)S(1)} %get-tuple-element.49), channel_id=1, source_target_pairs={{0,24},{4,28},{8,0},{12,4},{16,8},{20,12},{24,16},{28,20},{1,25},{... | collective-permute-start | bytes 49160 | tf_op jit(solution)/shard_map/ppermute | solution.py:301
  38.3 1.7 %collective-permute-done.8.from_far_left = bf16[64,128]{1,0:T(8,128)(2,1)S(1)} collective-permute-done((bf16[64,128]{1,0:T(8,128)(2,1)S(1)}, bf16[64,128]{1,0:T(8,128)(2,1)S(1)}, u32[]{:S(2)}, u32[]{:S(2)}) %collective-permute-start.8) | collective-permute-done | bytes 16416 | tf_op jit(solution)/shard_map/ppermute | solution.py:301
  40.0 0.0 collective-permute-done.9.from_far_right
  40.0 0.0 collective-permute-done.6.from_left
  40.0 0.0 collective-permute-done.7.from_right
  40.0 0.0 copy-done.5
  40.0 1.6 %shard_map.89 = (f32[637,128]{1,0:T(8,128)}, f32[1,637]{1,0:T(1,128)S(1)}) custom-call(f32[637,128]{1,0:T(8,128)S(1)} %get-tuple-element.43.previous, f32[637,128]{1,0:T(8,128)S(1)} %get-tuple-element.44.own_part, f32[192,128]{1,0:T(8,128)S(1)} %get-tuple-element.45.own_coeffs, bf16[256,128]{1,0:T(8,128)(2,1)S(1)} %collective-permute-done.6.from_left, ...), custom_call_target="tpu_custom_call" | custom-call | tf_op jit(solution)/shard_map/pallas_call | solution.py:281
  41.7 6.3 %psum.7 = f32[637]{0:T(1024)} all-reduce(f32[637]{0:T(1024)S(1)} %reduce), channel_id=1, replica_groups=mesh['cells'=8,'states'=4] {'states'}, use_global_device_ids=true, to_apply=%region_0.1 | all-reduce | flops 637 | bytes 5096 | tf_op jit(solution)/shard_map/psum | solution.py:366
  (2 shorter events, 0.0 us)
Async XLA Ops:
  0.6 9.6 %copy-start = (bf16[8,343,343]{2,0,1:T(8,128)(2,1)S(1)}, bf16[8,343,343]{2,0,1:T(8,128)(2,1)}, u32[]{:S(2)}) copy-start(bf16[8,343,343]{2,0,1:T(8,128)(2,1)} %param.8) | copy-start | bytes 5647156
  0.6 1.1 %copy-start.1 = (bf16[637,128]{1,0:T(8,128)(2,1)S(1)}, bf16[637,128]{1,0:T(8,128)(2,1)}, u32[]{:S(2)}) copy-start(bf16[637,128]{1,0:T(8,128)(2,1)} %x0.5) | copy-start | bytes 489220
  1.7 0.9 %copy-start.3 = (bf16[4,3,16,343]{3,2,1,0:T(8,128)(2,1)S(1)}, bf16[4,3,16,343]{3,2,1,0:T(8,128)(2,1)}, u32[]{:S(2)}) copy-start(bf16[4,3,16,343]{3,2,1,0:T(8,128)(2,1)} %proj.1) | copy-start | bytes 395140
  2.6 0.7 %copy-start.4 = (s32[4]{0:T(128)S(1)}, s32[4]{0:T(128)}, u32[]{:S(2)}) copy-start(s32[4]{0:T(128)} %center.1) | copy-start | bytes 52
  4.1 12.6 %collective-permute-start = (bf16[624,128]{1,0:T(8,128)(2,1)S(1)}, bf16[624,128]{1,0:T(8,128)(2,1)S(1)}, u32[]{:S(2)}, u32[]{:S(2)}) collective-permute-start(bf16[624,128]{1,0:T(8,128)(2,1)S(1)} %get-tuple-element.29.mine_right), channel_id=1, source_target_pairs={{0,4},{4,8},{8,12},{12,16},{16,20},{20,24},{24,28},{28,0},{1,5},{5... | collective-permute-start | bytes 479240 | tf_op jit(solution)/shard_map/ppermute | solution.py:301
  7.1 9.6 %collective-permute-start.1 = (bf16[624,128]{1,0:T(8,128)(2,1)S(1)}, bf16[624,128]{1,0:T(8,128)(2,1)S(1)}, u32[]{:S(2)}, u32[]{:S(2)}) collective-permute-start(bf16[624,128]{1,0:T(8,128)(2,1)S(1)} %get-tuple-element.30.mine_left), channel_id=1, source_target_pairs={{0,28},{4,0},{8,4},{12,8},{16,12},{20,16},{24,20},{28,24},{1,29},{... | collective-permute-start | bytes 479240 | tf_op jit(solution)/shard_map/ppermute | solution.py:301
  10.2 1.6 %copy-start.6 = (f32[16,16]{1,0:T(8,128)S(1)}, f32[16,16]{1,0:T(8,128)}, u32[]{:S(2)}) copy-start(f32[16,16]{1,0:T(8,128)} %param.12) | copy-start | bytes 3076
  11.8 4.9 %copy-start.2 = (bf16[637,128]{1,0:T(8,128)(2,1)S(1)}, bf16[637,128]{1,0:T(8,128)(2,1)}, u32[]{:S(2)}) copy-start(bf16[637,128]{1,0:T(8,128)(2,1)} %x0.5) | copy-start | bytes 489220
  15.6 24.4 %copy-start.5 = (f32[128]{0:T(128)S(1)}, f32[128]{0:T(128)}, u32[]{:S(2)}) copy-start(f32[128]{0:T(128)} %param.13) | copy-start | bytes 1540
  18.1 10.3 %collective-permute-start.2 = (bf16[256,128]{1,0:T(8,128)(2,1)S(1)}, bf16[256,128]{1,0:T(8,128)(2,1)S(1)}, u32[]{:S(2)}, u32[]{:S(2)}) collective-permute-start(bf16[256,128]{1,0:T(8,128)(2,1)S(1)} %get-tuple-element.33), channel_id=1, source_target_pairs={{0,4},{4,8},{8,12},{12,16},{16,20},{20,24},{24,28},{28,0},{1,5},{5... | collective-permute-start | bytes 196616 | tf_op jit(solution)/shard_map/ppermute | solution.py:301
  18.2 10.3 %collective-permute-start.3 = (bf16[256,128]{1,0:T(8,128)(2,1)S(1)}, bf16[256,128]{1,0:T(8,128)(2,1)S(1)}, u32[]{:S(2)}, u32[]{:S(2)}) collective-permute-start(bf16[256,128]{1,0:T(8,128)(2,1)S(1)} %get-tuple-element.34), channel_id=1, source_target_pairs={{0,28},{4,0},{8,4},{12,8},{16,12},{20,16},{24,20},{28,24},{1,29},{... | collective-permute-start | bytes 196616 | tf_op jit(solution)/shard_map/ppermute | solution.py:301
  22.9 5.5 %collective-permute-start.4 = (bf16[64,128]{1,0:T(8,128)(2,1)S(1)}, bf16[64,128]{1,0:T(8,128)(2,1)S(1)}, u32[]{:S(2)}, u32[]{:S(2)}) collective-permute-start(bf16[64,128]{1,0:T(8,128)(2,1)S(1)} %get-tuple-element.35), channel_id=1, source_target_pairs={{0,8},{4,12},{8,16},{12,20},{16,24},{20,28},{24,0},{28,4},{1,9},{5... | collective-permute-start | bytes 49160 | tf_op jit(solution)/shard_map/ppermute | solution.py:301
  22.9 5.5 %collective-permute-start.5 = (bf16[64,128]{1,0:T(8,128)(2,1)S(1)}, bf16[64,128]{1,0:T(8,128)(2,1)S(1)}, u32[]{:S(2)}, u32[]{:S(2)}) collective-permute-start(bf16[64,128]{1,0:T(8,128)(2,1)S(1)} %get-tuple-element.36), channel_id=1, source_target_pairs={{0,24},{4,28},{8,0},{12,4},{16,8},{20,12},{24,16},{28,20},{1,25},{... | collective-permute-start | bytes 49160 | tf_op jit(solution)/shard_map/ppermute | solution.py:301
  29.7 10.3 %collective-permute-start.6 = (bf16[256,128]{1,0:T(8,128)(2,1)S(1)}, bf16[256,128]{1,0:T(8,128)(2,1)S(1)}, u32[]{:S(2)}, u32[]{:S(2)}) collective-permute-start(bf16[256,128]{1,0:T(8,128)(2,1)S(1)} %get-tuple-element.46), channel_id=1, source_target_pairs={{0,4},{4,8},{8,12},{12,16},{16,20},{20,24},{24,28},{28,0},{1,5},{5... | collective-permute-start | bytes 196616 | tf_op jit(solution)/shard_map/ppermute | solution.py:301
  29.8 10.3 %collective-permute-start.7 = (bf16[256,128]{1,0:T(8,128)(2,1)S(1)}, bf16[256,128]{1,0:T(8,128)(2,1)S(1)}, u32[]{:S(2)}, u32[]{:S(2)}) collective-permute-start(bf16[256,128]{1,0:T(8,128)(2,1)S(1)} %get-tuple-element.47), channel_id=1, source_target_pairs={{0,28},{4,0},{8,4},{12,8},{16,12},{20,16},{24,20},{28,24},{1,29},{... | collective-permute-start | bytes 196616 | tf_op jit(solution)/shard_map/ppermute | solution.py:301
  34.5 5.5 %collective-permute-start.8 = (bf16[64,128]{1,0:T(8,128)(2,1)S(1)}, bf16[64,128]{1,0:T(8,128)(2,1)S(1)}, u32[]{:S(2)}, u32[]{:S(2)}) collective-permute-start(bf16[64,128]{1,0:T(8,128)(2,1)S(1)} %get-tuple-element.48), channel_id=1, source_target_pairs={{0,8},{4,12},{8,16},{12,20},{16,24},{20,28},{24,0},{28,4},{1,9},{5... | collective-permute-start | bytes 49160 | tf_op jit(solution)/shard_map/ppermute | solution.py:301
  34.5 5.5 %collective-permute-start.9 = (bf16[64,128]{1,0:T(8,128)(2,1)S(1)}, bf16[64,128]{1,0:T(8,128)(2,1)S(1)}, u32[]{:S(2)}, u32[]{:S(2)}) collective-permute-start(bf16[64,128]{1,0:T(8,128)(2,1)S(1)} %get-tuple-element.49), channel_id=1, source_target_pairs={{0,24},{4,28},{8,0},{12,4},{16,8},{20,12},{24,16},{28,20},{1,25},{... | collective-permute-start | bytes 49160 | tf_op jit(solution)/shard_map/ppermute | solution.py:301

commit v2 on v1

v2 whole, which is shorter than its diff:
```python
import functools

import jax
import jax.numpy as jnp
from jax import lax
from jax.experimental import pallas as pl
from jax.experimental.pallas import tpu as pltpu
from jax.sharding import PartitionSpec as P

STEPS = 3
LANES = 128
ROWS16 = 16

lower_edge = 4.0
upper_edge = 12.0
ground_edge = -2.0

F32 = jnp.float32
BF16 = jnp.bfloat16


def up16(n):
    return -(-n // ROWS16) * ROWS16


def down16(n):
    return n // ROWS16 * ROWS16


class Sizes:
    def __init__(self, node_rows, cells, cell_nodes, atoms, projectors):
        self.rows = node_rows
        self.nodes = cell_nodes
        self.stride = (node_rows - cell_nodes) // (cells - 1)
        self.face = cell_nodes - self.stride
        self.last = node_rows - cell_nodes
        self.end = node_rows - self.face
        self.atoms = atoms
        self.proj = projectors
        self.coef = atoms * projectors
        self.chunks = -(-cell_nodes // LANES)
        self.tail = cell_nodes - (self.chunks - 1) * LANES
        self.shift = self.stride - (self.chunks - 1) * LANES
        self.m_face = self.chunks * self.coef
        self.m_coef = self.m_face + self.coef
        self.m_rows = self.m_coef + self.coef
        self.right_lo, self.right_hi = down16(self.last), up16(self.end)
        self.left_lo, self.left_hi = down16(self.face), up16(cell_nodes)
        self.halo = max(self.right_hi - self.right_lo, self.left_hi - self.left_lo)
        self.first = self.m_rows + self.halo
        self.pad_face = up16(self.face)
        self.span = up16(self.shift + self.face)
        self.l_face = 2 * self.coef
        self.l_term = self.l_face + self.span
        self.later = self.l_term + self.pad_face


def dot(a, b):
    return jnp.dot(a, b, preferred_element_type=F32)


def exact_dot(a, b):
    return jnp.dot(a, b, preferred_element_type=F32, precision=lax.Precision.HIGHEST)


def halves(v):
    high = v.astype(BF16)
    return high, (v - high.astype(F32)).astype(BF16)


def pack_kernel(
    z, center_hbm, x0_hbm, proj_hbm, x0, right, left, own0, own1, coeffs, center, proj, xs, sems
):
    copies = [
        pltpu.make_async_copy(x0_hbm, x0, sems.at[0]),
        pltpu.make_async_copy(center_hbm, center, sems.at[1]),
        pltpu.make_async_copy(proj_hbm, proj, sems.at[2]),
    ]
    for copy in copies:
        copy.start()
    right[...] = jnp.zeros_like(right)
    left[...] = jnp.zeros_like(left)
    copies[0].wait()
    xs[...] = x0[...].astype(F32)
    n = z.right_hi - z.right_lo
    right[z.m_rows : z.m_rows + n, :] = x0[z.right_lo : z.right_hi, :]
    n = z.left_hi - z.left_lo
    left[z.m_rows : z.m_rows + n, :] = x0[z.left_lo : z.left_hi, :]
    copies[1].wait()
    copies[2].wait()
    for a in range(z.atoms):
        low = center[a] == 0
        before, here, after = proj[a, 0], proj[a, 1], proj[a, 2]
        none = jnp.zeros_like(before)
        at = slice(a * z.proj, (a + 1) * z.proj)
        on0 = jnp.where(low, here, before)
        on1 = jnp.where(low, after, here)
        own0[at, :] = on0
        own1[at, :] = on1
        reach_left = jnp.where(low, before, none)
        reach_right = jnp.where(low, none, after)
        for k in range(z.chunks):
            width = LANES if k < z.chunks - 1 else z.tail
            cols = slice(k * LANES, k * LANES + width)
            rows = slice(k * z.coef + a * z.proj, k * z.coef + (a + 1) * z.proj)
            right[rows, :width] = reach_right[:, cols]
            left[rows, :width] = reach_left[:, cols]
        rows = slice(z.m_face + a * z.proj, z.m_face + (a + 1) * z.proj)
        right[rows, : z.tail] = on1[:, (z.chunks - 1) * LANES :]
        left[rows, :] = on0[:, :LANES]
    s = dot(own0[...], x0[: z.nodes, :]) + dot(own1[...], xs[z.last :, :].astype(BF16))
    coeffs[...] = s
    sent = s.astype(BF16)
    right[z.m_coef : z.m_rows, :] = sent
    left[z.m_coef : z.m_rows, :] = sent


def add_cells(z, term0, term1, out):
    out[: z.nodes, :] += term0
    out[z.last :, :] += term1


def face_scale(z):
    row = lax.broadcasted_iota(jnp.int32, (z.rows, 1), 0)
    return jnp.where((row < z.face) | (row >= z.end), 0.5, 1.0).astype(F32)


CENTRE = (upper_edge + lower_edge) / 2.0


def twice(a, b):
    return jnp.concatenate([a, b, a, b], axis=0).astype(BF16)


def send_part(z, rows0, rows1, face0, face1, part, coeffs, right, left, far_right, far_left):
    c = z.coef
    right[z.l_face :, :] = jnp.zeros((z.later - z.l_face, right.shape[1]), BF16)
    left[z.l_face :, :] = jnp.zeros((z.later - z.l_face, left.shape[1]), BF16)
    right[z.l_face : z.l_face + z.face, :] = part[z.end :, :].astype(BF16)
    at = z.l_face + z.shift
    left[at : at + z.face, :] = part[: z.face, :].astype(BF16)
    last = right[z.l_face : z.l_term, :]
    first = left[z.l_face : z.l_term, :]
    s0 = dot(rows0[...], part[: z.nodes, :].astype(BF16)) + dot(face0[:, : z.span], first)
    s1 = dot(rows1[...], part[z.last :, :].astype(BF16)) + dot(face1[:, : z.span], last)
    before, own, after = s0[c:], s0[:c] + s1[:c], s1[c:]
    coeffs[:c, :] = before
    coeffs[c : 2 * c, :] = own
    coeffs[2 * c :, :] = after
    before, own, after = before.astype(BF16), own.astype(BF16), after.astype(BF16)
    right[:c, :] = own
    left[:c, :] = own
    right[c : 2 * c, :] = after
    left[c : 2 * c, :] = before
    far_right[...] = after
    far_left[...] = before


def whole_coeffs(z, own_ref, from_left, from_right, far_left, far_right):
    c = z.coef
    l0, l1 = from_left[:c, :].astype(F32), from_left[c : 2 * c, :].astype(F32)
    r0, r1 = from_right[:c, :].astype(F32), from_right[c : 2 * c, :].astype(F32)
    before = own_ref[:c, :] + l0 + far_left[...].astype(F32)
    own = own_ref[c : 2 * c, :] + l1 + r1
    after = own_ref[2 * c :, :] + r0 + far_right[...].astype(F32)
    return before, own, after


def face_rows(z, from_left, from_right):
    at = z.l_face + z.shift
    return (
        from_left[z.l_face : z.l_face + z.face, :].astype(F32),
        from_right[at : at + z.face, :].astype(F32),
    )


def neighbour_terms(z, s, from_left, from_right, cell0, cell1, spread0, spread1):
    before, own, after = s
    first = from_left[z.l_face : z.l_term, :]
    last = from_right[z.l_face : z.l_term, :]
    k_last = (z.chunks - 1) * LANES
    term0 = dot(spread0[...], twice(own, before)) + dot(cell0[:, : z.span], first)
    term1 = dot(spread1[...], twice(own, after)) + dot(cell1[:, k_last:], last[: z.tail])
    return term0, term1


def beside_first(
    z, coupling, x0, cell0, cell1, base, mix_high, mix_low, end_rows, xs
):
    xs[...] = x0[...].astype(F32)
    base[...] = (-CENTRE) * (face_scale(z) * xs[...])
    add_cells(
        z, dot(cell0[...], x0[: z.nodes, :]), dot(cell1[...], xs[z.last :, :].astype(BF16)), base
    )
    size = 2 * z.coef
    row = lax.broadcasted_iota(jnp.int32, (size, z.proj), 0)
    col = lax.broadcasted_iota(jnp.int32, (size, z.proj), 1)
    pick = jnp.where(lax.rem(row, z.proj) == col, 1.0, 0.0).astype(F32)
    wide = exact_dot(pick, coupling[...])
    wide = lax.dot_general(
        wide, pick, (((1,), (1,)), ((), ())),
        preferred_element_type=F32, precision=lax.Precision.HIGHEST,
    )
    row = lax.broadcasted_iota(jnp.int32, (size, size), 0)
    col = lax.broadcasted_iota(jnp.int32, (size, size), 1)
    mix = jnp.where(lax.div(row, z.proj) == lax.div(col, z.proj), wide, 0.0)
    mix_high[...], mix_low[...] = halves(mix)
    end_rows[...] = jnp.zeros_like(end_rows)
    end_rows[: z.face, :] = cell1[...].astype(F32)[z.stride :].astype(BF16)


def mixed(a, mix_high, mix_low):
    high, low = halves(dot(a, mix_high[...]) + dot(a, mix_low[...]))
    return jnp.concatenate([high, low], axis=1)


def first_kernel(
    z, gain,
    base, x0, own0, own1, own_coeffs, mine_right, mine_left, from_left, from_right,
    cell0, mix_high, mix_low, end_rows,
    part, coeffs, right, left, far_right, far_left,
    rows0, rows1, spread0, spread1, face0, face1,
    xs, ext, terms,
):
    c, k_last = z.coef, (z.chunks - 1) * LANES
    xs[...] = x0[...].astype(F32)
    rows0[:c, :] = own0[...]
    rows1[:c, :] = own1[...]
    for k in range(z.chunks):
        width = LANES if k < z.chunks - 1 else z.tail
        cols = slice(k * LANES, k * LANES + width)
        rows0[c:, cols] = from_left[k * c : (k + 1) * c, :width]
        rows1[c:, cols] = from_right[k * c : (k + 1) * c, :width]
    spread0[...] = mixed(rows0[...].T, mix_high, mix_low)
    spread1[...] = mixed(rows1[...].T, mix_high, mix_low)
    face0[:c, :] = mine_left[(z.chunks - 1) * c : z.chunks * c, :]
    face0[c:, :] = from_left[z.m_face : z.m_coef, :]
    face1[:c, :] = mine_right[:c, :]
    face1[c:, :] = from_right[z.m_face : z.m_coef, :]
    ext[...] = jnp.zeros_like(ext)
    halo = from_left[z.m_rows :, :].astype(F32)
    skip = z.last - z.right_lo
    ext[0, : z.stride, :] = halo[skip : skip + z.stride]
    ext[0, z.stride : z.nodes, :] = xs[: z.face, :]
    halo = from_right[z.m_rows :, :].astype(F32)
    skip = z.face - z.left_lo
    ext[1, : z.face, :] = xs[z.end :, :]
    ext[1, z.face : z.nodes, :] = halo[skip : skip + z.stride]
    own = own_coeffs[...]
    for k in range(z.chunks):
        cols = slice(k * LANES, (k + 1) * LANES)
        own += dot(mine_left[k * c : (k + 1) * c, :], ext[0, cols, :].astype(BF16))
        own += dot(mine_right[k * c : (k + 1) * c, :], ext[1, cols, :].astype(BF16))
    before = dot(rows0[c:, :], x0[: z.nodes, :])
    before += from_left[z.m_coef : z.m_rows, :].astype(F32)
    after = dot(rows1[c:, :], xs[z.last :, :].astype(BF16))
    after += from_right[z.m_coef : z.m_rows, :].astype(F32)
    terms[...] = base[...]
    add_cells(
        z, dot(spread0[...], twice(own, before)), dot(spread1[...], twice(own, after)), terms
    )
    part[...] = terms[...] * gain
    send_part(z, rows0, rows1, face0, face1, part, coeffs, right, left, far_right, far_left)
    right[z.l_term :, : z.tail] = end_rows[:, k_last:]
    left[z.l_term :, :] = cell0[: z.pad_face, :LANES]


def beside_second(z, gain, back, part, x0, cell0, cell1, mix_high, mix_low, face0, face1,
                  base, edge0, edge1):
    scale = face_scale(z)
    base[...] = scale * ((-CENTRE * gain) * part[...] - back * x0[...].astype(F32))
    add_cells(
        z,
        gain * dot(cell0[...], part[: z.nodes, :].astype(BF16)),
        gain * dot(cell1[...], part[z.last :, :].astype(BF16)),
        base,
    )
    edge0[...] = mixed(face0[...].T, mix_high, mix_low)
    edge1[...] = mixed(face1[...].T, mix_high, mix_low)


def second_kernel(
    z, gain,
    base, own_coeffs, from_left, from_right, from_far_left, from_far_right,
    cell0, cell1, end_rows, rows0, rows1, spread0, spread1, face0, face1,
    part, coeffs, right, left, far_right, far_left,
):
    s = whole_coeffs(z, own_coeffs, from_left, from_right, from_far_left, from_far_right)
    term0, term1 = neighbour_terms(
        z, s, from_left, from_right, cell0, cell1, spread0, spread1
    )
    part[...] = base[...]
    add_cells(z, gain * term0, gain * term1, part)
    first, last = face_rows(z, from_left, from_right)
    part[: z.face, :] -= (0.5 * CENTRE * gain) * first
    part[z.end :, :] -= (0.5 * CENTRE * gain) * last
    send_part(z, rows0, rows1, face0, face1, part, coeffs, right, left, far_right, far_left)
    right[z.l_term :, :] = dot(end_rows[...], part[z.last :, :].astype(BF16)).astype(BF16)
    left[z.l_term :, :] = dot(
        cell0[: z.pad_face, :], part[: z.nodes, :].astype(BF16)
    ).astype(BF16)


def beside_third(z, gain, back, part, earlier, from_left, from_right, mine_right, mine_left,
                 cell0, cell1, base):
    base[...] = (-CENTRE * gain) * part[...] - back * earlier[...]
    add_cells(
        z,
        gain * dot(cell0[...], part[: z.nodes, :].astype(BF16)),
        gain * dot(cell1[...], part[z.last :, :].astype(BF16)),
        base,
    )
    first, last = face_rows(z, from_left, from_right)
    faces = slice(z.l_face, z.l_term)
    term = dot(from_left[z.l_term :, : z.span], mine_left[faces, :])[: z.face]
    base[: z.face, :] += gain * term - back * first
    term = dot(from_right[z.l_term :, : z.span], mine_right[faces, :])[: z.face]
    base[z.end :, :] += gain * term - back * last


def third_kernel(
    z, gain, share,
    base, own_coeffs, from_left, from_right, from_far_left, from_far_right,
    cell0, cell1, spread0, spread1, edge0, edge1, occupation,
    out, density,
):
    s = whole_coeffs(z, own_coeffs, from_left, from_right, from_far_left, from_far_right)
    before, own, after = s
    term0, term1 = neighbour_terms(
        z, s, from_left, from_right, cell0, cell1, spread0, spread1
    )
    out[...] = base[...]
    add_cells(z, gain * term0, gain * term1, out)
    first, last = face_rows(z, from_left, from_right)
    faces = slice(z.l_term, z.l_term + z.face)
    at = slice(z.shift, z.shift + z.face)
    term = from_left[faces, :].astype(F32) + dot(edge0[...], twice(own, before))[at]
    out[: z.face, :] += gain * (term - CENTRE * first)
    term = from_right[faces, :].astype(F32) + dot(edge1[...], twice(own, after))[: z.face]
    out[z.end :, :] += gain * (term - CENTRE * last)
    result = out[...]
    density[...] = lax.dot_general(
        occupation[...] * share,
        result * result,
        (((1,), (1,)), ((), ())),
        preferred_element_type=F32,
        precision=lax.Precision.HIGHEST,
    )


def call(kernel, outs, scratch, *args, hbm=0):
    vmem = pl.BlockSpec(memory_space=pltpu.VMEM)
    far = pl.BlockSpec(memory_space=pltpu.HBM)
    return pl.pallas_call(
        kernel,
        out_shape=[jax.ShapeDtypeStruct(s, t) for s, t in outs],
        in_specs=[far] * hbm + [vmem] * (len(args) - hbm),
        out_specs=[vmem] * len(outs),
        scratch_shapes=scratch,
        compiler_params=pltpu.CompilerParams(vmem_limit_bytes=32 * 1024 * 1024),
    )(*args)


def body(filter_input, cell_table, cell_type, atom_center, proj_values, coupling, occupation):
    cells = cell_type.shape[0]
    atoms, projectors = proj_values.shape[0], proj_values.shape[2]
    rows, states = filter_input.shape
    z = Sizes(rows, cells, cell_table.shape[1], atoms, projectors)
    c, n = z.coef, z.nodes
    devices, groups = lax.axis_size("cells"), lax.axis_size("states")

    def shifted(array, by):
        return lax.ppermute(array, "cells", [(i, (i + by) % devices) for i in range(devices)])

    half_width = (upper_edge - lower_edge) / 2.0
    scale = half_width / (ground_edge - CENTRE)
    twice_inverse = 2.0 / scale
    gains, backs = [scale / half_width], [0.0]
    for _ in range(STEPS - 1):
        scale_next = 1.0 / (twice_inverse - scale)
        gains.append(2.0 * scale_next / half_width)
        backs.append(scale * scale_next)
        scale = scale_next

    field, share = ((rows, states), F32), ((c, states), F32)
    scratch = pltpu.VMEM(*field)
    x0, right, left, own0, own1, own_share = call(
        functools.partial(pack_kernel, z),
        [((rows, states), BF16)]
        + [((z.first, states), BF16)] * 2
        + [((c, n), BF16)] * 2
        + [share],
        [
            pltpu.SMEM(atom_center.shape, jnp.int32),
            pltpu.VMEM(proj_values.shape, BF16),
            scratch,
            pltpu.SemaphoreType.DMA((3,)),
        ],
        atom_center, filter_input, proj_values,
        hbm=3,
    )
    from_left, from_right = shifted(right, 1), shifted(left, -1)

    onehot = (cell_type[:, None] == jnp.arange(cell_table.shape[0])[None, :]).astype(BF16)
    matrices = jnp.einsum("ct,tij->cij", onehot, cell_table, preferred_element_type=F32)
    matrices = matrices.astype(BF16)
    cell0, cell1 = matrices[0], matrices[-1]
    base, mix_high, mix_low, end_rows = call(
        functools.partial(beside_first, z),
        [field] + [((2 * c, 2 * c), BF16)] * 2 + [((z.pad_face, n), BF16)],
        [scratch],
        coupling, x0, cell0, cell1,
    )

    coeffs = ((3 * c, states), F32)
    messages = [((z.later, states), BF16)] * 2 + [((c, states), BF16)] * 2
    part1, own_coeffs, right, left, far_right, far_left, rows0, rows1, spread0, spread1, face0, face1 = (
        call(
            functools.partial(first_kernel, z, gains[0]),
            [field, coeffs]
            + messages
            + [((2 * c, n), BF16)] * 2
            + [((n, 4 * c), BF16)] * 2
            + [((2 * c, LANES), BF16)] * 2,
            [scratch, pltpu.VMEM((2, z.chunks * LANES, states), F32), scratch],
            base, x0, own0, own1, own_share, right, left, from_left, from_right,
            cell0, mix_high, mix_low, end_rows,
        )
    )
    second_left, second_right = shifted(right, 1), shifted(left, -1)
    from_far_left, from_far_right = shifted(far_right, 2), shifted(far_left, -2)
    base, edge0, edge1 = call(
        functools.partial(beside_second, z, gains[1], backs[1]),
        [field] + [((LANES, 4 * c), BF16)] * 2,
        [],
        part1, x0, cell0, cell1, mix_high, mix_low, face0, face1,
    )
    part2, own_coeffs, right, left, far_right, far_left = call(
        functools.partial(second_kernel, z, gains[1]),
        [field, coeffs] + messages,
        [],
        base, own_coeffs, second_left, second_right, from_far_left, from_far_right,
        cell0, cell1, end_rows, rows0, rows1, spread0, spread1, face0, face1,
    )
    from_left, from_right = shifted(right, 1), shifted(left, -1)
    from_far_left, from_far_right = shifted(far_right, 2), shifted(far_left, -2)
    (base,) = call(
        functools.partial(beside_third, z, gains[2], backs[2]),
        [field],
        [],
        part2, part1, second_left, second_right, right, left, cell0, cell1,
    )
    filtered, density = call(
        functools.partial(third_kernel, z, gains[2], 1.0 / (states * groups)),
        [field, ((1, rows), F32)],
        [],
        base, own_coeffs, from_left, from_right, from_far_left, from_far_right,
        cell0, cell1, spread0, spread1, edge0, edge1, occupation[None, :],
    )
    return filtered, total(density, groups)[0]


def total(density, groups):
    if groups & (groups - 1):
        return lax.psum(density, "states")
    step = 1
    while step < groups:
        density += lax.ppermute(density, "states", [(i, i ^ step) for i in range(groups)])
        step *= 2
    return density


def solution(mesh):
    in_specs = (
        P("cells", "states"),
        P(),
        P("cells"),
        P("cells"),
        P("cells", None, None, None),
        P(),
        P("states"),
    )
    out_specs = (P("cells", "states"), P("cells"))
    return jax.shard_map(body, mesh=mesh, in_specs=in_specs, out_specs=out_specs, check_vma=False)
```

time: 48.2 us -> 45.1 us (0.936)
  blocking collectives: 6.26 us -> 0 us
  waiting for transfers between devices: 3.45 us -> 9.61 us
  local copies, waits for them, and re-layouts: 6.64 us -> 2.76 us
  starting transfers between devices: 23.3 us -> 24.8 us
    psum x1 -> x0, blocking collectives: 6.26 us -> none  [body(): return (filtered, lax.psum(density[0], 'states'))]
    another operation x2 -> x0, local copies, waits for them, and re-layouts: 3.87 us -> none  [body(): jnp.tile(coupling, (3 * atoms, 3 * atoms))]
    ppermute x0 -> x2, waiting for transfers between devices: none -> 3.26 us  [total(): lax.ppermute(density, 'states', [(i, i ^ step) for i in range(groups)])]
    ppermute x10, waiting for transfers between devices: 3.45 us -> 6.35 us  [shifted(): lax.ppermute(array, 'cells', [(i, (i + by) % devices) for i in range(devi...]
    ppermute x0 -> x2, starting transfers between devices: none -> 1.5 us  [total(): lax.ppermute(density, 'states', [(i, i ^ step) for i in range(groups)])]
    select_n x2 -> x0, other arithmetic: 1.03 us -> none  [the longest x1 1.03 us: body(): jnp.where(group[:, None] == group[None, :], jnp.tile(coupling, (3 * atoms...]
    add x0 -> x2, other arithmetic: none -> 0.61 us  [total(): density += lax.ppermute(density, 'states', [(i, i ^ step) for i in range(...]
    pallas_call x4 -> x7, Pallas kernels: 5.05 us -> 4.99 us  [call(): pl.pallas_call(kernel, out_shape=[jax.ShapeDtypeStruct(s, t) for s, t in...]
  transfers between devices with their start and end apart: 10 -> 12, of which waited for: 2 -> 6; matrix products, arithmetic and copies ran while one was open for 13% -> 3% of each run, Pallas kernels for 0% -> 3%
where the time goes in v2:
time: 45.1 us; the launch traced here: 44.9 us
  starting transfers between devices  24.8 us (55%)
  waiting for transfers between devices  9.61 us (21%)
  Pallas kernels  4.99 us (11%)
  local copies, waits for them, and re-layouts  2.76 us (6%)
  matrix products  1.41 us (3%)
  between operations  0.75 us (2%)
  other arithmetic  0.61 us (1%)
    ppermute x10, starting transfers between devices, shifted(): lax.ppermute(array, 'cells', [(i, (i + by) % devices) for i in range(devi...  23.3 us
    ppermute x10, waiting for transfers between devices, shifted(): lax.ppermute(array, 'cells', [(i, (i + by) % devices) for i in range(devi...  6.35 us
    pallas_call x7, Pallas kernels, call(): pl.pallas_call(kernel, out_shape=[jax.ShapeDtypeStruct(s, t) for s, t in...  4.99 us
    ppermute x2, waiting for transfers between devices, total(): lax.ppermute(density, 'states', [(i, i ^ step) for i in range(groups)])  3.26 us
    unnamed x12, local copies, waits for them, and re-layouts  2.64 us
    ppermute x2, starting transfers between devices, total(): lax.ppermute(density, 'states', [(i, i ^ step) for i in range(groups)])  1.5 us
    dot_general x1, matrix products, body(): jnp.einsum('ct,tij->cij', onehot, cell_table, preferred_element_type=F32)  1.41 us
  transfers between devices with their start and end apart: 12, of which 6 were waited for; matrix products, arithmetic and copies ran while one was open for 3% of the time, Pallas kernels for 3%

profile of v2, /device:TPU:0, one launch (start us, length us, event | category | flops | bytes accessed | tf_op | source)
XLA Modules:
  0.0 44.9 jit_solution(10277030609804636515)
XLA Ops:
  0.6 0.0 copy-start
  0.6 0.0 copy-start.1
  0.7 1.1 %copy-done.1 = bf16[637,128]{1,0:T(8,128)(2,1)S(1)} copy-done((bf16[637,128]{1,0:T(8,128)(2,1)S(1)}, bf16[637,128]{1,0:T(8,128)(2,1)}, u32[]{:S(2)}) %copy-start.1) | copy-done | bytes 163096
  1.7 0.0 copy-start.2
  1.7 0.9 %copy-done.2 = bf16[4,3,16,343]{3,2,1,0:T(8,128)(2,1)S(1)} copy-done((bf16[4,3,16,343]{3,2,1,0:T(8,128)(2,1)S(1)}, bf16[4,3,16,343]{3,2,1,0:T(8,128)(2,1)}, u32[]{:S(2)}) %copy-start.2) | copy-done | bytes 131736
  2.6 0.0 copy-start.4
  2.6 0.7 %copy-done.4 = s32[4]{0:T(128)S(1)} copy-done((s32[4]{0:T(128)S(1)}, s32[4]{0:T(128)}, u32[]{:S(2)}) %copy-start.4) | copy-done | bytes 40
  3.3 0.9 %shard_map.86 = (bf16[637,128]{1,0:T(8,128)(2,1)S(1)}, bf16[624,128]{1,0:T(8,128)(2,1)S(1)}, bf16[624,128]{1,0:T(8,128)(2,1)S(1)}, bf16[64,343]{1,0:T(8,128)(2,1...) custom-call(s32[4]{0:T(128)S(1)} %copy-done.4, bf16[637,128]{1,0:T(8,128)(2,1)S(1)} %copy-done.1, ...), custom_call_target="tpu_custom_call" | custom-call | tf_op jit(solution)/shard_map/pallas_call | solution.py:354
  4.2 3.0 %collective-permute-start = (bf16[624,128]{1,0:T(8,128)(2,1)S(1)}, bf16[624,128]{1,0:T(8,128)(2,1)S(1)}, u32[]{:S(2)}, u32[]{:S(2)}) collective-permute-start(bf16[624,128]{1,0:T(8,128)(2,1)S(1)} %get-tuple-element.40.mine_right), channel_id=1, source_target_pairs={{0,4},{4,8},{8,12},{12,16},{16,20},{20,24},{24,28},{28,0},{1,5},{5... | collective-permute-start | bytes 479240 | tf_op jit(solution)/shard_map/ppermute | solution.py:373
  7.2 0.0 copy-start.3
  7.2 3.1 %collective-permute-start.1 = (bf16[624,128]{1,0:T(8,128)(2,1)S(1)}, bf16[624,128]{1,0:T(8,128)(2,1)S(1)}, u32[]{:S(2)}, u32[]{:S(2)}) collective-permute-start(bf16[624,128]{1,0:T(8,128)(2,1)S(1)} %get-tuple-element.41.mine_left), channel_id=1, source_target_pairs={{0,28},{4,0},{8,4},{12,8},{16,12},{20,16},{24,20},{28,24},{1,29},{... | collective-permute-start | bytes 479240 | tf_op jit(solution)/shard_map/ppermute | solution.py:373
  10.3 0.0 copy-done
  10.3 1.4 %fusion = bf16[2,343,343]{2,0,1:T(2,128)(2,1)S(1)} fusion(bf16[8,343,343]{2,0,1:T(8,128)(2,1)S(1)} %copy-done, s32[2]{0:T(128)} %param.9), kind=kOutput, calls=%fused_computation.4 | convolution fusion | flops 3764784 | bytes 2352988 | tf_op jit(solution)/shard_map/ct,tij->cij/dot_general | solution.py:405
  11.8 0.1 copy.11
  11.8 0.1 slice_bitcast_fusion
  11.9 0.0 copy-done.3
  11.9 0.7 %shard_map.87 = (f32[637,128]{1,0:T(8,128)S(1)}, bf16[128,128]{1,0:T(8,128)(2,1)S(1)}, bf16[128,128]{1,0:T(8,128)(2,1)S(1)}, bf16[64,343]{1,0:T(8,128)(2,1)S(1)}) custom-call(f32[16,16]{1,0:T(8,128)S(1)} %copy-done.3, bf16[637,128]{1,0:T(8,128)(2,1)S(1)} %get-tuple-element.35.x0, bf16[343,343]{1,0:T(8,128)(2,1)S(1)} %get-tuple-element.69.cell0, ...), custom_call_target="tpu_custom_call" | custom-call | tf_op jit(solution)/shard_map/pallas_call | solution.py:354
  12.7 1.8 %collective-permute-done.from_left = bf16[624,128]{1,0:T(8,128)(2,1)S(1)} collective-permute-done((bf16[624,128]{1,0:T(8,128)(2,1)S(1)}, bf16[624,128]{1,0:T(8,128)(2,1)S(1)}, u32[]{:S(2)}, u32[]{:S(2)}) %collective-permute-start) | collective-permute-done | bytes 159776 | tf_op jit(solution)/shard_map/ppermute | solution.py:373
  14.5 1.7 %collective-permute-done.1.from_right = bf16[624,128]{1,0:T(8,128)(2,1)S(1)} collective-permute-done((bf16[624,128]{1,0:T(8,128)(2,1)S(1)}, bf16[624,128]{1,0:T(8,128)(2,1)S(1)}, u32[]{:S(2)}, u32[]{:S(2)}) %collective-permute-start.1) | collective-permute-done | bytes 159776 | tf_op jit(solution)/shard_map/ppermute | solution.py:373
  16.2 0.9 %shard_map.88 = (f32[637,128]{1,0:T(8,128)S(1)}, f32[192,128]{1,0:T(8,128)S(1)}, bf16[288,128]{1,0:T(8,128)(2,1)S(1)}, bf16[288,128]{1,0:T(8,128)(2,1)S(1)}, bf1...) custom-call(f32[637,128]{1,0:T(8,128)S(1)} %get-tuple-element.36.bas, ...), custom_call_target="tpu_custom_call" | custom-call | tf_op jit(solution)/shard_map/pallas_call | solution.py:354
  17.1 0.3 collective-permute-start.2
  17.5 4.4 %collective-permute-start.3 = (bf16[288,128]{1,0:T(8,128)(2,1)S(1)}, bf16[288,128]{1,0:T(8,128)(2,1)S(1)}, u32[]{:S(2)}, u32[]{:S(2)}) collective-permute-start(bf16[288,128]{1,0:T(8,128)(2,1)S(1)} %get-tuple-element.51), channel_id=1, source_target_pairs={{0,28},{4,0},{8,4},{12,8},{16,12},{20,16},{24,20},{28,24},{1,29},{... | collective-permute-start | bytes 221192 | tf_op jit(solution)/shard_map/ppermute | solution.py:373
  21.9 0.0 collective-permute-start.4
  21.9 3.8 %collective-permute-start.5 = (bf16[64,128]{1,0:T(8,128)(2,1)S(1)}, bf16[64,128]{1,0:T(8,128)(2,1)S(1)}, u32[]{:S(2)}, u32[]{:S(2)}) collective-permute-start(bf16[64,128]{1,0:T(8,128)(2,1)S(1)} %get-tuple-element.53), channel_id=1, source_target_pairs={{0,24},{4,28},{8,0},{12,4},{16,8},{20,12},{24,16},{28,20},{1,25},{... | collective-permute-start | bytes 49160 | tf_op jit(solution)/shard_map/ppermute | solution.py:373
  25.7 0.0 copy-start.5
  25.7 0.3 shard_map.89
  26.1 1.4 %collective-permute-done.4.from_far_left = bf16[64,128]{1,0:T(8,128)(2,1)S(1)} collective-permute-done((bf16[64,128]{1,0:T(8,128)(2,1)S(1)}, bf16[64,128]{1,0:T(8,128)(2,1)S(1)}, u32[]{:S(2)}, u32[]{:S(2)}) %collective-permute-start.4) | collective-permute-done | bytes 16416 | tf_op jit(solution)/shard_map/ppermute | solution.py:373
  27.4 0.0 collective-permute-done.5.from_far_right
  27.4 0.0 collective-permute-done.2.from_left
  27.4 0.0 collective-permute-done.3.from_right
  27.4 0.6 %shard_map.90 = (f32[637,128]{1,0:T(8,128)S(1)}, f32[192,128]{1,0:T(8,128)S(1)}, bf16[288,128]{1,0:T(8,128)(2,1)S(1)}, bf16[288,128]{1,0:T(8,128)(2,1)S(1)}, bf1...) custom-call(f32[637,128]{1,0:T(8,128)S(1)} %get-tuple-element.48.base, ...), custom_call_target="tpu_custom_call" | custom-call | tf_op jit(solution)/shard_map/pallas_call | solution.py:354
  28.0 0.1 collective-permute-start.6
  28.1 4.7 %collective-permute-start.7 = (bf16[288,128]{1,0:T(8,128)(2,1)S(1)}, bf16[288,128]{1,0:T(8,128)(2,1)S(1)}, u32[]{:S(2)}, u32[]{:S(2)}) collective-permute-start(bf16[288,128]{1,0:T(8,128)(2,1)S(1)} %get-tuple-element.60.mine_left), channel_id=1, source_target_pairs={{0,28},{4,0},{8,4},{12,8},{16,12},{20,16},{24,20},{28,24},{1,29},{... | collective-permute-start | bytes 221192 | tf_op jit(solution)/shard_map/ppermute | solution.py:373
  32.8 0.0 collective-permute-start.8
  32.8 3.8 %collective-permute-start.9 = (bf16[64,128]{1,0:T(8,128)(2,1)S(1)}, bf16[64,128]{1,0:T(8,128)(2,1)S(1)}, u32[]{:S(2)}, u32[]{:S(2)}) collective-permute-start(bf16[64,128]{1,0:T(8,128)(2,1)S(1)} %get-tuple-element.63), channel_id=1, source_target_pairs={{0,24},{4,28},{8,0},{12,4},{16,8},{20,12},{24,16},{28,20},{1,25},{... | collective-permute-start | bytes 49160 | tf_op jit(solution)/shard_map/ppermute | solution.py:373
  36.6 0.3 shard_map.91.base
  36.9 1.4 %collective-permute-done.8.from_far_left = bf16[64,128]{1,0:T(8,128)(2,1)S(1)} collective-permute-done((bf16[64,128]{1,0:T(8,128)(2,1)S(1)}, bf16[64,128]{1,0:T(8,128)(2,1)S(1)}, u32[]{:S(2)}, u32[]{:S(2)}) %collective-permute-start.8) | collective-permute-done | bytes 16416 | tf_op jit(solution)/shard_map/ppermute | solution.py:373
  38.3 0.0 collective-permute-done.9.from_far_right
  38.3 0.0 collective-permute-done.6.from_left
  38.4 0.0 collective-permute-done.7.from_right
  38.4 0.0 copy-done.5
  38.4 1.2 %shard_map.92 = (f32[637,128]{1,0:T(8,128)}, f32[1,637]{1,0:T(1,128)S(1)}) custom-call(f32[637,128]{1,0:T(8,128)S(1)} %shard_map.91.base, f32[192,128]{1,0:T(8,128)S(1)} %get-tuple-element.61.own_coeffs, bf16[288,128]{1,0:T(8,128)(2,1)S(1)} %collective-permute-done.6.from_left, bf16[288,128]{1,0:T(8,128)(2,1)S(1)} %collective-permute-done.7.from_right, ...), custom_call_target="tpu_custom_call" | custom-call | tf_op jit(solution)/shard_map/pallas_call | solution.py:354
  39.6 0.0 collective-permute-start.10
  39.6 1.2 %collective-permute-done.10 = f32[1,637]{1,0:T(1,128)S(1)} collective-permute-done((f32[1,637]{1,0:T(1,128)S(1)}, f32[1,637]{1,0:T(1,128)S(1)}, u32[]{:S(2)}, u32[]{:S(2)}) %collective-permute-start.10) | collective-permute-done | bytes 2580 | tf_op jit(solution)/shard_map/ppermute | solution.py:468
  40.7 1.5 %collective-permute-start.11 = (f32[1,637]{1,0:T(1,128)S(1)}, f32[1,637]{1,0:T(1,128)S(1)}, u32[]{:S(2)}, u32[]{:S(2)}) collective-permute-start(f32[1,637]{1,0:T(1,128)S(1)} %add.6), channel_id=1, source_target_pairs={{0,2},{1,3},{2,0},{3,1},{4,6},{5,7},{6,4},{7,5},{8,10},{9,11},{10,... | collective-permute-start | bytes 7652 | tf_op jit(solution)/shard_map/ppermute | solution.py:468
  42.2 2.1 %collective-permute-done.11 = f32[1,637]{1,0:T(1,128)S(1)} collective-permute-done((f32[1,637]{1,0:T(1,128)S(1)}, f32[1,637]{1,0:T(1,128)S(1)}, u32[]{:S(2)}, u32[]{:S(2)}) %collective-permute-start.11) | collective-permute-done | bytes 2580 | tf_op jit(solution)/shard_map/ppermute | solution.py:468
  44.3 0.6 %add_reduce_fusion = f32[637]{0:T(1024)} fusion(f32[1,637]{1,0:T(1,128)S(1)} %add.6, f32[1,637]{1,0:T(1,128)S(1)} %collective-permute-done.11), kind=kLoop, calls=%fused_computation.3 | loop fusion | flops 637 | bytes 7644 | tf_op jit(solution)/shard_map/add | solution.py:468
  (1 shorter events, 0.0 us)
Async XLA Ops:
  0.6 9.7 %copy-start = (bf16[8,343,343]{2,0,1:T(8,128)(2,1)S(1)}, bf16[8,343,343]{2,0,1:T(8,128)(2,1)}, u32[]{:S(2)}) copy-start(bf16[8,343,343]{2,0,1:T(8,128)(2,1)} %param.8) | copy-start | bytes 5647156
  0.6 1.1 %copy-start.1 = (bf16[637,128]{1,0:T(8,128)(2,1)S(1)}, bf16[637,128]{1,0:T(8,128)(2,1)}, u32[]{:S(2)}) copy-start(bf16[637,128]{1,0:T(8,128)(2,1)} %x0_hbm.1) | copy-start | bytes 489220
  1.7 0.9 %copy-start.2 = (bf16[4,3,16,343]{3,2,1,0:T(8,128)(2,1)S(1)}, bf16[4,3,16,343]{3,2,1,0:T(8,128)(2,1)}, u32[]{:S(2)}) copy-start(bf16[4,3,16,343]{3,2,1,0:T(8,128)(2,1)} %proj_hbm.1) | copy-start | bytes 395140
  2.6 0.7 %copy-start.4 = (s32[4]{0:T(128)S(1)}, s32[4]{0:T(128)}, u32[]{:S(2)}) copy-start(s32[4]{0:T(128)} %center_hbm.1) | copy-start | bytes 52
  4.2 10.3 %collective-permute-start = (bf16[624,128]{1,0:T(8,128)(2,1)S(1)}, bf16[624,128]{1,0:T(8,128)(2,1)S(1)}, u32[]{:S(2)}, u32[]{:S(2)}) collective-permute-start(bf16[624,128]{1,0:T(8,128)(2,1)S(1)} %get-tuple-element.40.mine_right), channel_id=1, source_target_pairs={{0,4},{4,8},{8,12},{12,16},{16,20},{20,24},{24,28},{28,0},{1,5},{5... | collective-permute-start | bytes 479240 | tf_op jit(solution)/shard_map/ppermute | solution.py:373
  7.2 4.7 %copy-start.3 = (f32[16,16]{1,0:T(8,128)S(1)}, f32[16,16]{1,0:T(8,128)}, u32[]{:S(2)}) copy-start(f32[16,16]{1,0:T(8,128)} %coupling.1) | copy-start | bytes 3076
  7.2 9.0 %collective-permute-start.1 = (bf16[624,128]{1,0:T(8,128)(2,1)S(1)}, bf16[624,128]{1,0:T(8,128)(2,1)S(1)}, u32[]{:S(2)}, u32[]{:S(2)}) collective-permute-start(bf16[624,128]{1,0:T(8,128)(2,1)S(1)} %get-tuple-element.41.mine_left), channel_id=1, source_target_pairs={{0,28},{4,0},{8,4},{12,8},{16,12},{20,16},{24,20},{28,24},{1,29},{... | collective-permute-start | bytes 479240 | tf_op jit(solution)/shard_map/ppermute | solution.py:373
  17.1 10.3 %collective-permute-start.2 = (bf16[288,128]{1,0:T(8,128)(2,1)S(1)}, bf16[288,128]{1,0:T(8,128)(2,1)S(1)}, u32[]{:S(2)}, u32[]{:S(2)}) collective-permute-start(bf16[288,128]{1,0:T(8,128)(2,1)S(1)} %get-tuple-element.50), channel_id=1, source_target_pairs={{0,4},{4,8},{8,12},{12,16},{16,20},{20,24},{24,28},{28,0},{1,5},{5... | collective-permute-start | bytes 221192 | tf_op jit(solution)/shard_map/ppermute | solution.py:373
  17.5 10.0 %collective-permute-start.3 = (bf16[288,128]{1,0:T(8,128)(2,1)S(1)}, bf16[288,128]{1,0:T(8,128)(2,1)S(1)}, u32[]{:S(2)}, u32[]{:S(2)}) collective-permute-start(bf16[288,128]{1,0:T(8,128)(2,1)S(1)} %get-tuple-element.51), channel_id=1, source_target_pairs={{0,28},{4,0},{8,4},{12,8},{16,12},{20,16},{24,20},{28,24},{1,29},{... | collective-permute-start | bytes 221192 | tf_op jit(solution)/shard_map/ppermute | solution.py:373
  21.9 5.5 %collective-permute-start.4 = (bf16[64,128]{1,0:T(8,128)(2,1)S(1)}, bf16[64,128]{1,0:T(8,128)(2,1)S(1)}, u32[]{:S(2)}, u32[]{:S(2)}) collective-permute-start(bf16[64,128]{1,0:T(8,128)(2,1)S(1)} %get-tuple-element.52), channel_id=1, source_target_pairs={{0,8},{4,12},{8,16},{12,20},{16,24},{20,28},{24,0},{28,4},{1,9},{5... | collective-permute-start | bytes 49160 | tf_op jit(solution)/shard_map/ppermute | solution.py:373
  21.9 5.5 %collective-permute-start.5 = (bf16[64,128]{1,0:T(8,128)(2,1)S(1)}, bf16[64,128]{1,0:T(8,128)(2,1)S(1)}, u32[]{:S(2)}, u32[]{:S(2)}) collective-permute-start(bf16[64,128]{1,0:T(8,128)(2,1)S(1)} %get-tuple-element.53), channel_id=1, source_target_pairs={{0,24},{4,28},{8,0},{12,4},{16,8},{20,12},{24,16},{28,20},{1,25},{... | collective-permute-start | bytes 49160 | tf_op jit(solution)/shard_map/ppermute | solution.py:373
  25.7 12.6 %copy-start.5 = (f32[128]{0:T(128)S(1)}, f32[128]{0:T(128)}, u32[]{:S(2)}) copy-start(f32[128]{0:T(128)} %param.13) | copy-start | bytes 1540
  28.0 10.3 %collective-permute-start.6 = (bf16[288,128]{1,0:T(8,128)(2,1)S(1)}, bf16[288,128]{1,0:T(8,128)(2,1)S(1)}, u32[]{:S(2)}, u32[]{:S(2)}) collective-permute-start(bf16[288,128]{1,0:T(8,128)(2,1)S(1)} %get-tuple-element.59.mine_right), channel_id=1, source_target_pairs={{0,4},{4,8},{8,12},{12,16},{16,20},{20,24},{24,28},{28,0},{1,5},{5... | collective-permute-start | bytes 221192 | tf_op jit(solution)/shard_map/ppermute | solution.py:373
  28.1 10.3 %collective-permute-start.7 = (bf16[288,128]{1,0:T(8,128)(2,1)S(1)}, bf16[288,128]{1,0:T(8,128)(2,1)S(1)}, u32[]{:S(2)}, u32[]{:S(2)}) collective-permute-start(bf16[288,128]{1,0:T(8,128)(2,1)S(1)} %get-tuple-element.60.mine_left), channel_id=1, source_target_pairs={{0,28},{4,0},{8,4},{12,8},{16,12},{20,16},{24,20},{28,24},{1,29},{... | collective-permute-start | bytes 221192 | tf_op jit(solution)/shard_map/ppermute | solution.py:373
  32.8 5.5 %collective-permute-start.8 = (bf16[64,128]{1,0:T(8,128)(2,1)S(1)}, bf16[64,128]{1,0:T(8,128)(2,1)S(1)}, u32[]{:S(2)}, u32[]{:S(2)}) collective-permute-start(bf16[64,128]{1,0:T(8,128)(2,1)S(1)} %get-tuple-element.62), channel_id=1, source_target_pairs={{0,8},{4,12},{8,16},{12,20},{16,24},{20,28},{24,0},{28,4},{1,9},{5... | collective-permute-start | bytes 49160 | tf_op jit(solution)/shard_map/ppermute | solution.py:373
  32.8 5.5 %collective-permute-start.9 = (bf16[64,128]{1,0:T(8,128)(2,1)S(1)}, bf16[64,128]{1,0:T(8,128)(2,1)S(1)}, u32[]{:S(2)}, u32[]{:S(2)}) collective-permute-start(bf16[64,128]{1,0:T(8,128)(2,1)S(1)} %get-tuple-element.63), channel_id=1, source_target_pairs={{0,24},{4,28},{8,0},{12,4},{16,8},{20,12},{24,16},{28,20},{1,25},{... | collective-permute-start | bytes 49160 | tf_op jit(solution)/shard_map/ppermute | solution.py:373
  39.6 1.2 %collective-permute-start.10 = (f32[1,637]{1,0:T(1,128)S(1)}, f32[1,637]{1,0:T(1,128)S(1)}, u32[]{:S(2)}, u32[]{:S(2)}) collective-permute-start(f32[1,637]{1,0:T(1,128)S(1)} %get-tuple-element.67), channel_id=1, source_target_pairs={{0,1},{1,0},{2,3},{3,2},{4,5},{5,4},{6,7},{7,6},{8,9},{9,8},{10,11... | collective-permute-start | bytes 7652 | tf_op jit(solution)/shard_map/ppermute | solution.py:468
  40.7 3.6 %collective-permute-start.11 = (f32[1,637]{1,0:T(1,128)S(1)}, f32[1,637]{1,0:T(1,128)S(1)}, u32[]{:S(2)}, u32[]{:S(2)}) collective-permute-start(f32[1,637]{1,0:T(1,128)S(1)} %add.6), channel_id=1, source_target_pairs={{0,2},{1,3},{2,0},{3,1},{4,6},{5,7},{6,4},{7,5},{8,10},{9,11},{10,... | collective-permute-start | bytes 7652 | tf_op jit(solution)/shard_map/ppermute | solution.py:468

commit v3 on v2

v3 whole, which is shorter than its diff:
```python
import functools

import jax
import jax.numpy as jnp
from jax import lax
from jax.experimental import pallas as pl
from jax.experimental.pallas import tpu as pltpu
from jax.sharding import PartitionSpec as P

STEPS = 3
LANES = 128
ROWS16 = 16

lower_edge = 4.0
upper_edge = 12.0
ground_edge = -2.0

F32 = jnp.float32
BF16 = jnp.bfloat16


def up16(n):
    return -(-n // ROWS16) * ROWS16


def down16(n):
    return n // ROWS16 * ROWS16


class Sizes:
    def __init__(self, node_rows, cells, cell_nodes, atoms, projectors):
        self.rows = node_rows
        self.nodes = cell_nodes
        self.stride = (node_rows - cell_nodes) // (cells - 1)
        self.face = cell_nodes - self.stride
        self.last = node_rows - cell_nodes
        self.end = node_rows - self.face
        self.atoms = atoms
        self.proj = projectors
        self.coef = atoms * projectors
        self.chunks = -(-cell_nodes // LANES)
        self.tail = cell_nodes - (self.chunks - 1) * LANES
        self.shift = self.stride - (self.chunks - 1) * LANES
        self.m_face = self.chunks * self.coef
        self.m_coef = self.m_face + self.coef
        self.m_rows = self.m_coef + self.coef
        self.right_lo, self.right_hi = down16(self.last), up16(self.end)
        self.left_lo, self.left_hi = down16(self.face), up16(cell_nodes)
        self.halo = max(self.right_hi - self.right_lo, self.left_hi - self.left_lo)
        self.first = self.m_rows + self.halo
        self.pad_face = up16(self.face)
        self.span = up16(self.shift + self.face)
        self.l_face = 2 * self.coef
        self.l_term = self.l_face + self.span
        self.later = self.l_term + self.pad_face


def dot(a, b):
    return jnp.dot(a, b, preferred_element_type=F32)


def exact_dot(a, b):
    return jnp.dot(a, b, preferred_element_type=F32, precision=lax.Precision.HIGHEST)


def halves(v):
    high = v.astype(BF16)
    return high, (v - high.astype(F32)).astype(BF16)


def is_even():
    return lax.rem(lax.axis_index("cells"), 2) == 0


def put(near, over, at, to_right, to_left):
    even = is_even()
    near[at] = jnp.where(even, to_right, to_left)
    over[at] = jnp.where(even, to_left, to_right)


def take(near, over, at):
    even = is_even()
    a, b = near[at], over[at]
    return jnp.where(even, b, a), jnp.where(even, a, b)


def pack_kernel(
    z, center_hbm, x0_hbm, proj_hbm, x0, near, over, own0, own1, coeffs, center, proj, xs, sems
):
    copies = [
        pltpu.make_async_copy(x0_hbm, x0, sems.at[0]),
        pltpu.make_async_copy(center_hbm, center, sems.at[1]),
        pltpu.make_async_copy(proj_hbm, proj, sems.at[2]),
    ]
    for copy in copies:
        copy.start()
    near[: z.m_coef, :] = jnp.zeros((z.m_coef, near.shape[1]), BF16)
    over[: z.m_coef, :] = jnp.zeros((z.m_coef, near.shape[1]), BF16)
    copies[0].wait()
    xs[...] = x0[...].astype(F32)
    put(
        near, over, (slice(z.m_rows, z.first), slice(None)),
        x0[z.right_lo : z.right_lo + z.halo, :], x0[z.left_lo : z.left_lo + z.halo, :],
    )
    copies[1].wait()
    copies[2].wait()
    for a in range(z.atoms):
        low = center[a] == 0
        before, here, after = proj[a, 0], proj[a, 1], proj[a, 2]
        none = jnp.zeros_like(before)
        at = slice(a * z.proj, (a + 1) * z.proj)
        on0 = jnp.where(low, here, before)
        on1 = jnp.where(low, after, here)
        own0[at, :] = on0
        own1[at, :] = on1
        reach_left = jnp.where(low, before, none)
        reach_right = jnp.where(low, none, after)
        for k in range(z.chunks):
            width = LANES if k < z.chunks - 1 else z.tail
            cols = slice(k * LANES, k * LANES + width)
            rows = slice(k * z.coef + a * z.proj, k * z.coef + (a + 1) * z.proj)
            put(
                near, over, (rows, slice(0, width)), reach_right[:, cols], reach_left[:, cols]
            )
        rows = slice(z.m_face + a * z.proj, z.m_face + (a + 1) * z.proj)
        wide = jnp.zeros((z.proj, LANES - z.tail), BF16)
        end = jnp.concatenate([on1[:, (z.chunks - 1) * LANES :], wide], axis=1)
        put(near, over, (rows, slice(None)), end, on0[:, :LANES])
    s = dot(own0[...], x0[: z.nodes, :]) + dot(own1[...], xs[z.last :, :].astype(BF16))
    coeffs[...] = s
    sent = s.astype(BF16)
    near[z.m_coef : z.m_rows, :] = sent
    over[z.m_coef : z.m_rows, :] = sent


def add_cells(z, term0, term1, out):
    out[: z.nodes, :] += term0
    out[z.last :, :] += term1


def face_scale(z):
    row = lax.broadcasted_iota(jnp.int32, (z.rows, 1), 0)
    return jnp.where((row < z.face) | (row >= z.end), 0.5, 1.0).astype(F32)


CENTRE = (upper_edge + lower_edge) / 2.0


def twice(a, b):
    return jnp.concatenate([a, b, a, b], axis=0).astype(BF16)


def send_part(
    z, rows0, rows1, face0, face1, end0, end1, part, coeffs, near, over, far, farther, first, last
):
    c = z.coef
    last[...] = jnp.zeros_like(last)
    first[...] = jnp.zeros_like(first)
    last[: z.face, :] = part[z.end :, :]
    first[z.shift : z.shift + z.face, :] = part[: z.face, :]
    last_rows, first_rows = last[...].astype(BF16), first[...].astype(BF16)
    put(near, over, (slice(z.l_face, z.l_term), slice(None)), last_rows, first_rows)
    on0, on1 = part[: z.nodes, :].astype(BF16), part[z.last :, :].astype(BF16)
    s0 = dot(rows0[...], on0) + dot(face0[:, : z.span], first_rows)
    s1 = dot(rows1[...], on1) + dot(face1[:, : z.span], last_rows)
    before, own, after = s0[c:], s0[:c] + s1[:c], s1[c:]
    coeffs[:c, :] = before
    coeffs[c : 2 * c, :] = own
    coeffs[2 * c :, :] = after
    before, own, after = before.astype(BF16), own.astype(BF16), after.astype(BF16)
    near[:c, :] = own
    over[:c, :] = own
    put(near, over, (slice(c, 2 * c), slice(None)), after, before)
    even = is_even()
    far[...] = jnp.where(even, before, after)
    farther[...] = jnp.where(even, after, before)
    if end0 is None:
        return
    put(
        near, over, (slice(z.l_term, z.later), slice(None)),
        dot(end1[...], on1).astype(BF16), dot(end0[: z.pad_face, :], on0).astype(BF16),
    )


def whole_coeffs(z, own_ref, near, over, far, farther):
    c = z.coef
    left, right = (v.astype(F32) for v in take(near, over, (slice(0, 2 * c), slice(None))))
    even = is_even()
    a, b = far[...], farther[...]
    far_left, far_right = jnp.where(even, b, a), jnp.where(even, a, b)
    before = own_ref[:c, :] + left[:c] + far_left.astype(F32)
    own = own_ref[c : 2 * c, :] + left[c:] + right[c:]
    after = own_ref[2 * c :, :] + right[:c] + far_right.astype(F32)
    return before, own, after


def face_rows(z, near, over):
    first, last = take(near, over, (slice(z.l_face, z.l_term), slice(None)))
    return (
        first.astype(F32)[: z.face],
        last.astype(F32)[z.shift : z.shift + z.face],
    )


def neighbour_terms(z, s, near, over, cell0, cell1, spread0, spread1):
    before, own, after = s
    first, last = take(near, over, (slice(z.l_face, z.l_term), slice(None)))
    k_last = (z.chunks - 1) * LANES
    term0 = dot(spread0[...], twice(own, before)) + dot(cell0[:, : z.span], first)
    term1 = dot(spread1[...], twice(own, after)) + dot(cell1[:, k_last:], last[: z.tail])
    return term0, term1


def beside_first(
    z, coupling, x0, cell0, cell1, base, mix_high, mix_low, end_rows, xs
):
    xs[...] = x0[...].astype(F32)
    base[...] = (-CENTRE) * (face_scale(z) * xs[...])
    add_cells(
        z, dot(cell0[...], x0[: z.nodes, :]), dot(cell1[...], xs[z.last :, :].astype(BF16)), base
    )
    size = 2 * z.coef
    row = lax.broadcasted_iota(jnp.int32, (size, z.proj), 0)
    col = lax.broadcasted_iota(jnp.int32, (size, z.proj), 1)
    pick = jnp.where(lax.rem(row, z.proj) == col, 1.0, 0.0).astype(F32)
    wide = exact_dot(pick, coupling[...])
    wide = lax.dot_general(
        wide, pick, (((1,), (1,)), ((), ())),
        preferred_element_type=F32, precision=lax.Precision.HIGHEST,
    )
    row = lax.broadcasted_iota(jnp.int32, (size, size), 0)
    col = lax.broadcasted_iota(jnp.int32, (size, size), 1)
    mix = jnp.where(lax.div(row, z.proj) == lax.div(col, z.proj), wide, 0.0)
    mix_high[...], mix_low[...] = halves(mix)
    end_rows[...] = jnp.zeros_like(end_rows)
    end_rows[: z.face, :] = cell1[...].astype(F32)[z.stride :].astype(BF16)


def mixed(a, mix_high, mix_low):
    high, low = halves(dot(a, mix_high[...]) + dot(a, mix_low[...]))
    return jnp.concatenate([high, low], axis=1)


def first_kernel(
    z, gain,
    base, x0, own0, own1, own_coeffs, mine_near, mine_over, from_near, from_over,
    cell0, mix_high, mix_low, end_rows,
    part, coeffs, near, over, far, farther,
    rows0, rows1, spread0, spread1, face0, face1,
    xs, ext, terms, first, last,
):
    c, k_last = z.coef, (z.chunks - 1) * LANES
    xs[...] = x0[...].astype(F32)
    rows0[:c, :] = own0[...]
    rows1[:c, :] = own1[...]
    for k in range(z.chunks):
        width = LANES if k < z.chunks - 1 else z.tail
        cols = slice(k * LANES, k * LANES + width)
        rows0[c:, cols], rows1[c:, cols] = take(
            from_near, from_over, (slice(k * c, (k + 1) * c), slice(0, width))
        )
    spread0[...] = mixed(rows0[...].T, mix_high, mix_low)
    spread1[...] = mixed(rows1[...].T, mix_high, mix_low)
    chunks = [
        take(mine_near, mine_over, (slice(k * c, (k + 1) * c), slice(None)))
        for k in range(z.chunks)
    ]
    face0[:c, :] = chunks[-1][0]
    face1[:c, :] = chunks[0][1]
    face0[c:, :], face1[c:, :] = take(
        from_near, from_over, (slice(z.m_face, z.m_coef), slice(None))
    )
    ext[...] = jnp.zeros_like(ext)
    halo = take(from_near, from_over, (slice(z.m_rows, z.first), slice(None)))
    skip = z.last - z.right_lo
    ext[0, : z.stride, :] = halo[0].astype(F32)[skip : skip + z.stride]
    ext[0, z.stride : z.nodes, :] = xs[: z.face, :]
    skip = z.face - z.left_lo
    ext[1, : z.face, :] = xs[z.end :, :]
    ext[1, z.face : z.nodes, :] = halo[1].astype(F32)[skip : skip + z.stride]
    own = own_coeffs[...]
    for k in range(z.chunks):
        cols = slice(k * LANES, (k + 1) * LANES)
        own += dot(chunks[k][0], ext[0, cols, :].astype(BF16))
        own += dot(chunks[k][1], ext[1, cols, :].astype(BF16))
    before, after = take(from_near, from_over, (slice(z.m_coef, z.m_rows), slice(None)))
    before = before.astype(F32) + dot(rows0[c:, :], x0[: z.nodes, :])
    after = after.astype(F32) + dot(rows1[c:, :], xs[z.last :, :].astype(BF16))
    terms[...] = base[...]
    add_cells(
        z, dot(spread0[...], twice(own, before)), dot(spread1[...], twice(own, after)), terms
    )
    part[...] = terms[...] * gain
    send_part(
        z, rows0, rows1, face0, face1, None, None,
        part, coeffs, near, over, far, farther, first, last,
    )
    wide = jnp.zeros((z.pad_face, LANES - z.tail), BF16)
    put(
        near, over, (slice(z.l_term, z.later), slice(None)),
        jnp.concatenate([end_rows[:, k_last:], wide], axis=1), cell0[: z.pad_face, :LANES],
    )


def beside_second(z, gain, back, part, x0, cell0, cell1, mix_high, mix_low, face0, face1,
                  base, edge0, edge1):
    scale = face_scale(z)
    base[...] = scale * ((-CENTRE * gain) * part[...] - back * x0[...].astype(F32))
    add_cells(
        z,
        gain * dot(cell0[...], part[: z.nodes, :].astype(BF16)),
        gain * dot(cell1[...], part[z.last :, :].astype(BF16)),
        base,
    )
    edge0[...] = mixed(face0[...].T, mix_high, mix_low)
    edge1[...] = mixed(face1[...].T, mix_high, mix_low)


def second_kernel(
    z, gain,
    base, own_coeffs, from_near, from_over, from_far, from_farther,
    cell0, cell1, end_rows, rows0, rows1, spread0, spread1, face0, face1,
    part, coeffs, near, over, far, farther,
    first_rows, last_rows,
):
    s = whole_coeffs(z, own_coeffs, from_near, from_over, from_far, from_farther)
    term0, term1 = neighbour_terms(z, s, from_near, from_over, cell0, cell1, spread0, spread1)
    part[...] = base[...]
    add_cells(z, gain * term0, gain * term1, part)
    first, last = face_rows(z, from_near, from_over)
    part[: z.face, :] -= (0.5 * CENTRE * gain) * first
    part[z.end :, :] -= (0.5 * CENTRE * gain) * last
    send_part(
        z, rows0, rows1, face0, face1, cell0, end_rows,
        part, coeffs, near, over, far, farther, first_rows, last_rows,
    )


def beside_third(z, gain, back, part, earlier, from_near, from_over, mine_near, mine_over,
                 cell0, cell1, base):
    base[...] = (-CENTRE * gain) * part[...] - back * earlier[...]
    add_cells(
        z,
        gain * dot(cell0[...], part[: z.nodes, :].astype(BF16)),
        gain * dot(cell1[...], part[z.last :, :].astype(BF16)),
        base,
    )
    first, last = face_rows(z, from_near, from_over)
    blocks = take(from_near, from_over, (slice(z.l_term, z.later), slice(0, z.span)))
    mine = take(mine_near, mine_over, (slice(z.l_face, z.l_term), slice(None)))
    base[: z.face, :] += gain * dot(blocks[0], mine[0])[: z.face] - back * first
    base[z.end :, :] += gain * dot(blocks[1], mine[1])[: z.face] - back * last


def third_kernel(
    z, gain, share,
    base, own_coeffs, from_near, from_over, from_far, from_farther,
    cell0, cell1, spread0, spread1, edge0, edge1, occupation,
    out, density,
):
    s = whole_coeffs(z, own_coeffs, from_near, from_over, from_far, from_farther)
    before, own, after = s
    term0, term1 = neighbour_terms(z, s, from_near, from_over, cell0, cell1, spread0, spread1)
    out[...] = base[...]
    add_cells(z, gain * term0, gain * term1, out)
    first, last = face_rows(z, from_near, from_over)
    terms = take(from_near, from_over, (slice(z.l_term, z.later), slice(None)))
    left, right = (v.astype(F32)[: z.face] for v in terms)
    left += dot(edge0[...], twice(own, before))[z.shift : z.shift + z.face]
    right += dot(edge1[...], twice(own, after))[: z.face]
    out[: z.face, :] += gain * (left - CENTRE * first)
    out[z.end :, :] += gain * (right - CENTRE * last)
    result = out[...]
    density[...] = lax.dot_general(
        occupation[...] * share,
        result * result,
        (((1,), (1,)), ((), ())),
        preferred_element_type=F32,
        precision=lax.Precision.HIGHEST,
    )


def call(kernel, outs, scratch, *args, hbm=0, megabytes=32):
    vmem = pl.BlockSpec(memory_space=pltpu.VMEM)
    far = pl.BlockSpec(memory_space=pltpu.HBM)
    return pl.pallas_call(
        kernel,
        out_shape=[jax.ShapeDtypeStruct(s, t) for s, t in outs],
        in_specs=[far] * hbm + [vmem] * (len(args) - hbm),
        out_specs=[vmem] * len(outs),
        scratch_shapes=scratch,
        compiler_params=pltpu.CompilerParams(vmem_limit_bytes=megabytes * 1024 * 1024),
    )(*args)


def body(filter_input, cell_table, cell_type, atom_center, proj_values, coupling, occupation):
    cells = cell_type.shape[0]
    atoms, projectors = proj_values.shape[0], proj_values.shape[2]
    rows, states = filter_input.shape
    z = Sizes(rows, cells, cell_table.shape[1], atoms, projectors)
    c, n = z.coef, z.nodes
    devices, groups = lax.axis_size("cells"), lax.axis_size("states")

    def exchanged(array, even_by):
        pairs = [
            (i, (i + (even_by if i % 2 == 0 else -even_by)) % devices) for i in range(devices)
        ]
        return lax.ppermute(array, "cells", pairs)

    def exchange_all(near, over, far, farther):
        far = exchanged(far, -2)
        near = exchanged(near, 1)
        farther = exchanged(farther, 2)
        over = exchanged(over, -1)
        return near, over, far, farther

    half_width = (upper_edge - lower_edge) / 2.0
    scale = half_width / (ground_edge - CENTRE)
    twice_inverse = 2.0 / scale
    gains, backs = [scale / half_width], [0.0]
    for _ in range(STEPS - 1):
        scale_next = 1.0 / (twice_inverse - scale)
        gains.append(2.0 * scale_next / half_width)
        backs.append(scale * scale_next)
        scale = scale_next

    field, share = ((rows, states), F32), ((c, states), F32)
    scratch = pltpu.VMEM(*field)
    x0, near, over, own0, own1, own_share = call(
        functools.partial(pack_kernel, z),
        [((rows, states), BF16)]
        + [((z.first, states), BF16)] * 2
        + [((c, n), BF16)] * 2
        + [share],
        [
            pltpu.SMEM(atom_center.shape, jnp.int32),
            pltpu.VMEM(proj_values.shape, BF16),
            scratch,
            pltpu.SemaphoreType.DMA((3,)),
        ],
        atom_center, filter_input, proj_values,
        hbm=3,
        megabytes=56,
    )
    from_over, from_near = exchanged(over, -1), exchanged(near, 1)

    onehot = (cell_type[:, None] == jnp.arange(cell_table.shape[0])[None, :]).astype(BF16)
    matrices = jnp.einsum("ct,tij->cij", onehot, cell_table, preferred_element_type=F32)
    matrices = matrices.astype(BF16)
    cell0, cell1 = matrices[0], matrices[-1]
    base, mix_high, mix_low, end_rows = call(
        functools.partial(beside_first, z),
        [field] + [((2 * c, 2 * c), BF16)] * 2 + [((z.pad_face, n), BF16)],
        [scratch],
        coupling, x0, cell0, cell1,
    )

    coeffs = ((3 * c, states), F32)
    messages = [((z.later, states), BF16)] * 2 + [((c, states), BF16)] * 2
    faces = [pltpu.VMEM((z.span, states), F32)] * 2
    part1, own_coeffs, near, over, far, farther, rows0, rows1, spread0, spread1, face0, face1 = (
        call(
            functools.partial(first_kernel, z, gains[0]),
            [field, coeffs]
            + messages
            + [((2 * c, n), BF16)] * 2
            + [((n, 4 * c), BF16)] * 2
            + [((2 * c, LANES), BF16)] * 2,
            [scratch, pltpu.VMEM((2, z.chunks * LANES, states), F32), scratch] + faces,
            base, x0, own0, own1, own_share, near, over, from_near, from_over,
            cell0, mix_high, mix_low, end_rows,
        )
    )
    second = exchange_all(near, over, far, farther)
    base, edge0, edge1 = call(
        functools.partial(beside_second, z, gains[1], backs[1]),
        [field] + [((LANES, 4 * c), BF16)] * 2,
        [],
        part1, x0, cell0, cell1, mix_high, mix_low, face0, face1,
    )
    part2, own_coeffs, near, over, far, farther = call(
        functools.partial(second_kernel, z, gains[1]),
        [field, coeffs] + messages,
        faces,
        base, own_coeffs, *second,
        cell0, cell1, end_rows, rows0, rows1, spread0, spread1, face0, face1,
    )
    third = exchange_all(near, over, far, farther)
    (base,) = call(
        functools.partial(beside_third, z, gains[2], backs[2]),
        [field],
        [],
        part2, part1, second[0], second[1], near, over, cell0, cell1,
    )
    filtered, density = call(
        functools.partial(third_kernel, z, gains[2], 1.0 / (states * groups)),
        [field, ((1, rows), F32)],
        [],
        base, own_coeffs, *third,
        cell0, cell1, spread0, spread1, edge0, edge1, occupation[None, :],
    )
    return filtered, total(density, groups)[0]


def total(density, groups):
    if groups & (groups - 1):
        return lax.psum(density, "states")
    step = 1
    while step < groups:
        density += lax.ppermute(density, "states", [(i, i ^ step) for i in range(groups)])
        step *= 2
    return density


def solution(mesh):
    in_specs = (
        P("cells", "states"),
        P(),
        P("cells"),
        P("cells"),
        P("cells", None, None, None),
        P(),
        P("states"),
    )
    out_specs = (P("cells", "states"), P("cells"))
    return jax.shard_map(body, mesh=mesh, in_specs=in_specs, out_specs=out_specs, check_vma=False)
```

time: 45.1 us -> 41.8 us (0.927)
  starting transfers between devices: 24.8 us -> 19.1 us
  waiting for transfers between devices: 9.61 us -> 13.3 us
  local copies, waits for them, and re-layouts: 2.76 us -> 0.16 us
  Pallas kernels: 4.99 us -> 6.19 us
    ppermute x10, starting transfers between devices: 23.3 us -> 17.7 us  [exchanged(): return lax.ppermute(array, 'cells', pairs)]
    ppermute x10, waiting for transfers between devices: 6.35 us -> 10 us  [exchanged(): return lax.ppermute(array, 'cells', pairs)]
    unnamed x12 -> x18, local copies, waits for them, and re-layouts: 2.64 us -> 0.04 us
    pallas_call x7, Pallas kernels: 4.99 us -> 6.19 us  [call(): pl.pallas_call(kernel, out_shape=[jax.ShapeDtypeStruct(s, t) for s, t in...]
  transfers between devices with their start and end apart: 12 -> 12, of which waited for: 6 -> 8; matrix products, arithmetic and copies ran while one was open for 3% -> 4% of each run, Pallas kernels for 3% -> 3%
where the time goes in v3:
time: 41.8 us; the launch traced here: 41.6 us
  starting transfers between devices  19.1 us (46%)
  waiting for transfers between devices  13.3 us (32%)
  Pallas kernels  6.19 us (15%)
  matrix products  1.41 us (3%)
  between operations  0.79 us (2%)
  other arithmetic  0.61 us (1%)
    ppermute x10, starting transfers between devices, exchanged(): return lax.ppermute(array, 'cells', pairs)  17.7 us
    ppermute x10, waiting for transfers between devices, exchanged(): return lax.ppermute(array, 'cells', pairs)  10 us
    pallas_call x7, Pallas kernels, call(): pl.pallas_call(kernel, out_shape=[jax.ShapeDtypeStruct(s, t) for s, t in...  6.19 us
    ppermute x2, waiting for transfers between devices, total(): lax.ppermute(density, 'states', [(i, i ^ step) for i in range(groups)])  3.26 us
    ppermute x2, starting transfers between devices, total(): lax.ppermute(density, 'states', [(i, i ^ step) for i in range(groups)])  1.49 us
    dot_general x1, matrix products, body(): jnp.einsum('ct,tij->cij', onehot, cell_table, preferred_element_type=F32)  1.41 us
  transfers between devices with their start and end apart: 12, of which 8 were waited for; matrix products, arithmetic and copies ran while one was open for 4% of the time, Pallas kernels for 3%

profile of v3, /device:TPU:0, one launch (start us, length us, event | category | flops | bytes accessed | tf_op | source)
XLA Modules:
  0.0 41.6 jit_solution(12316905557446183162)
XLA Ops:
  0.6 0.0 copy-start
  0.6 2.1 %shard_map.86 = (bf16[637,128]{1,0:T(8,128)(2,1)}, bf16[624,128]{1,0:T(8,128)(2,1)}, bf16[624,128]{1,0:T(8,128)(2,1)}, bf16[64,343]{1,0:T(8,128)(2,1)}, bf16[64,343]{1,0:T(8,128)(2,1)}, /*index=5*/f32[64,128]{1,0:T(8,128)}) custom-call(s32[4]{0:T(128)} %center_hbm.1, bf16[637,128]{1,0:T(8,128)(2,1)} %x0_hbm.1, bf16[4,3,16,343]{3,2,1,0:T(8,128)(2,1)} %proj_hbm.1), custom_call_target="tpu_custom_call" | custom-call | tf_op jit(solution)/shard_map/pallas_call | solution.py:386
  2.7 3.0 %collective-permute-start = (bf16[624,128]{1,0:T(8,128)(2,1)}, bf16[624,128]{1,0:T(8,128)(2,1)S(1)}, u32[]{:S(2)}, u32[]{:S(2)}) collective-permute-start(bf16[624,128]{1,0:T(8,128)(2,1)} %get-tuple-element.40.mine_near), channel_id=1, source_target_pairs={{0,4},{4,0},{8,12},{12,8},{16,20},{20,16},{24,28},{28,24},{1,5},{5... | collective-permute-start | bytes 479240 | tf_op jit(solution)/shard_map/ppermute | solution.py:408
  5.7 0.0 copy-start.1
  5.8 0.0 copy-start.7
  5.8 0.0 copy-start.2
  5.8 0.0 copy-start.3
  5.8 0.0 copy-start.4
  5.8 0.0 copy-start.5
  5.8 0.0 copy-start.6
  5.8 3.6 %collective-permute-start.1 = (bf16[624,128]{1,0:T(8,128)(2,1)}, bf16[624,128]{1,0:T(8,128)(2,1)S(1)}, u32[]{:S(2)}, u32[]{:S(2)}) collective-permute-start(bf16[624,128]{1,0:T(8,128)(2,1)} %get-tuple-element.41.mine_over), channel_id=1, source_target_pairs={{0,28},{4,8},{8,4},{12,16},{16,12},{20,24},{24,20},{28,0},{1,29},{... | collective-permute-start | bytes 479240 | tf_op jit(solution)/shard_map/ppermute | solution.py:408
  9.4 0.0 copy-done
  9.4 1.4 %fusion = bf16[2,343,343]{2,0,1:T(2,128)(2,1)S(1)} fusion(bf16[8,343,343]{2,0,1:T(8,128)(2,1)S(1)} %copy-done, s32[2]{0:T(128)} %param.9), kind=kOutput, calls=%fused_computation.4 | convolution fusion | flops 3764784 | bytes 2352988 | tf_op jit(solution)/shard_map/ct,tij->cij/dot_general | solution.py:448
  10.8 0.1 copy.11
  10.9 0.1 slice_bitcast_fusion
  11.0 0.0 copy-done.1
  11.0 0.0 copy-done.7
  11.0 0.7 %shard_map.87 = (f32[637,128]{1,0:T(8,128)S(1)}, bf16[128,128]{1,0:T(8,128)(2,1)S(1)}, bf16[128,128]{1,0:T(8,128)(2,1)S(1)}, bf16[64,343]{1,0:T(8,128)(2,1)S(1)}) custom-call(f32[16,16]{1,0:T(8,128)S(1)} %copy-done.7, bf16[637,128]{1,0:T(8,128)(2,1)S(1)} %copy-done.1, bf16[343,343]{1,0:T(8,128)(2,1)S(1)} %get-tuple-element.69.cell0, ...), custom_call_target="tpu_custom_call" | custom-call | tf_op jit(solution)/shard_map/pallas_call | solution.py:386
  11.7 1.1 %collective-permute-done.from_near = bf16[624,128]{1,0:T(8,128)(2,1)S(1)} collective-permute-done((bf16[624,128]{1,0:T(8,128)(2,1)}, bf16[624,128]{1,0:T(8,128)(2,1)S(1)}, u32[]{:S(2)}, u32[]{:S(2)}) %collective-permute-start) | collective-permute-done | bytes 159776 | tf_op jit(solution)/shard_map/ppermute | solution.py:408
  12.9 1.5 %collective-permute-done.1.from_over = bf16[624,128]{1,0:T(8,128)(2,1)S(1)} collective-permute-done((bf16[624,128]{1,0:T(8,128)(2,1)}, bf16[624,128]{1,0:T(8,128)(2,1)S(1)}, u32[]{:S(2)}, u32[]{:S(2)}) %collective-permute-start.1) | collective-permute-done | bytes 159776 | tf_op jit(solution)/shard_map/ppermute | solution.py:408
  14.3 0.0 copy-done.2
  14.3 0.0 copy-done.3
  14.3 0.0 copy-done.4
  14.3 0.0 copy-done.5
  14.4 0.0 copy-done.6
  14.4 0.9 %shard_map.88 = (f32[637,128]{1,0:T(8,128)S(1)}, f32[192,128]{1,0:T(8,128)S(1)}, bf16[288,128]{1,0:T(8,128)(2,1)S(1)}, bf16[288,128]{1,0:T(8,128)(2,1)S(1)}, bf1...) custom-call(f32[637,128]{1,0:T(8,128)S(1)} %get-tuple-element.36.bas, ...), custom_call_target="tpu_custom_call" | custom-call | tf_op jit(solution)/shard_map/pallas_call | solution.py:386
  15.3 1.0 %collective-permute-start.2 = (bf16[288,128]{1,0:T(8,128)(2,1)S(1)}, bf16[288,128]{1,0:T(8,128)(2,1)S(1)}, u32[]{:S(2)}, u32[]{:S(2)}) collective-permute-start(bf16[288,128]{1,0:T(8,128)(2,1)S(1)} %get-tuple-element.50), channel_id=1, source_target_pairs={{0,4},{4,0},{8,12},{12,8},{16,20},{20,16},{24,28},{28,24},{1,5},{5... | collective-permute-start | bytes 221192 | tf_op jit(solution)/shard_map/ppermute | solution.py:408
  16.3 3.5 %collective-permute-start.3 = (bf16[288,128]{1,0:T(8,128)(2,1)S(1)}, bf16[288,128]{1,0:T(8,128)(2,1)S(1)}, u32[]{:S(2)}, u32[]{:S(2)}) collective-permute-start(bf16[288,128]{1,0:T(8,128)(2,1)S(1)} %get-tuple-element.51), channel_id=1, source_target_pairs={{0,28},{4,8},{8,4},{12,16},{16,12},{20,24},{24,20},{28,0},{1,29},{... | collective-permute-start | bytes 221192 | tf_op jit(solution)/shard_map/ppermute | solution.py:408
  19.8 0.5 %collective-permute-start.4 = (bf16[64,128]{1,0:T(8,128)(2,1)S(1)}, bf16[64,128]{1,0:T(8,128)(2,1)S(1)}, u32[]{:S(2)}, u32[]{:S(2)}) collective-permute-start(bf16[64,128]{1,0:T(8,128)(2,1)S(1)} %get-tuple-element.52), channel_id=1, source_target_pairs={{0,24},{4,12},{8,0},{12,20},{16,8},{20,28},{24,16},{28,4},{1,25},{... | collective-permute-start | bytes 49160 | tf_op jit(solution)/shard_map/ppermute | solution.py:408
  20.3 1.6 %collective-permute-start.5 = (bf16[64,128]{1,0:T(8,128)(2,1)S(1)}, bf16[64,128]{1,0:T(8,128)(2,1)S(1)}, u32[]{:S(2)}, u32[]{:S(2)}) collective-permute-start(bf16[64,128]{1,0:T(8,128)(2,1)S(1)} %get-tuple-element.53), channel_id=1, source_target_pairs={{0,8},{4,28},{8,16},{12,4},{16,24},{20,12},{24,0},{28,20},{1,9},{5... | collective-permute-start | bytes 49160 | tf_op jit(solution)/shard_map/ppermute | solution.py:408
  21.8 0.0 copy-start.8
  21.8 0.3 shard_map.89
  22.2 1.4 %collective-permute-done.4.from_far = bf16[64,128]{1,0:T(8,128)(2,1)S(1)} collective-permute-done((bf16[64,128]{1,0:T(8,128)(2,1)S(1)}, bf16[64,128]{1,0:T(8,128)(2,1)S(1)}, u32[]{:S(2)}, u32[]{:S(2)}) %collective-permute-start.4) | collective-permute-done | bytes 16416 | tf_op jit(solution)/shard_map/ppermute | solution.py:408
  23.6 2.4 %collective-permute-done.5.from_farther = bf16[64,128]{1,0:T(8,128)(2,1)S(1)} collective-permute-done((bf16[64,128]{1,0:T(8,128)(2,1)S(1)}, bf16[64,128]{1,0:T(8,128)(2,1)S(1)}, u32[]{:S(2)}, u32[]{:S(2)}) %collective-permute-start.5) | collective-permute-done | bytes 16416 | tf_op jit(solution)/shard_map/ppermute | solution.py:408
  25.9 0.0 collective-permute-done.2.from_near
  25.9 0.0 collective-permute-done.3.from_over
  25.9 0.6 %shard_map.90 = (f32[637,128]{1,0:T(8,128)S(1)}, f32[192,128]{1,0:T(8,128)S(1)}, bf16[288,128]{1,0:T(8,128)(2,1)S(1)}, bf16[288,128]{1,0:T(8,128)(2,1)S(1)}, bf1...) custom-call(f32[637,128]{1,0:T(8,128)S(1)} %get-tuple-element.48.base, ...), custom_call_target="tpu_custom_call" | custom-call | tf_op jit(solution)/shard_map/pallas_call | solution.py:386
  26.5 0.1 collective-permute-start.6
  26.6 2.4 %collective-permute-start.7 = (bf16[288,128]{1,0:T(8,128)(2,1)S(1)}, bf16[288,128]{1,0:T(8,128)(2,1)S(1)}, u32[]{:S(2)}, u32[]{:S(2)}) collective-permute-start(bf16[288,128]{1,0:T(8,128)(2,1)S(1)} %get-tuple-element.60.mine_over), channel_id=1, source_target_pairs={{0,28},{4,8},{8,4},{12,16},{16,12},{20,24},{24,20},{28,0},{1,29},{... | collective-permute-start | bytes 221192 | tf_op jit(solution)/shard_map/ppermute | solution.py:408
  29.0 0.5 %collective-permute-start.8 = (bf16[64,128]{1,0:T(8,128)(2,1)S(1)}, bf16[64,128]{1,0:T(8,128)(2,1)S(1)}, u32[]{:S(2)}, u32[]{:S(2)}) collective-permute-start(bf16[64,128]{1,0:T(8,128)(2,1)S(1)} %get-tuple-element.62), channel_id=1, source_target_pairs={{0,24},{4,12},{8,0},{12,20},{16,8},{20,28},{24,16},{28,4},{1,25},{... | collective-permute-start | bytes 49160 | tf_op jit(solution)/shard_map/ppermute | solution.py:408
  29.5 1.5 %collective-permute-start.9 = (bf16[64,128]{1,0:T(8,128)(2,1)S(1)}, bf16[64,128]{1,0:T(8,128)(2,1)S(1)}, u32[]{:S(2)}, u32[]{:S(2)}) collective-permute-start(bf16[64,128]{1,0:T(8,128)(2,1)S(1)} %get-tuple-element.63), channel_id=1, source_target_pairs={{0,8},{4,28},{8,16},{12,4},{16,24},{20,12},{24,0},{28,20},{1,9},{5... | collective-permute-start | bytes 49160 | tf_op jit(solution)/shard_map/ppermute | solution.py:408
  31.0 0.3 shard_map.91.base
  31.3 1.4 %collective-permute-done.8.from_far = bf16[64,128]{1,0:T(8,128)(2,1)S(1)} collective-permute-done((bf16[64,128]{1,0:T(8,128)(2,1)S(1)}, bf16[64,128]{1,0:T(8,128)(2,1)S(1)}, u32[]{:S(2)}, u32[]{:S(2)}) %collective-permute-start.8) | collective-permute-done | bytes 16416 | tf_op jit(solution)/shard_map/ppermute | solution.py:408
  32.7 2.3 %collective-permute-done.9.from_farther = bf16[64,128]{1,0:T(8,128)(2,1)S(1)} collective-permute-done((bf16[64,128]{1,0:T(8,128)(2,1)S(1)}, bf16[64,128]{1,0:T(8,128)(2,1)S(1)}, u32[]{:S(2)}, u32[]{:S(2)}) %collective-permute-start.9) | collective-permute-done | bytes 16416 | tf_op jit(solution)/shard_map/ppermute | solution.py:408
  35.0 0.0 collective-permute-done.6.from_near
  35.0 0.0 collective-permute-done.7.from_over
  35.0 0.0 copy-done.8
  35.0 1.2 %shard_map.92 = (f32[637,128]{1,0:T(8,128)}, f32[1,637]{1,0:T(1,128)S(1)}) custom-call(f32[637,128]{1,0:T(8,128)S(1)} %shard_map.91.base, f32[192,128]{1,0:T(8,128)S(1)} %get-tuple-element.61.own_coeffs, bf16[288,128]{1,0:T(8,128)(2,1)S(1)} %collective-permute-done.6.from_near, bf16[288,128]{1,0:T(8,128)(2,1)S(1)} %collective-permute-done.7.from_over, ...), custom_call_target="tpu_custom_call" | custom-call | tf_op jit(solution)/shard_map/pallas_call | solution.py:386
  36.2 0.0 collective-permute-start.10
  36.2 1.2 %collective-permute-done.10 = f32[1,637]{1,0:T(1,128)S(1)} collective-permute-done((f32[1,637]{1,0:T(1,128)S(1)}, f32[1,637]{1,0:T(1,128)S(1)}, u32[]{:S(2)}, u32[]{:S(2)}) %collective-permute-start.10) | collective-permute-done | bytes 2580 | tf_op jit(solution)/shard_map/ppermute | solution.py:510
  37.4 1.5 %collective-permute-start.11 = (f32[1,637]{1,0:T(1,128)S(1)}, f32[1,637]{1,0:T(1,128)S(1)}, u32[]{:S(2)}, u32[]{:S(2)}) collective-permute-start(f32[1,637]{1,0:T(1,128)S(1)} %add.6), channel_id=1, source_target_pairs={{0,2},{1,3},{2,0},{3,1},{4,6},{5,7},{6,4},{7,5},{8,10},{9,11},{10,... | collective-permute-start | bytes 7652 | tf_op jit(solution)/shard_map/ppermute | solution.py:510
  38.9 2.1 %collective-permute-done.11 = f32[1,637]{1,0:T(1,128)S(1)} collective-permute-done((f32[1,637]{1,0:T(1,128)S(1)}, f32[1,637]{1,0:T(1,128)S(1)}, u32[]{:S(2)}, u32[]{:S(2)}) %collective-permute-start.11) | collective-permute-done | bytes 2580 | tf_op jit(solution)/shard_map/ppermute | solution.py:510
  41.0 0.6 %add_reduce_fusion = f32[637]{0:T(1024)} fusion(f32[1,637]{1,0:T(1,128)S(1)} %add.6, f32[1,637]{1,0:T(1,128)S(1)} %collective-permute-done.11), kind=kLoop, calls=%fused_computation.3 | loop fusion | flops 637 | bytes 7644 | tf_op jit(solution)/shard_map/add | solution.py:510
  (1 shorter events, 0.0 us)
Async XLA Ops:
  0.6 8.8 %copy-start = (bf16[8,343,343]{2,0,1:T(8,128)(2,1)S(1)}, bf16[8,343,343]{2,0,1:T(8,128)(2,1)}, u32[]{:S(2)}) copy-start(bf16[8,343,343]{2,0,1:T(8,128)(2,1)} %param.8) | copy-start | bytes 5647156
  2.7 10.1 %collective-permute-start = (bf16[624,128]{1,0:T(8,128)(2,1)}, bf16[624,128]{1,0:T(8,128)(2,1)S(1)}, u32[]{:S(2)}, u32[]{:S(2)}) collective-permute-start(bf16[624,128]{1,0:T(8,128)(2,1)} %get-tuple-element.40.mine_near), channel_id=1, source_target_pairs={{0,4},{4,0},{8,12},{12,8},{16,20},{20,16},{24,28},{28,24},{1,5},{5... | collective-permute-start | bytes 479240 | tf_op jit(solution)/shard_map/ppermute | solution.py:408
  5.7 5.2 %copy-start.1 = (bf16[637,128]{1,0:T(8,128)(2,1)S(1)}, bf16[637,128]{1,0:T(8,128)(2,1)}, u32[]{:S(2)}) copy-start(bf16[637,128]{1,0:T(8,128)(2,1)} %get-tuple-element.35.x0) | copy-start | bytes 489220
  5.8 5.2 %copy-start.7 = (f32[16,16]{1,0:T(8,128)S(1)}, f32[16,16]{1,0:T(8,128)}, u32[]{:S(2)}) copy-start(f32[16,16]{1,0:T(8,128)} %coupling.1) | copy-start | bytes 3076
  5.8 8.6 %copy-start.2 = (bf16[624,128]{1,0:T(8,128)(2,1)S(1)}, bf16[624,128]{1,0:T(8,128)(2,1)}, u32[]{:S(2)}) copy-start(bf16[624,128]{1,0:T(8,128)(2,1)} %get-tuple-element.40.mine_near) | copy-start | bytes 479236
  5.8 8.6 %copy-start.3 = (bf16[624,128]{1,0:T(8,128)(2,1)S(1)}, bf16[624,128]{1,0:T(8,128)(2,1)}, u32[]{:S(2)}) copy-start(bf16[624,128]{1,0:T(8,128)(2,1)} %get-tuple-element.41.mine_over) | copy-start | bytes 479236
  5.8 8.6 %copy-start.4 = (bf16[64,343]{1,0:T(8,128)(2,1)S(1)}, bf16[64,343]{1,0:T(8,128)(2,1)}, u32[]{:S(2)}) copy-start(bf16[64,343]{1,0:T(8,128)(2,1)} %get-tuple-element.37.own0) | copy-start | bytes 131716
  5.8 8.6 %copy-start.5 = (bf16[64,343]{1,0:T(8,128)(2,1)S(1)}, bf16[64,343]{1,0:T(8,128)(2,1)}, u32[]{:S(2)}) copy-start(bf16[64,343]{1,0:T(8,128)(2,1)} %get-tuple-element.38.own1) | copy-start | bytes 131716
  5.8 8.6 %copy-start.6 = (f32[64,128]{1,0:T(8,128)S(1)}, f32[64,128]{1,0:T(8,128)}, u32[]{:S(2)}) copy-start(f32[64,128]{1,0:T(8,128)} %get-tuple-element.39.own_coeffs) | copy-start | bytes 98308
  5.8 8.5 %collective-permute-start.1 = (bf16[624,128]{1,0:T(8,128)(2,1)}, bf16[624,128]{1,0:T(8,128)(2,1)S(1)}, u32[]{:S(2)}, u32[]{:S(2)}) collective-permute-start(bf16[624,128]{1,0:T(8,128)(2,1)} %get-tuple-element.41.mine_over), channel_id=1, source_target_pairs={{0,28},{4,8},{8,4},{12,16},{16,12},{20,24},{24,20},{28,0},{1,29},{... | collective-permute-start | bytes 479240 | tf_op jit(solution)/shard_map/ppermute | solution.py:408
  15.3 10.6 %collective-permute-start.2 = (bf16[288,128]{1,0:T(8,128)(2,1)S(1)}, bf16[288,128]{1,0:T(8,128)(2,1)S(1)}, u32[]{:S(2)}, u32[]{:S(2)}) collective-permute-start(bf16[288,128]{1,0:T(8,128)(2,1)S(1)} %get-tuple-element.50), channel_id=1, source_target_pairs={{0,4},{4,0},{8,12},{12,8},{16,20},{20,16},{24,28},{28,24},{1,5},{5... | collective-permute-start | bytes 221192 | tf_op jit(solution)/shard_map/ppermute | solution.py:408
  16.3 9.6 %collective-permute-start.3 = (bf16[288,128]{1,0:T(8,128)(2,1)S(1)}, bf16[288,128]{1,0:T(8,128)(2,1)S(1)}, u32[]{:S(2)}, u32[]{:S(2)}) collective-permute-start(bf16[288,128]{1,0:T(8,128)(2,1)S(1)} %get-tuple-element.51), channel_id=1, source_target_pairs={{0,28},{4,8},{8,4},{12,16},{16,12},{20,24},{24,20},{28,0},{1,29},{... | collective-permute-start | bytes 221192 | tf_op jit(solution)/shard_map/ppermute | solution.py:408
  19.8 3.7 %collective-permute-start.4 = (bf16[64,128]{1,0:T(8,128)(2,1)S(1)}, bf16[64,128]{1,0:T(8,128)(2,1)S(1)}, u32[]{:S(2)}, u32[]{:S(2)}) collective-permute-start(bf16[64,128]{1,0:T(8,128)(2,1)S(1)} %get-tuple-element.52), channel_id=1, source_target_pairs={{0,24},{4,12},{8,0},{12,20},{16,8},{20,28},{24,16},{28,4},{1,25},{... | collective-permute-start | bytes 49160 | tf_op jit(solution)/shard_map/ppermute | solution.py:408
  20.3 5.6 %collective-permute-start.5 = (bf16[64,128]{1,0:T(8,128)(2,1)S(1)}, bf16[64,128]{1,0:T(8,128)(2,1)S(1)}, u32[]{:S(2)}, u32[]{:S(2)}) collective-permute-start(bf16[64,128]{1,0:T(8,128)(2,1)S(1)} %get-tuple-element.53), channel_id=1, source_target_pairs={{0,8},{4,28},{8,16},{12,4},{16,24},{20,12},{24,0},{28,20},{1,9},{5... | collective-permute-start | bytes 49160 | tf_op jit(solution)/shard_map/ppermute | solution.py:408
  21.8 13.2 %copy-start.8 = (f32[128]{0:T(128)S(1)}, f32[128]{0:T(128)}, u32[]{:S(2)}) copy-start(f32[128]{0:T(128)} %param.13) | copy-start | bytes 1540
  26.5 8.5 %collective-permute-start.6 = (bf16[288,128]{1,0:T(8,128)(2,1)S(1)}, bf16[288,128]{1,0:T(8,128)(2,1)S(1)}, u32[]{:S(2)}, u32[]{:S(2)}) collective-permute-start(bf16[288,128]{1,0:T(8,128)(2,1)S(1)} %get-tuple-element.59.mine_near), channel_id=1, source_target_pairs={{0,4},{4,0},{8,12},{12,8},{16,20},{20,16},{24,28},{28,24},{1,5},{5... | collective-permute-start | bytes 221192 | tf_op jit(solution)/shard_map/ppermute | solution.py:408
  26.6 8.4 %collective-permute-start.7 = (bf16[288,128]{1,0:T(8,128)(2,1)S(1)}, bf16[288,128]{1,0:T(8,128)(2,1)S(1)}, u32[]{:S(2)}, u32[]{:S(2)}) collective-permute-start(bf16[288,128]{1,0:T(8,128)(2,1)S(1)} %get-tuple-element.60.mine_over), channel_id=1, source_target_pairs={{0,28},{4,8},{8,4},{12,16},{16,12},{20,24},{24,20},{28,0},{1,29},{... | collective-permute-start | bytes 221192 | tf_op jit(solution)/shard_map/ppermute | solution.py:408
  29.0 3.7 %collective-permute-start.8 = (bf16[64,128]{1,0:T(8,128)(2,1)S(1)}, bf16[64,128]{1,0:T(8,128)(2,1)S(1)}, u32[]{:S(2)}, u32[]{:S(2)}) collective-permute-start(bf16[64,128]{1,0:T(8,128)(2,1)S(1)} %get-tuple-element.62), channel_id=1, source_target_pairs={{0,24},{4,12},{8,0},{12,20},{16,8},{20,28},{24,16},{28,4},{1,25},{... | collective-permute-start | bytes 49160 | tf_op jit(solution)/shard_map/ppermute | solution.py:408
  29.5 5.5 %collective-permute-start.9 = (bf16[64,128]{1,0:T(8,128)(2,1)S(1)}, bf16[64,128]{1,0:T(8,128)(2,1)S(1)}, u32[]{:S(2)}, u32[]{:S(2)}) collective-permute-start(bf16[64,128]{1,0:T(8,128)(2,1)S(1)} %get-tuple-element.63), channel_id=1, source_target_pairs={{0,8},{4,28},{8,16},{12,4},{16,24},{20,12},{24,0},{28,20},{1,9},{5... | collective-permute-start | bytes 49160 | tf_op jit(solution)/shard_map/ppermute | solution.py:408
  36.2 1.2 %collective-permute-start.10 = (f32[1,637]{1,0:T(1,128)S(1)}, f32[1,637]{1,0:T(1,128)S(1)}, u32[]{:S(2)}, u32[]{:S(2)}) collective-permute-start(f32[1,637]{1,0:T(1,128)S(1)} %get-tuple-element.67), channel_id=1, source_target_pairs={{0,1},{1,0},{2,3},{3,2},{4,5},{5,4},{6,7},{7,6},{8,9},{9,8},{10,11... | collective-permute-start | bytes 7652 | tf_op jit(solution)/shard_map/ppermute | solution.py:510
  37.4 3.6 %collective-permute-start.11 = (f32[1,637]{1,0:T(1,128)S(1)}, f32[1,637]{1,0:T(1,128)S(1)}, u32[]{:S(2)}, u32[]{:S(2)}) collective-permute-start(f32[1,637]{1,0:T(1,128)S(1)} %add.6), channel_id=1, source_target_pairs={{0,2},{1,3},{2,0},{3,1},{4,6},{5,7},{6,4},{7,5},{8,10},{9,11},{10,... | collective-permute-start | bytes 7652 | tf_op jit(solution)/shard_map/ppermute | solution.py:510

commit v4 on v3

--- a/solution.py
+++ b/solution.py
@@ -145,6 +145,9 @@
 
 CENTRE = (upper_edge + lower_edge) / 2.0
 
+FIRST_ORDER = (7, 8)
+ORDER = (3, 2, 5, 4)
+
 
 def twice(a, b):
     return jnp.concatenate([a, b, a, b], axis=0).astype(BF16)
@@ -380,17 +383,24 @@
     )
 
 
-def call(kernel, outs, scratch, *args, hbm=0, megabytes=32):
+def call(kernel, outs, scratch, *args, hbm=0, megabytes=32, order=()):
     vmem = pl.BlockSpec(memory_space=pltpu.VMEM)
     far = pl.BlockSpec(memory_space=pltpu.HBM)
+    inputs = len(args)
+    order = list(order) + [i for i in range(inputs) if i not in order]
+    where = [order.index(i) for i in range(inputs)]
+
+    def ordered(*refs):
+        kernel(*(refs[i] for i in where), *refs[inputs:])
+
     return pl.pallas_call(
-        kernel,
-        out_shape=[jax.ShapeDtypeStruct(s, t) for s, t in outs],
-        in_specs=[far] * hbm + [vmem] * (len(args) - hbm),
+        ordered,
+        out_shape=[pltpu.VMEM(s, t) for s, t in outs],
+        in_specs=[far] * hbm + [vmem] * (inputs - hbm),
         out_specs=[vmem] * len(outs),
         scratch_shapes=scratch,
         compiler_params=pltpu.CompilerParams(vmem_limit_bytes=megabytes * 1024 * 1024),
-    )(*args)
+    )(*(args[i] for i in order))
 
 
 def body(filter_input, cell_table, cell_type, atom_center, proj_values, coupling, occupation):
@@ -469,6 +479,7 @@
             [scratch, pltpu.VMEM((2, z.chunks * LANES, states), F32), scratch] + faces,
             base, x0, own0, own1, own_share, near, over, from_near, from_over,
             cell0, mix_high, mix_low, end_rows,
+            order=FIRST_ORDER,
         )
     )
     second = exchange_all(near, over, far, farther)
@@ -484,6 +495,7 @@
         faces,
         base, own_coeffs, *second,
         cell0, cell1, end_rows, rows0, rows1, spread0, spread1, face0, face1,
+        order=ORDER,
     )
     third = exchange_all(near, over, far, farther)
     (base,) = call(
@@ -498,6 +510,7 @@
         [],
         base, own_coeffs, *third,
         cell0, cell1, spread0, spread1, edge0, edge1, occupation[None, :],
+        order=ORDER,
     )
     return filtered, total(density, groups)[0]
 

time: 41.8 us -> 39.4 us (0.943)
  waiting for transfers between devices: 13.3 us -> 7.94 us
  starting transfers between devices: 19.1 us -> 22.4 us
  Pallas kernels: 6.19 us -> 5 us
  local copies, waits for them, and re-layouts: 0.16 us -> 0.86 us
    ppermute x10, waiting for transfers between devices: 10 us -> 5.38 us  [exchanged(): return lax.ppermute(array, 'cells', pairs)]
    ppermute x10, starting transfers between devices: 17.7 us -> 20.9 us  [exchanged(): return lax.ppermute(array, 'cells', pairs)]
    pallas_call x7, Pallas kernels: 6.19 us -> 5 us  [call(): pl.pallas_call(ordered, out_shape=[pltpu.VMEM(s, t) for s, t in outs], in...]
    unnamed x18 -> x7, local copies, waits for them, and re-layouts: 0.04 us -> 0.74 us
    ppermute x2, waiting for transfers between devices: 3.26 us -> 2.56 us  [total(): lax.ppermute(density, 'states', [(i, i ^ step) for i in range(groups)])]
  transfers between devices with their start and end apart: 12 -> 12, of which waited for: 8 -> 7; matrix products, arithmetic and copies ran while one was open for 4% -> 6% of each run, Pallas kernels for 3% -> 4%
where the time goes in v4:
time: 39.4 us; the launch traced here: 39 us
  starting transfers between devices  22.4 us (57%)
  waiting for transfers between devices  7.94 us (20%)
  Pallas kernels  5 us (13%)
  matrix products  1.41 us (4%)
  local copies, waits for them, and re-layouts  0.86 us (2%)
  between operations  0.73 us (2%)
  other arithmetic  0.61 us (2%)
    ppermute x10, starting transfers between devices, exchanged(): return lax.ppermute(array, 'cells', pairs)  20.9 us
    ppermute x10, waiting for transfers between devices, exchanged(): return lax.ppermute(array, 'cells', pairs)  5.38 us
    pallas_call x7, Pallas kernels, call(): pl.pallas_call(ordered, out_shape=[pltpu.VMEM(s, t) for s, t in outs], in...  5 us
    ppermute x2, waiting for transfers between devices, total(): lax.ppermute(density, 'states', [(i, i ^ step) for i in range(groups)])  2.56 us
    ppermute x2, starting transfers between devices, total(): lax.ppermute(density, 'states', [(i, i ^ step) for i in range(groups)])  1.49 us
    dot_general x1, matrix products, body(): jnp.einsum('ct,tij->cij', onehot, cell_table, preferred_element_type=F32)  1.41 us
  transfers between devices with their start and end apart: 12, of which 7 were waited for; matrix products, arithmetic and copies ran while one was open for 6% of the time, Pallas kernels for 4%

profile of v4, /device:TPU:0, one launch (start us, length us, event | category | flops | bytes accessed | tf_op | source)
XLA Modules:
  0.0 39.0 jit_solution(17015735176155349972)
XLA Ops:
  0.6 0.0 copy-start
  0.6 1.3 %shard_map.86 = (bf16[637,128]{1,0:T(8,128)(2,1)S(1)}, bf16[624,128]{1,0:T(8,128)(2,1)S(1)}, bf16[624,128]{1,0:T(8,128)(2,1)S(1)}, bf16[64,343]{1,0:T(8,128)(2,1...) custom-call(s32[4]{0:T(128)} %refs_0_.2, bf16[637,128]{1,0:T(8,128)(2,1)} %refs_1_.1, ...), custom_call_target="tpu_custom_call" | custom-call | tf_op jit(solution)/shard_map/pallas_call | solution.py:396
  2.0 3.0 %collective-permute-start = (bf16[624,128]{1,0:T(8,128)(2,1)S(1)}, bf16[624,128]{1,0:T(8,128)(2,1)S(1)}, u32[]{:S(2)}, u32[]{:S(2)}) collective-permute-start(bf16[624,128]{1,0:T(8,128)(2,1)S(1)} %get-tuple-element.35.refs_7_), channel_id=1, source_target_pairs={{0,4},{4,0},{8,12},{12,8},{16,20},{20,16},{24,28},{28,24},{1,5},{5... | collective-permute-start | bytes 479240 | tf_op jit(solution)/shard_map/ppermute | solution.py:418
  5.0 0.0 copy-start.1
  5.0 3.5 %collective-permute-start.1 = (bf16[624,128]{1,0:T(8,128)(2,1)S(1)}, bf16[624,128]{1,0:T(8,128)(2,1)S(1)}, u32[]{:S(2)}, u32[]{:S(2)}) collective-permute-start(bf16[624,128]{1,0:T(8,128)(2,1)S(1)} %get-tuple-element.36.refs_8_), channel_id=1, source_target_pairs={{0,28},{4,8},{8,4},{12,16},{16,12},{20,24},{24,20},{28,0},{1,29},{... | collective-permute-start | bytes 479240 | tf_op jit(solution)/shard_map/ppermute | solution.py:418
  8.6 0.0 copy-done
  8.6 1.4 %fusion = bf16[2,343,343]{2,0,1:T(2,128)(2,1)S(1)} fusion(bf16[8,343,343]{2,0,1:T(8,128)(2,1)S(1)} %copy-done, s32[2]{0:T(128)} %param.9), kind=kOutput, calls=%fused_computation.4 | convolution fusion | flops 3764784 | bytes 2352988 | tf_op jit(solution)/shard_map/ct,tij->cij/dot_general | solution.py:458
  10.0 0.1 copy.11
  10.1 0.1 slice_bitcast_fusion
  10.1 0.0 copy-done.1
  10.1 0.7 %shard_map.87 = (f32[637,128]{1,0:T(8,128)S(1)}, bf16[128,128]{1,0:T(8,128)(2,1)S(1)}, bf16[128,128]{1,0:T(8,128)(2,1)S(1)}, bf16[64,343]{1,0:T(8,128)(2,1)S(1)}) custom-call(f32[16,16]{1,0:T(8,128)S(1)} %copy-done.1, bf16[637,128]{1,0:T(8,128)(2,1)S(1)} %get-tuple-element.37.refs_1_.refs_3_, bf16[343,343]{1,0:T(8,128)(2,1)S(1)} %get-tuple-element.69.refs_2_.refs_9_.refs_6_, ...), custom_call_target="tpu_custom_call" | custom-call | tf_op jit(solution)/shard_map/pallas_call | solution.py:396
  10.9 0.9 %collective-permute-done.refs_0_ = bf16[624,128]{1,0:T(8,128)(2,1)S(1)} collective-permute-done((bf16[624,128]{1,0:T(8,128)(2,1)S(1)}, bf16[624,128]{1,0:T(8,128)(2,1)S(1)}, u32[]{:S(2)}, u32[]{:S(2)}) %collective-permute-start) | collective-permute-done | bytes 159776 | tf_op jit(solution)/shard_map/ppermute | solution.py:418
  11.8 1.5 %collective-permute-done.1.refs_1_ = bf16[624,128]{1,0:T(8,128)(2,1)S(1)} collective-permute-done((bf16[624,128]{1,0:T(8,128)(2,1)S(1)}, bf16[624,128]{1,0:T(8,128)(2,1)S(1)}, u32[]{:S(2)}, u32[]{:S(2)}) %collective-permute-start.1) | collective-permute-done | bytes 159776 | tf_op jit(solution)/shard_map/ppermute | solution.py:418
  13.3 0.9 %shard_map.88 = (f32[637,128]{1,0:T(8,128)S(1)}, f32[192,128]{1,0:T(8,128)S(1)}, bf16[288,128]{1,0:T(8,128)(2,1)S(1)}, bf16[288,128]{1,0:T(8,128)(2,1)S(1)}, bf1...) custom-call(bf16[624,128]{1,0:T(8,128)(2,1)S(1)} %collective-permute, ...), custom_call_target="tpu_custom_call" | custom-call | tf_op jit(solution)/shard_map/pallas_call | solution.py:396
  14.2 4.1 %collective-permute-start.2 = (bf16[288,128]{1,0:T(8,128)(2,1)S(1)}, bf16[288,128]{1,0:T(8,128)(2,1)S(1)}, u32[]{:S(2)}, u32[]{:S(2)}) collective-permute-start(bf16[288,128]{1,0:T(8,128)(2,1)S(1)} %get-tuple-element.45), channel_id=1, source_target_pairs={{0,28},{4,8},{8,4},{12,16},{16,12},{20,24},{24,20},{28,0},{1,29},{... | collective-permute-start | bytes 221192 | tf_op jit(solution)/shard_map/ppermute | solution.py:418
  18.3 0.0 collective-permute-start.3
  18.3 0.1 collective-permute-start.4
  18.4 3.8 %collective-permute-start.5 = (bf16[64,128]{1,0:T(8,128)(2,1)S(1)}, bf16[64,128]{1,0:T(8,128)(2,1)S(1)}, u32[]{:S(2)}, u32[]{:S(2)}) collective-permute-start(bf16[64,128]{1,0:T(8,128)(2,1)S(1)} %get-tuple-element.48), channel_id=1, source_target_pairs={{0,24},{4,12},{8,0},{12,20},{16,8},{20,28},{24,16},{28,4},{1,25},{... | collective-permute-start | bytes 49160 | tf_op jit(solution)/shard_map/ppermute | solution.py:418
  22.1 0.0 copy-start.2
  22.1 0.3 shard_map.89
  22.5 1.4 %collective-permute-done.4.refs_2_ = bf16[64,128]{1,0:T(8,128)(2,1)S(1)} collective-permute-done((bf16[64,128]{1,0:T(8,128)(2,1)S(1)}, bf16[64,128]{1,0:T(8,128)(2,1)S(1)}, u32[]{:S(2)}, u32[]{:S(2)}) %collective-permute-start.4) | collective-permute-done | bytes 16416 | tf_op jit(solution)/shard_map/ppermute | solution.py:418
  23.9 0.0 collective-permute-done.5.refs_3_
  23.9 0.0 collective-permute-done.2.refs_0_.refs_3_
  23.9 0.0 collective-permute-done.3.refs_1_.refs_2_
  23.9 0.6 %shard_map.90 = (f32[637,128]{1,0:T(8,128)S(1)}, f32[192,128]{1,0:T(8,128)S(1)}, bf16[288,128]{1,0:T(8,128)(2,1)S(1)}, bf16[288,128]{1,0:T(8,128)(2,1)S(1)}, bf1...) custom-call(bf16[288,128]{1,0:T(8,128)(2,1)S(1)} %collective-permute-done.2.refs_0_.refs_3_, ...), custom_call_target="tpu_custom_call" | custom-call | tf_op jit(solution)/shard_map/pallas_call | solution.py:396
  24.5 2.0 %collective-permute-start.6 = (bf16[288,128]{1,0:T(8,128)(2,1)S(1)}, bf16[288,128]{1,0:T(8,128)(2,1)S(1)}, u32[]{:S(2)}, u32[]{:S(2)}) collective-permute-start(bf16[288,128]{1,0:T(8,128)(2,1)S(1)} %get-tuple-element.58.refs_5_), channel_id=1, source_target_pairs={{0,28},{4,8},{8,4},{12,16},{16,12},{20,24},{24,20},{28,0},{1,29},{... | collective-permute-start | bytes 221192 | tf_op jit(solution)/shard_map/ppermute | solution.py:418
  26.5 0.6 %collective-permute-start.7 = (bf16[288,128]{1,0:T(8,128)(2,1)S(1)}, bf16[288,128]{1,0:T(8,128)(2,1)S(1)}, u32[]{:S(2)}, u32[]{:S(2)}) collective-permute-start(bf16[288,128]{1,0:T(8,128)(2,1)S(1)} %get-tuple-element.59.refs_4_), channel_id=1, source_target_pairs={{0,4},{4,0},{8,12},{12,8},{16,20},{20,16},{24,28},{28,24},{1,5},{5... | collective-permute-start | bytes 221192 | tf_op jit(solution)/shard_map/ppermute | solution.py:418
  27.1 1.4 %collective-permute-start.8 = (bf16[64,128]{1,0:T(8,128)(2,1)S(1)}, bf16[64,128]{1,0:T(8,128)(2,1)S(1)}, u32[]{:S(2)}, u32[]{:S(2)}) collective-permute-start(bf16[64,128]{1,0:T(8,128)(2,1)S(1)} %get-tuple-element.60), channel_id=1, source_target_pairs={{0,8},{4,28},{8,16},{12,4},{16,24},{20,12},{24,0},{28,20},{1,9},{5... | collective-permute-start | bytes 49160 | tf_op jit(solution)/shard_map/ppermute | solution.py:418
  28.5 2.4 %collective-permute-start.9 = (bf16[64,128]{1,0:T(8,128)(2,1)S(1)}, bf16[64,128]{1,0:T(8,128)(2,1)S(1)}, u32[]{:S(2)}, u32[]{:S(2)}) collective-permute-start(bf16[64,128]{1,0:T(8,128)(2,1)S(1)} %get-tuple-element.61), channel_id=1, source_target_pairs={{0,24},{4,12},{8,0},{12,20},{16,8},{20,28},{24,16},{28,4},{1,25},{... | collective-permute-start | bytes 49160 | tf_op jit(solution)/shard_map/ppermute | solution.py:418
  30.9 0.3 shard_map.91.refs_4_
  31.2 1.4 %collective-permute-done.8.refs_2_ = bf16[64,128]{1,0:T(8,128)(2,1)S(1)} collective-permute-done((bf16[64,128]{1,0:T(8,128)(2,1)S(1)}, bf16[64,128]{1,0:T(8,128)(2,1)S(1)}, u32[]{:S(2)}, u32[]{:S(2)}) %collective-permute-start.8) | collective-permute-done | bytes 16416 | tf_op jit(solution)/shard_map/ppermute | solution.py:418
  32.6 0.2 collective-permute-done.9.refs_3_
  32.8 0.0 collective-permute-done.6.refs_0_
  32.8 0.0 collective-permute-done.7.refs_1_
  32.8 0.0 copy-done.2
  32.8 0.8 %shard_map.92 = (f32[637,128]{1,0:T(8,128)S(1)}, f32[1,637]{1,0:T(1,128)S(1)}) custom-call(bf16[288,128]{1,0:T(8,128)(2,1)S(1)} %collective-permute-done.6.refs_0_, bf16[288,128]{1,0:T(8,128)(2,1)S(1)} %collective-permute-done.7.refs_1_, bf16[64,128]{1,0:T(8,128)(2,1)S(1)} %collective-permute-done.8.refs_2_, ...), custom_call_target="tpu_custom_call" | custom-call | tf_op jit(solution)/shard_map/pallas_call | solution.py:396
  33.6 0.0 collective-permute-start.10
  33.6 1.2 %collective-permute-done.10 = f32[1,637]{1,0:T(1,128)S(1)} collective-permute-done((f32[1,637]{1,0:T(1,128)S(1)}, f32[1,637]{1,0:T(1,128)S(1)}, u32[]{:S(2)}, u32[]{:S(2)}) %collective-permute-start.10) | collective-permute-done | bytes 2580 | tf_op jit(solution)/shard_map/ppermute | solution.py:523
  34.8 1.5 %collective-permute-start.11 = (f32[1,637]{1,0:T(1,128)S(1)}, f32[1,637]{1,0:T(1,128)S(1)}, u32[]{:S(2)}, u32[]{:S(2)}) collective-permute-start(f32[1,637]{1,0:T(1,128)S(1)} %add.6), channel_id=1, source_target_pairs={{0,2},{1,3},{2,0},{3,1},{4,6},{5,7},{6,4},{7,5},{8,10},{9,11},{10,... | collective-permute-start | bytes 7652 | tf_op jit(solution)/shard_map/ppermute | solution.py:523
  36.3 0.7 %copy.12 = f32[637,128]{1,0:T(8,128)} copy(f32[637,128]{1,0:T(8,128)S(1)} %get-tuple-element.70) | data formatting | bytes 652288
  37.0 1.4 %collective-permute-done.11 = f32[1,637]{1,0:T(1,128)S(1)} collective-permute-done((f32[1,637]{1,0:T(1,128)S(1)}, f32[1,637]{1,0:T(1,128)S(1)}, u32[]{:S(2)}, u32[]{:S(2)}) %collective-permute-start.11) | collective-permute-done | bytes 2580 | tf_op jit(solution)/shard_map/ppermute | solution.py:523
  38.4 0.6 %add_reduce_fusion = f32[637]{0:T(1024)} fusion(f32[1,637]{1,0:T(1,128)S(1)} %add.6, f32[1,637]{1,0:T(1,128)S(1)} %collective-permute-done.11), kind=kLoop, calls=%fused_computation.3 | loop fusion | flops 637 | bytes 7644 | tf_op jit(solution)/shard_map/add | solution.py:523
  (1 shorter events, 0.0 us)
Async XLA Ops:
  0.6 7.9 %copy-start = (bf16[8,343,343]{2,0,1:T(8,128)(2,1)S(1)}, bf16[8,343,343]{2,0,1:T(8,128)(2,1)}, u32[]{:S(2)}) copy-start(bf16[8,343,343]{2,0,1:T(8,128)(2,1)} %param.8) | copy-start | bytes 5647156
  2.0 9.8 %collective-permute-start = (bf16[624,128]{1,0:T(8,128)(2,1)S(1)}, bf16[624,128]{1,0:T(8,128)(2,1)S(1)}, u32[]{:S(2)}, u32[]{:S(2)}) collective-permute-start(bf16[624,128]{1,0:T(8,128)(2,1)S(1)} %get-tuple-element.35.refs_7_), channel_id=1, source_target_pairs={{0,4},{4,0},{8,12},{12,8},{16,20},{20,16},{24,28},{28,24},{1,5},{5... | collective-permute-start | bytes 479240 | tf_op jit(solution)/shard_map/ppermute | solution.py:418
  5.0 5.1 %copy-start.1 = (f32[16,16]{1,0:T(8,128)S(1)}, f32[16,16]{1,0:T(8,128)}, u32[]{:S(2)}) copy-start(f32[16,16]{1,0:T(8,128)} %refs_0_.3) | copy-start | bytes 3076
  5.0 8.3 %collective-permute-start.1 = (bf16[624,128]{1,0:T(8,128)(2,1)S(1)}, bf16[624,128]{1,0:T(8,128)(2,1)S(1)}, u32[]{:S(2)}, u32[]{:S(2)}) collective-permute-start(bf16[624,128]{1,0:T(8,128)(2,1)S(1)} %get-tuple-element.36.refs_8_), channel_id=1, source_target_pairs={{0,28},{4,8},{8,4},{12,16},{16,12},{20,24},{24,20},{28,0},{1,29},{... | collective-permute-start | bytes 479240 | tf_op jit(solution)/shard_map/ppermute | solution.py:418
  14.2 9.7 %collective-permute-start.2 = (bf16[288,128]{1,0:T(8,128)(2,1)S(1)}, bf16[288,128]{1,0:T(8,128)(2,1)S(1)}, u32[]{:S(2)}, u32[]{:S(2)}) collective-permute-start(bf16[288,128]{1,0:T(8,128)(2,1)S(1)} %get-tuple-element.45), channel_id=1, source_target_pairs={{0,28},{4,8},{8,4},{12,16},{16,12},{20,24},{24,20},{28,0},{1,29},{... | collective-permute-start | bytes 221192 | tf_op jit(solution)/shard_map/ppermute | solution.py:418
  18.3 5.5 %collective-permute-start.3 = (bf16[288,128]{1,0:T(8,128)(2,1)S(1)}, bf16[288,128]{1,0:T(8,128)(2,1)S(1)}, u32[]{:S(2)}, u32[]{:S(2)}) collective-permute-start(bf16[288,128]{1,0:T(8,128)(2,1)S(1)} %get-tuple-element.46), channel_id=1, source_target_pairs={{0,4},{4,0},{8,12},{12,8},{16,20},{20,16},{24,28},{28,24},{1,5},{5... | collective-permute-start | bytes 221192 | tf_op jit(solution)/shard_map/ppermute | solution.py:418
  18.3 5.5 %collective-permute-start.4 = (bf16[64,128]{1,0:T(8,128)(2,1)S(1)}, bf16[64,128]{1,0:T(8,128)(2,1)S(1)}, u32[]{:S(2)}, u32[]{:S(2)}) collective-permute-start(bf16[64,128]{1,0:T(8,128)(2,1)S(1)} %get-tuple-element.47), channel_id=1, source_target_pairs={{0,8},{4,28},{8,16},{12,4},{16,24},{20,12},{24,0},{28,20},{1,9},{5... | collective-permute-start | bytes 49160 | tf_op jit(solution)/shard_map/ppermute | solution.py:418
  18.4 5.5 %collective-permute-start.5 = (bf16[64,128]{1,0:T(8,128)(2,1)S(1)}, bf16[64,128]{1,0:T(8,128)(2,1)S(1)}, u32[]{:S(2)}, u32[]{:S(2)}) collective-permute-start(bf16[64,128]{1,0:T(8,128)(2,1)S(1)} %get-tuple-element.48), channel_id=1, source_target_pairs={{0,24},{4,12},{8,0},{12,20},{16,8},{20,28},{24,16},{28,4},{1,25},{... | collective-permute-start | bytes 49160 | tf_op jit(solution)/shard_map/ppermute | solution.py:418
  22.1 10.7 %copy-start.2 = (f32[128]{0:T(128)S(1)}, f32[128]{0:T(128)}, u32[]{:S(2)}) copy-start(f32[128]{0:T(128)} %param.13) | copy-start | bytes 1540
  24.5 8.3 %collective-permute-start.6 = (bf16[288,128]{1,0:T(8,128)(2,1)S(1)}, bf16[288,128]{1,0:T(8,128)(2,1)S(1)}, u32[]{:S(2)}, u32[]{:S(2)}) collective-permute-start(bf16[288,128]{1,0:T(8,128)(2,1)S(1)} %get-tuple-element.58.refs_5_), channel_id=1, source_target_pairs={{0,28},{4,8},{8,4},{12,16},{16,12},{20,24},{24,20},{28,0},{1,29},{... | collective-permute-start | bytes 221192 | tf_op jit(solution)/shard_map/ppermute | solution.py:418
  26.5 6.3 %collective-permute-start.7 = (bf16[288,128]{1,0:T(8,128)(2,1)S(1)}, bf16[288,128]{1,0:T(8,128)(2,1)S(1)}, u32[]{:S(2)}, u32[]{:S(2)}) collective-permute-start(bf16[288,128]{1,0:T(8,128)(2,1)S(1)} %get-tuple-element.59.refs_4_), channel_id=1, source_target_pairs={{0,4},{4,0},{8,12},{12,8},{16,20},{20,16},{24,28},{28,24},{1,5},{5... | collective-permute-start | bytes 221192 | tf_op jit(solution)/shard_map/ppermute | solution.py:418
  27.1 5.5 %collective-permute-start.8 = (bf16[64,128]{1,0:T(8,128)(2,1)S(1)}, bf16[64,128]{1,0:T(8,128)(2,1)S(1)}, u32[]{:S(2)}, u32[]{:S(2)}) collective-permute-start(bf16[64,128]{1,0:T(8,128)(2,1)S(1)} %get-tuple-element.60), channel_id=1, source_target_pairs={{0,8},{4,28},{8,16},{12,4},{16,24},{20,12},{24,0},{28,20},{1,9},{5... | collective-permute-start | bytes 49160 | tf_op jit(solution)/shard_map/ppermute | solution.py:418
  28.5 4.3 %collective-permute-start.9 = (bf16[64,128]{1,0:T(8,128)(2,1)S(1)}, bf16[64,128]{1,0:T(8,128)(2,1)S(1)}, u32[]{:S(2)}, u32[]{:S(2)}) collective-permute-start(bf16[64,128]{1,0:T(8,128)(2,1)S(1)} %get-tuple-element.61), channel_id=1, source_target_pairs={{0,24},{4,12},{8,0},{12,20},{16,8},{20,28},{24,16},{28,4},{1,25},{... | collective-permute-start | bytes 49160 | tf_op jit(solution)/shard_map/ppermute | solution.py:418
  33.6 1.2 %collective-permute-start.10 = (f32[1,637]{1,0:T(1,128)S(1)}, f32[1,637]{1,0:T(1,128)S(1)}, u32[]{:S(2)}, u32[]{:S(2)}) collective-permute-start(f32[1,637]{1,0:T(1,128)S(1)} %get-tuple-element.67), channel_id=1, source_target_pairs={{0,1},{1,0},{2,3},{3,2},{4,5},{5,4},{6,7},{7,6},{8,9},{9,8},{10,11... | collective-permute-start | bytes 7652 | tf_op jit(solution)/shard_map/ppermute | solution.py:523
  34.8 3.6 %collective-permute-start.11 = (f32[1,637]{1,0:T(1,128)S(1)}, f32[1,637]{1,0:T(1,128)S(1)}, u32[]{:S(2)}, u32[]{:S(2)}) collective-permute-start(f32[1,637]{1,0:T(1,128)S(1)} %add.6), channel_id=1, source_target_pairs={{0,2},{1,3},{2,0},{3,1},{4,6},{5,7},{6,4},{7,5},{8,10},{9,11},{10,... | collective-permute-start | bytes 7652 | tf_op jit(solution)/shard_map/ppermute | solution.py:523

commit v5 on v4

--- a/solution.py
+++ b/solution.py
@@ -41,8 +41,7 @@
         self.chunks = -(-cell_nodes // LANES)
         self.tail = cell_nodes - (self.chunks - 1) * LANES
         self.shift = self.stride - (self.chunks - 1) * LANES
-        self.m_face = self.chunks * self.coef
-        self.m_coef = self.m_face + self.coef
+        self.m_coef = self.chunks * self.coef
         self.m_rows = self.m_coef + self.coef
         self.right_lo, self.right_hi = down16(self.last), up16(self.end)
         self.left_lo, self.left_hi = down16(self.face), up16(cell_nodes)
@@ -94,8 +93,6 @@
     ]
     for copy in copies:
         copy.start()
-    near[: z.m_coef, :] = jnp.zeros((z.m_coef, near.shape[1]), BF16)
-    over[: z.m_coef, :] = jnp.zeros((z.m_coef, near.shape[1]), BF16)
     copies[0].wait()
     xs[...] = x0[...].astype(F32)
     put(
@@ -104,33 +101,60 @@
     )
     copies[1].wait()
     copies[2].wait()
+    on0, on1, reach_left, reach_right = [], [], [], []
     for a in range(z.atoms):
         low = center[a] == 0
         before, here, after = proj[a, 0], proj[a, 1], proj[a, 2]
         none = jnp.zeros_like(before)
-        at = slice(a * z.proj, (a + 1) * z.proj)
-        on0 = jnp.where(low, here, before)
-        on1 = jnp.where(low, after, here)
-        own0[at, :] = on0
-        own1[at, :] = on1
-        reach_left = jnp.where(low, before, none)
-        reach_right = jnp.where(low, none, after)
-        for k in range(z.chunks):
-            width = LANES if k < z.chunks - 1 else z.tail
-            cols = slice(k * LANES, k * LANES + width)
-            rows = slice(k * z.coef + a * z.proj, k * z.coef + (a + 1) * z.proj)
-            put(
-                near, over, (rows, slice(0, width)), reach_right[:, cols], reach_left[:, cols]
-            )
-        rows = slice(z.m_face + a * z.proj, z.m_face + (a + 1) * z.proj)
-        wide = jnp.zeros((z.proj, LANES - z.tail), BF16)
-        end = jnp.concatenate([on1[:, (z.chunks - 1) * LANES :], wide], axis=1)
-        put(near, over, (rows, slice(None)), end, on0[:, :LANES])
-    s = dot(own0[...], x0[: z.nodes, :]) + dot(own1[...], xs[z.last :, :].astype(BF16))
-    coeffs[...] = s
-    sent = s.astype(BF16)
-    near[z.m_coef : z.m_rows, :] = sent
-    over[z.m_coef : z.m_rows, :] = sent
+        on0.append(jnp.where(low, here, before))
+        on1.append(jnp.where(low, after, here))
+        reach_left.append(jnp.where(low, before, none))
+        reach_right.append(jnp.where(low, none, after))
+    on0, on1, reach_left, reach_right = (
+        jnp.concatenate(v, axis=0) for v in (on0, on1, reach_left, reach_right)
+    )
+    k_last = (z.chunks - 1) * LANES
+
+    def last_chunk(v):
+        zeros = jnp.zeros((z.coef, LANES - z.tail), BF16)
+        return jnp.concatenate([v[:, k_last:], zeros], axis=1).astype(F32)
+
+    lane = lax.broadcasted_iota(jnp.int32, (z.coef, LANES), 1)
+    on_first = lane < z.face
+    on_last = (lane >= z.shift) & (lane < z.shift + z.face)
+
+    def to_last(v):
+        return pltpu.roll(jnp.where(on_first, v, 0.0), z.shift, 1)
+
+    def to_first(v):
+        return pltpu.roll(jnp.where(on_last, v, 0.0), LANES - z.shift, 1)
+
+    own_first, own_last = on0[:, :LANES].astype(F32), last_chunk(on1)
+    far_first, far_last = reach_right[:, :LANES].astype(F32), last_chunk(reach_left)
+    own0[:, :LANES] = (own_first + to_first(far_last)).astype(BF16)
+    own0[:, LANES:] = on0[:, LANES:]
+    own1[:, :k_last] = on1[:, :k_last]
+    own1[:, k_last:] = (own_last + to_last(far_first)).astype(BF16)[:, : z.tail]
+    for k in range(z.chunks):
+        cols = slice(k * LANES, (k + 1) * LANES)
+        to_right, to_left = reach_right[:, cols], reach_left[:, cols]
+        if k == z.chunks - 1:
+            to_right = last_chunk(reach_right).astype(BF16)
+            to_left = (far_last + to_last(own_first)).astype(BF16)
+        if k == 0:
+            to_right = (far_first + to_first(own_last)).astype(BF16)
+        put(near, over, (slice(k * z.coef, (k + 1) * z.coef), slice(None)), to_right, to_left)
+    row = lax.broadcasted_iota(jnp.int32, (z.nodes, 1), 0)
+    x_first, x_last = xs[: z.nodes, :], xs[z.last :, :]
+    first = dot(own0[...], x_first.astype(BF16))
+    last = dot(own1[...], x_last.astype(BF16))
+    inner_first = dot(own0[...], jnp.where(row < z.face, 0.0, x_first).astype(BF16))
+    inner_last = dot(own1[...], jnp.where(row >= z.stride, 0.0, x_last).astype(BF16))
+    coeffs[...] = inner_first + inner_last
+    put(
+        near, over, (slice(z.m_coef, z.m_rows), slice(None)),
+        (first + inner_last).astype(BF16), (inner_first + last).astype(BF16),
+    )
 
 
 def add_cells(z, term0, term1, out):
@@ -154,7 +178,7 @@
 
 
 def send_part(
-    z, rows0, rows1, face0, face1, end0, end1, part, coeffs, near, over, far, farther, first, last
+    z, rows0, rows1, end0, end1, part, coeffs, near, over, far, farther, first, last
 ):
     c = z.coef
     last[...] = jnp.zeros_like(last)
@@ -164,8 +188,7 @@
     last_rows, first_rows = last[...].astype(BF16), first[...].astype(BF16)
     put(near, over, (slice(z.l_face, z.l_term), slice(None)), last_rows, first_rows)
     on0, on1 = part[: z.nodes, :].astype(BF16), part[z.last :, :].astype(BF16)
-    s0 = dot(rows0[...], on0) + dot(face0[:, : z.span], first_rows)
-    s1 = dot(rows1[...], on1) + dot(face1[:, : z.span], last_rows)
+    s0, s1 = dot(rows0[...], on0), dot(rows1[...], on1)
     before, own, after = s0[c:], s0[:c] + s1[:c], s1[c:]
     coeffs[:c, :] = before
     coeffs[c : 2 * c, :] = own
@@ -249,7 +272,7 @@
     base, x0, own0, own1, own_coeffs, mine_near, mine_over, from_near, from_over,
     cell0, mix_high, mix_low, end_rows,
     part, coeffs, near, over, far, farther,
-    rows0, rows1, spread0, spread1, face0, face1,
+    rows0, rows1, spread0, spread1, inner0, inner1,
     xs, ext, terms, first, last,
 ):
     c, k_last = z.coef, (z.chunks - 1) * LANES
@@ -264,16 +287,24 @@
         )
     spread0[...] = mixed(rows0[...].T, mix_high, mix_low)
     spread1[...] = mixed(rows1[...].T, mix_high, mix_low)
+    inner0[...] = spread0[...]
+    inner1[...] = spread1[...]
+    top = inner0[: z.pad_face, :]
+    row = lax.broadcasted_iota(jnp.int32, top.shape, 0)
+    lane = lax.broadcasted_iota(jnp.int32, top.shape, 1)
+    shared = (row < z.face) & (lax.rem(lane, 2 * c) >= c)
+    inner0[: z.pad_face, :] = jnp.where(shared, 0.0, top.astype(F32)).astype(BF16)
+    start = down16(z.stride)
+    top = inner1[start:, :]
+    row = lax.broadcasted_iota(jnp.int32, top.shape, 0)
+    lane = lax.broadcasted_iota(jnp.int32, top.shape, 1)
+    shared = (row >= z.stride - start) & (lax.rem(lane, 2 * c) >= c)
+    inner1[start:, :] = jnp.where(shared, 0.0, top.astype(F32)).astype(BF16)
     chunks = [
         take(mine_near, mine_over, (slice(k * c, (k + 1) * c), slice(None)))
         for k in range(z.chunks)
     ]
-    face0[:c, :] = chunks[-1][0]
-    face1[:c, :] = chunks[0][1]
-    face0[c:, :], face1[c:, :] = take(
-        from_near, from_over, (slice(z.m_face, z.m_coef), slice(None))
-    )
-    ext[...] = jnp.zeros_like(ext)
+    ext[:, z.nodes :, :] = jnp.zeros((2, ext.shape[1] - z.nodes, ext.shape[2]), F32)
     halo = take(from_near, from_over, (slice(z.m_rows, z.first), slice(None)))
     skip = z.last - z.right_lo
     ext[0, : z.stride, :] = halo[0].astype(F32)[skip : skip + z.stride]
@@ -291,11 +322,11 @@
     after = after.astype(F32) + dot(rows1[c:, :], xs[z.last :, :].astype(BF16))
     terms[...] = base[...]
     add_cells(
-        z, dot(spread0[...], twice(own, before)), dot(spread1[...], twice(own, after)), terms
+        z, dot(inner0[...], twice(own, before)), dot(inner1[...], twice(own, after)), terms
     )
     part[...] = terms[...] * gain
     send_part(
-        z, rows0, rows1, face0, face1, None, None,
+        z, rows0, rows1, None, None,
         part, coeffs, near, over, far, farther, first, last,
     )
     wide = jnp.zeros((z.pad_face, LANES - z.tail), BF16)
@@ -305,8 +336,7 @@
     )
 
 
-def beside_second(z, gain, back, part, x0, cell0, cell1, mix_high, mix_low, face0, face1,
-                  base, edge0, edge1):
+def beside_second(z, gain, back, part, x0, cell0, cell1, base):
     scale = face_scale(z)
     base[...] = scale * ((-CENTRE * gain) * part[...] - back * x0[...].astype(F32))
     add_cells(
@@ -315,26 +345,24 @@
         gain * dot(cell1[...], part[z.last :, :].astype(BF16)),
         base,
     )
-    edge0[...] = mixed(face0[...].T, mix_high, mix_low)
-    edge1[...] = mixed(face1[...].T, mix_high, mix_low)
 
 
 def second_kernel(
     z, gain,
     base, own_coeffs, from_near, from_over, from_far, from_farther,
-    cell0, cell1, end_rows, rows0, rows1, spread0, spread1, face0, face1,
+    cell0, cell1, end_rows, rows0, rows1, inner0, inner1,
     part, coeffs, near, over, far, farther,
     first_rows, last_rows,
 ):
     s = whole_coeffs(z, own_coeffs, from_near, from_over, from_far, from_farther)
-    term0, term1 = neighbour_terms(z, s, from_near, from_over, cell0, cell1, spread0, spread1)
+    term0, term1 = neighbour_terms(z, s, from_near, from_over, cell0, cell1, inner0, inner1)
     part[...] = base[...]
     add_cells(z, gain * term0, gain * term1, part)
     first, last = face_rows(z, from_near, from_over)
     part[: z.face, :] -= (0.5 * CENTRE * gain) * first
     part[z.end :, :] -= (0.5 * CENTRE * gain) * last
     send_part(
-        z, rows0, rows1, face0, face1, cell0, end_rows,
+        z, rows0, rows1, cell0, end_rows,
         part, coeffs, near, over, far, farther, first_rows, last_rows,
     )
 
@@ -358,19 +386,16 @@
 def third_kernel(
     z, gain, share,
     base, own_coeffs, from_near, from_over, from_far, from_farther,
-    cell0, cell1, spread0, spread1, edge0, edge1, occupation,
+    cell0, cell1, spread0, spread1, occupation,
     out, density,
 ):
     s = whole_coeffs(z, own_coeffs, from_near, from_over, from_far, from_farther)
-    before, own, after = s
     term0, term1 = neighbour_terms(z, s, from_near, from_over, cell0, cell1, spread0, spread1)
     out[...] = base[...]
     add_cells(z, gain * term0, gain * term1, out)
     first, last = face_rows(z, from_near, from_over)
     terms = take(from_near, from_over, (slice(z.l_term, z.later), slice(None)))
     left, right = (v.astype(F32)[: z.face] for v in terms)
-    left += dot(edge0[...], twice(own, before))[z.shift : z.shift + z.face]
-    right += dot(edge1[...], twice(own, after))[: z.face]
     out[: z.face, :] += gain * (left - CENTRE * first)
     out[z.end :, :] += gain * (right - CENTRE * last)
     result = out[...]
@@ -468,14 +493,13 @@
     coeffs = ((3 * c, states), F32)
     messages = [((z.later, states), BF16)] * 2 + [((c, states), BF16)] * 2
     faces = [pltpu.VMEM((z.span, states), F32)] * 2
-    part1, own_coeffs, near, over, far, farther, rows0, rows1, spread0, spread1, face0, face1 = (
+    part1, own_coeffs, near, over, far, farther, rows0, rows1, spread0, spread1, inner0, inner1 = (
         call(
             functools.partial(first_kernel, z, gains[0]),
             [field, coeffs]
             + messages
             + [((2 * c, n), BF16)] * 2
-            + [((n, 4 * c), BF16)] * 2
-            + [((2 * c, LANES), BF16)] * 2,
+            + [((n, 4 * c), BF16)] * 4,
             [scratch, pltpu.VMEM((2, z.chunks * LANES, states), F32), scratch] + faces,
             base, x0, own0, own1, own_share, near, over, from_near, from_over,
             cell0, mix_high, mix_low, end_rows,
@@ -483,18 +507,18 @@
         )
     )
     second = exchange_all(near, over, far, farther)
-    base, edge0, edge1 = call(
+    (base,) = call(
         functools.partial(beside_second, z, gains[1], backs[1]),
-        [field] + [((LANES, 4 * c), BF16)] * 2,
+        [field],
         [],
-        part1, x0, cell0, cell1, mix_high, mix_low, face0, face1,
+        part1, x0, cell0, cell1,
     )
     part2, own_coeffs, near, over, far, farther = call(
         functools.partial(second_kernel, z, gains[1]),
         [field, coeffs] + messages,
         faces,
         base, own_coeffs, *second,
-        cell0, cell1, end_rows, rows0, rows1, spread0, spread1, face0, face1,
+        cell0, cell1, end_rows, rows0, rows1, inner0, inner1,
         order=ORDER,
     )
     third = exchange_all(near, over, far, farther)
@@ -509,7 +533,7 @@
         [field, ((1, rows), F32)],
         [],
         base, own_coeffs, *third,
-        cell0, cell1, spread0, spread1, edge0, edge1, occupation[None, :],
+        cell0, cell1, spread0, spread1, occupation[None, :],
         order=ORDER,
     )
     return filtered, total(density, groups)[0]
@@ -518,9 +542,15 @@
 def total(density, groups):
     if groups & (groups - 1):
         return lax.psum(density, "states")
+
+    def partner(array, by):
+        return lax.ppermute(array, "states", [(i, i ^ by) for i in range(groups)])
+
+    if groups <= 4:
+        return sum((partner(density, by) for by in range(1, groups)), density)
     step = 1
     while step < groups:
-        density += lax.ppermute(density, "states", [(i, i ^ step) for i in range(groups)])
+        density += partner(density, step)
         step *= 2
     return density
 

time: 39.4 us -> 38.2 us (0.970)
  the two profiles are of different devices: /device:TPU:0 before, /device:TPU:5 now
where the time goes in v5:
time: 38.2 us; the launch traced here: 38 us
  starting transfers between devices  17.8 us (47%)
  waiting for transfers between devices  11.6 us (30%)
  Pallas kernels  5 us (13%)
  matrix products  1.41 us (4%)
  local copies, waits for them, and re-layouts  0.87 us (2%)
  between operations  0.76 us (2%)
  other arithmetic  0.61 us (2%)
    ppermute x10, starting transfers between devices, exchanged(): return lax.ppermute(array, 'cells', pairs)  11 us
    ppermute x10, waiting for transfers between devices, exchanged(): return lax.ppermute(array, 'cells', pairs)  10.3 us
    ppermute x3, starting transfers between devices, partner(): return lax.ppermute(array, 'states', [(i, i ^ by) for i in range(groups)])  6.83 us
    pallas_call x7, Pallas kernels, call(): pl.pallas_call(ordered, out_shape=[pltpu.VMEM(s, t) for s, t in outs], in...  5 us
    dot_general x1, matrix products, body(): jnp.einsum('ct,tij->cij', onehot, cell_table, preferred_element_type=F32)  1.41 us
    ppermute x3, waiting for transfers between devices, partner(): return lax.ppermute(array, 'states', [(i, i ^ by) for i in range(groups)])  1.28 us
  transfers between devices with their start and end apart: 13, of which 7 were waited for; matrix products, arithmetic and copies ran while one was open for 6% of the time, Pallas kernels for 4%

profile of v5, /device:TPU:5, one launch (start us, length us, event | category | flops | bytes accessed | tf_op | source)
XLA Modules:
  0.0 38.0 jit_solution(3381982094851740933)
XLA Ops:
  0.6 0.0 copy-start
  0.6 1.4 %shard_map.86 = (bf16[637,128]{1,0:T(8,128)(2,1)S(1)}, bf16[560,128]{1,0:T(8,128)(2,1)S(1)}, bf16[560,128]{1,0:T(8,128)(2,1)S(1)}, bf16[64,343]{1,0:T(8,128)(2,1...) custom-call(s32[4]{0:T(128)} %refs_0_.2, bf16[637,128]{1,0:T(8,128)(2,1)} %refs_1_.1, ...), custom_call_target="tpu_custom_call" | custom-call | tf_op jit(solution)/shard_map/pallas_call | solution.py:421
  2.1 0.1 collective-permute-start
  2.2 0.0 copy-start.1
  2.2 2.5 %collective-permute-start.1 = (bf16[560,128]{1,0:T(8,128)(2,1)S(1)}, bf16[560,128]{1,0:T(8,128)(2,1)S(1)}, u32[]{:S(2)}, u32[]{:S(2)}) collective-permute-start(bf16[560,128]{1,0:T(8,128)(2,1)S(1)} %get-tuple-element.33.refs_8_), channel_id=1, source_target_pairs={{0,28},{4,8},{8,4},{12,16},{16,12},{20,24},{24,20},{28,0},{1,29},{... | collective-permute-start | bytes 430088 | tf_op jit(solution)/shard_map/ppermute | solution.py:443
  4.6 0.0 copy-done
  4.7 1.4 %fusion = bf16[2,343,343]{2,0,1:T(2,128)(2,1)S(1)} fusion(bf16[8,343,343]{2,0,1:T(8,128)(2,1)S(1)} %copy-done, s32[2]{0:T(128)} %param.9), kind=kOutput, calls=%fused_computation.4 | convolution fusion | flops 3764784 | bytes 2352988 | tf_op jit(solution)/shard_map/ct,tij->cij/dot_general | solution.py:483
  6.1 0.1 copy.11
  6.1 0.1 slice_bitcast_fusion
  6.2 0.0 copy-done.1
  6.2 0.7 %shard_map.87 = (f32[637,128]{1,0:T(8,128)S(1)}, bf16[128,128]{1,0:T(8,128)(2,1)S(1)}, bf16[128,128]{1,0:T(8,128)(2,1)S(1)}, bf16[64,343]{1,0:T(8,128)(2,1)S(1)}) custom-call(f32[16,16]{1,0:T(8,128)S(1)} %copy-done.1, bf16[637,128]{1,0:T(8,128)(2,1)S(1)} %get-tuple-element.34.refs_1_.refs_3_, bf16[343,343]{1,0:T(8,128)(2,1)S(1)} %get-tuple-element.63.refs_2_.refs_9_.refs_6_, ...), custom_call_target="tpu_custom_call" | custom-call | tf_op jit(solution)/shard_map/pallas_call | solution.py:421
  7.0 2.9 %collective-permute-done.refs_0_ = bf16[560,128]{1,0:T(8,128)(2,1)S(1)} collective-permute-done((bf16[560,128]{1,0:T(8,128)(2,1)S(1)}, bf16[560,128]{1,0:T(8,128)(2,1)S(1)}, u32[]{:S(2)}, u32[]{:S(2)}) %collective-permute-start) | collective-permute-done | bytes 143392 | tf_op jit(solution)/shard_map/ppermute | solution.py:443
  9.9 0.0 collective-permute-done.1.refs_1_
  9.9 0.9 %shard_map.88 = (f32[637,128]{1,0:T(8,128)S(1)}, f32[192,128]{1,0:T(8,128)S(1)}, bf16[288,128]{1,0:T(8,128)(2,1)S(1)}, bf16[288,128]{1,0:T(8,128)(2,1)S(1)}, bf1...) custom-call(bf16[560,128]{1,0:T(8,128)(2,1)S(1)} %collective-permute, ...), custom_call_target="tpu_custom_call" | custom-call | tf_op jit(solution)/shard_map/pallas_call | solution.py:421
  10.8 0.2 collective-permute-start.2
  11.0 3.9 %collective-permute-start.3 = (bf16[288,128]{1,0:T(8,128)(2,1)S(1)}, bf16[288,128]{1,0:T(8,128)(2,1)S(1)}, u32[]{:S(2)}, u32[]{:S(2)}) collective-permute-start(bf16[288,128]{1,0:T(8,128)(2,1)S(1)} %get-tuple-element.43), channel_id=1, source_target_pairs={{0,4},{4,0},{8,12},{12,8},{16,20},{20,16},{24,28},{28,24},{1,5},{5... | collective-permute-start | bytes 221192 | tf_op jit(solution)/shard_map/ppermute | solution.py:443
  14.9 0.6 %collective-permute-start.4 = (bf16[64,128]{1,0:T(8,128)(2,1)S(1)}, bf16[64,128]{1,0:T(8,128)(2,1)S(1)}, u32[]{:S(2)}, u32[]{:S(2)}) collective-permute-start(bf16[64,128]{1,0:T(8,128)(2,1)S(1)} %get-tuple-element.44), channel_id=1, source_target_pairs={{0,8},{4,28},{8,16},{12,4},{16,24},{20,12},{24,0},{28,20},{1,9},{5... | collective-permute-start | bytes 49160 | tf_op jit(solution)/shard_map/ppermute | solution.py:443
  15.5 0.8 %collective-permute-start.5 = (bf16[64,128]{1,0:T(8,128)(2,1)S(1)}, bf16[64,128]{1,0:T(8,128)(2,1)S(1)}, u32[]{:S(2)}, u32[]{:S(2)}) collective-permute-start(bf16[64,128]{1,0:T(8,128)(2,1)S(1)} %get-tuple-element.45), channel_id=1, source_target_pairs={{0,24},{4,12},{8,0},{12,20},{16,8},{20,28},{24,16},{28,4},{1,25},{... | collective-permute-start | bytes 49160 | tf_op jit(solution)/shard_map/ppermute | solution.py:443
  16.3 0.3 shard_map.89.refs_4_
  16.6 0.0 copy-start.2
  16.6 0.8 %collective-permute-done.4.refs_2_ = bf16[64,128]{1,0:T(8,128)(2,1)S(1)} collective-permute-done((bf16[64,128]{1,0:T(8,128)(2,1)S(1)}, bf16[64,128]{1,0:T(8,128)(2,1)S(1)}, u32[]{:S(2)}, u32[]{:S(2)}) %collective-permute-start.4) | collective-permute-done | bytes 16416 | tf_op jit(solution)/shard_map/ppermute | solution.py:443
  17.5 2.4 %collective-permute-done.5.refs_3_ = bf16[64,128]{1,0:T(8,128)(2,1)S(1)} collective-permute-done((bf16[64,128]{1,0:T(8,128)(2,1)S(1)}, bf16[64,128]{1,0:T(8,128)(2,1)S(1)}, u32[]{:S(2)}, u32[]{:S(2)}) %collective-permute-start.5) | collective-permute-done | bytes 16416 | tf_op jit(solution)/shard_map/ppermute | solution.py:443
  19.9 0.0 collective-permute-done.2.refs_0_.refs_3_
  19.9 0.0 collective-permute-done.3.refs_1_.refs_2_
  19.9 0.5 %shard_map.90 = (f32[637,128]{1,0:T(8,128)S(1)}, f32[192,128]{1,0:T(8,128)S(1)}, bf16[288,128]{1,0:T(8,128)(2,1)S(1)}, bf16[288,128]{1,0:T(8,128)(2,1)S(1)}, bf1...) custom-call(bf16[288,128]{1,0:T(8,128)(2,1)S(1)} %collective-permute-done.2.refs_0_.refs_3_, ...), custom_call_target="tpu_custom_call" | custom-call | tf_op jit(solution)/shard_map/pallas_call | solution.py:421
  20.4 0.1 collective-permute-start.6
  20.5 1.2 %collective-permute-start.7 = (bf16[288,128]{1,0:T(8,128)(2,1)S(1)}, bf16[288,128]{1,0:T(8,128)(2,1)S(1)}, u32[]{:S(2)}, u32[]{:S(2)}) collective-permute-start(bf16[288,128]{1,0:T(8,128)(2,1)S(1)} %get-tuple-element.53.refs_4_), channel_id=1, source_target_pairs={{0,4},{4,0},{8,12},{12,8},{16,20},{20,16},{24,28},{28,24},{1,5},{5... | collective-permute-start | bytes 221192 | tf_op jit(solution)/shard_map/ppermute | solution.py:443
  21.7 1.7 %collective-permute-start.8 = (bf16[64,128]{1,0:T(8,128)(2,1)S(1)}, bf16[64,128]{1,0:T(8,128)(2,1)S(1)}, u32[]{:S(2)}, u32[]{:S(2)}) collective-permute-start(bf16[64,128]{1,0:T(8,128)(2,1)S(1)} %get-tuple-element.54), channel_id=1, source_target_pairs={{0,8},{4,28},{8,16},{12,4},{16,24},{20,12},{24,0},{28,20},{1,9},{5... | collective-permute-start | bytes 49160 | tf_op jit(solution)/shard_map/ppermute | solution.py:443
  23.4 0.0 collective-permute-start.9
  23.4 0.3 shard_map.91.refs_4_
  23.7 0.6 %collective-permute-done.8.refs_2_ = bf16[64,128]{1,0:T(8,128)(2,1)S(1)} collective-permute-done((bf16[64,128]{1,0:T(8,128)(2,1)S(1)}, bf16[64,128]{1,0:T(8,128)(2,1)S(1)}, u32[]{:S(2)}, u32[]{:S(2)}) %collective-permute-start.8) | collective-permute-done | bytes 16416 | tf_op jit(solution)/shard_map/ppermute | solution.py:443
  24.3 3.5 %collective-permute-done.9.refs_3_ = bf16[64,128]{1,0:T(8,128)(2,1)S(1)} collective-permute-done((bf16[64,128]{1,0:T(8,128)(2,1)S(1)}, bf16[64,128]{1,0:T(8,128)(2,1)S(1)}, u32[]{:S(2)}, u32[]{:S(2)}) %collective-permute-start.9) | collective-permute-done | bytes 16416 | tf_op jit(solution)/shard_map/ppermute | solution.py:443
  27.8 0.0 collective-permute-done.6.refs_0_
  27.8 0.0 collective-permute-done.7.refs_1_
  27.8 0.0 copy-done.2
  27.8 0.8 %shard_map.92 = (f32[637,128]{1,0:T(8,128)S(1)}, f32[1,637]{1,0:T(1,128)S(1)}) custom-call(bf16[288,128]{1,0:T(8,128)(2,1)S(1)} %collective-permute-done.6.refs_0_, bf16[288,128]{1,0:T(8,128)(2,1)S(1)} %collective-permute-done.7.refs_1_, bf16[64,128]{1,0:T(8,128)(2,1)S(1)} %collective-permute-done.8.refs_2_, ...), custom_call_target="tpu_custom_call" | custom-call | tf_op jit(solution)/shard_map/pallas_call | solution.py:421
  28.6 6.4 %collective-permute-start.12 = (f32[1,637]{1,0:T(1,128)S(1)}, f32[1,637]{1,0:T(1,128)S(1)}, u32[]{:S(2)}, u32[]{:S(2)}) collective-permute-start(f32[1,637]{1,0:T(1,128)S(1)} %get-tuple-element.61), channel_id=1, source_target_pairs={{0,3},{1,2},{2,1},{3,0},{4,7},{5,6},{6,5},{7,4},{8,11},{9,10},{10,... | collective-permute-start | bytes 7652 | tf_op jit(solution)/shard_map/ppermute | solution.py:547
  35.0 0.3 collective-permute-start.11
  35.2 0.2 collective-permute-start.10
  35.4 0.7 %copy.12 = f32[637,128]{1,0:T(8,128)} copy(f32[637,128]{1,0:T(8,128)S(1)} %get-tuple-element.64) | data formatting | bytes 652288
  36.1 0.4 collective-permute-done.12
  36.5 0.9 %collective-permute-done.11 = f32[1,637]{1,0:T(1,128)S(1)} collective-permute-done((f32[1,637]{1,0:T(1,128)S(1)}, f32[1,637]{1,0:T(1,128)S(1)}, u32[]{:S(2)}, u32[]{:S(2)}) %collective-permute-start.11) | collective-permute-done | bytes 2580 | tf_op jit(solution)/shard_map/ppermute | solution.py:547
  37.4 0.0 collective-permute-done.10
  37.4 0.6 %add_reduce_fusion = f32[637]{0:T(1024)} fusion(f32[1,637]{1,0:T(1,128)S(1)} %collective-permute-done.12, f32[1,637]{1,0:T(1,128)S(1)} %collective-permute-done.11, f32[1,637]{1,0:T(1,128)S(1)} %get-tuple-element.61, f32[1,637]{1,0:T(1,128)S(1)} %collective-permute-done.10), kind=kLoop, calls=%fused_computation.3 | loop fusion | flops 1911 | bytes 12740 | tf_op jit(solution)/shard_map/add | solution.py:550
Async XLA Ops:
  0.6 4.0 %copy-start = (bf16[8,343,343]{2,0,1:T(8,128)(2,1)S(1)}, bf16[8,343,343]{2,0,1:T(8,128)(2,1)}, u32[]{:S(2)}) copy-start(bf16[8,343,343]{2,0,1:T(8,128)(2,1)} %param.8) | copy-start | bytes 5647156
  2.1 7.8 %collective-permute-start = (bf16[560,128]{1,0:T(8,128)(2,1)S(1)}, bf16[560,128]{1,0:T(8,128)(2,1)S(1)}, u32[]{:S(2)}, u32[]{:S(2)}) collective-permute-start(bf16[560,128]{1,0:T(8,128)(2,1)S(1)} %get-tuple-element.32.refs_7_), channel_id=1, source_target_pairs={{0,4},{4,0},{8,12},{12,8},{16,20},{20,16},{24,28},{28,24},{1,5},{5... | collective-permute-start | bytes 430088 | tf_op jit(solution)/shard_map/ppermute | solution.py:443
  2.2 4.0 %copy-start.1 = (f32[16,16]{1,0:T(8,128)S(1)}, f32[16,16]{1,0:T(8,128)}, u32[]{:S(2)}) copy-start(f32[16,16]{1,0:T(8,128)} %refs_0_.3) | copy-start | bytes 3076
  2.2 7.7 %collective-permute-start.1 = (bf16[560,128]{1,0:T(8,128)(2,1)S(1)}, bf16[560,128]{1,0:T(8,128)(2,1)S(1)}, u32[]{:S(2)}, u32[]{:S(2)}) collective-permute-start(bf16[560,128]{1,0:T(8,128)(2,1)S(1)} %get-tuple-element.33.refs_8_), channel_id=1, source_target_pairs={{0,28},{4,8},{8,4},{12,16},{16,12},{20,24},{24,20},{28,0},{1,29},{... | collective-permute-start | bytes 430088 | tf_op jit(solution)/shard_map/ppermute | solution.py:443
  10.8 9.1 %collective-permute-start.2 = (bf16[288,128]{1,0:T(8,128)(2,1)S(1)}, bf16[288,128]{1,0:T(8,128)(2,1)S(1)}, u32[]{:S(2)}, u32[]{:S(2)}) collective-permute-start(bf16[288,128]{1,0:T(8,128)(2,1)S(1)} %get-tuple-element.42), channel_id=1, source_target_pairs={{0,28},{4,8},{8,4},{12,16},{16,12},{20,24},{24,20},{28,0},{1,29},{... | collective-permute-start | bytes 221192 | tf_op jit(solution)/shard_map/ppermute | solution.py:443
  11.0 8.9 %collective-permute-start.3 = (bf16[288,128]{1,0:T(8,128)(2,1)S(1)}, bf16[288,128]{1,0:T(8,128)(2,1)S(1)}, u32[]{:S(2)}, u32[]{:S(2)}) collective-permute-start(bf16[288,128]{1,0:T(8,128)(2,1)S(1)} %get-tuple-element.43), channel_id=1, source_target_pairs={{0,4},{4,0},{8,12},{12,8},{16,20},{20,16},{24,28},{28,24},{1,5},{5... | collective-permute-start | bytes 221192 | tf_op jit(solution)/shard_map/ppermute | solution.py:443
  14.9 2.6 %collective-permute-start.4 = (bf16[64,128]{1,0:T(8,128)(2,1)S(1)}, bf16[64,128]{1,0:T(8,128)(2,1)S(1)}, u32[]{:S(2)}, u32[]{:S(2)}) collective-permute-start(bf16[64,128]{1,0:T(8,128)(2,1)S(1)} %get-tuple-element.44), channel_id=1, source_target_pairs={{0,8},{4,28},{8,16},{12,4},{16,24},{20,12},{24,0},{28,20},{1,9},{5... | collective-permute-start | bytes 49160 | tf_op jit(solution)/shard_map/ppermute | solution.py:443
  15.5 4.4 %collective-permute-start.5 = (bf16[64,128]{1,0:T(8,128)(2,1)S(1)}, bf16[64,128]{1,0:T(8,128)(2,1)S(1)}, u32[]{:S(2)}, u32[]{:S(2)}) collective-permute-start(bf16[64,128]{1,0:T(8,128)(2,1)S(1)} %get-tuple-element.45), channel_id=1, source_target_pairs={{0,24},{4,12},{8,0},{12,20},{16,8},{20,28},{24,16},{28,4},{1,25},{... | collective-permute-start | bytes 49160 | tf_op jit(solution)/shard_map/ppermute | solution.py:443
  16.6 11.2 %copy-start.2 = (f32[128]{0:T(128)S(1)}, f32[128]{0:T(128)}, u32[]{:S(2)}) copy-start(f32[128]{0:T(128)} %param.13) | copy-start | bytes 1540
  20.4 7.3 %collective-permute-start.6 = (bf16[288,128]{1,0:T(8,128)(2,1)S(1)}, bf16[288,128]{1,0:T(8,128)(2,1)S(1)}, u32[]{:S(2)}, u32[]{:S(2)}) collective-permute-start(bf16[288,128]{1,0:T(8,128)(2,1)S(1)} %get-tuple-element.52.refs_5_), channel_id=1, source_target_pairs={{0,28},{4,8},{8,4},{12,16},{16,12},{20,24},{24,20},{28,0},{1,29},{... | collective-permute-start | bytes 221192 | tf_op jit(solution)/shard_map/ppermute | solution.py:443
  20.5 7.3 %collective-permute-start.7 = (bf16[288,128]{1,0:T(8,128)(2,1)S(1)}, bf16[288,128]{1,0:T(8,128)(2,1)S(1)}, u32[]{:S(2)}, u32[]{:S(2)}) collective-permute-start(bf16[288,128]{1,0:T(8,128)(2,1)S(1)} %get-tuple-element.53.refs_4_), channel_id=1, source_target_pairs={{0,4},{4,0},{8,12},{12,8},{16,20},{20,16},{24,28},{28,24},{1,5},{5... | collective-permute-start | bytes 221192 | tf_op jit(solution)/shard_map/ppermute | solution.py:443
  21.7 2.6 %collective-permute-start.8 = (bf16[64,128]{1,0:T(8,128)(2,1)S(1)}, bf16[64,128]{1,0:T(8,128)(2,1)S(1)}, u32[]{:S(2)}, u32[]{:S(2)}) collective-permute-start(bf16[64,128]{1,0:T(8,128)(2,1)S(1)} %get-tuple-element.54), channel_id=1, source_target_pairs={{0,8},{4,28},{8,16},{12,4},{16,24},{20,12},{24,0},{28,20},{1,9},{5... | collective-permute-start | bytes 49160 | tf_op jit(solution)/shard_map/ppermute | solution.py:443
  23.4 4.4 %collective-permute-start.9 = (bf16[64,128]{1,0:T(8,128)(2,1)S(1)}, bf16[64,128]{1,0:T(8,128)(2,1)S(1)}, u32[]{:S(2)}, u32[]{:S(2)}) collective-permute-start(bf16[64,128]{1,0:T(8,128)(2,1)S(1)} %get-tuple-element.55), channel_id=1, source_target_pairs={{0,24},{4,12},{8,0},{12,20},{16,8},{20,28},{24,16},{28,4},{1,25},{... | collective-permute-start | bytes 49160 | tf_op jit(solution)/shard_map/ppermute | solution.py:443
  28.6 7.9 %collective-permute-start.12 = (f32[1,637]{1,0:T(1,128)S(1)}, f32[1,637]{1,0:T(1,128)S(1)}, u32[]{:S(2)}, u32[]{:S(2)}) collective-permute-start(f32[1,637]{1,0:T(1,128)S(1)} %get-tuple-element.61), channel_id=1, source_target_pairs={{0,3},{1,2},{2,1},{3,0},{4,7},{5,6},{6,5},{7,4},{8,11},{9,10},{10,... | collective-permute-start | bytes 7652 | tf_op jit(solution)/shard_map/ppermute | solution.py:547
  35.0 2.4 %collective-permute-start.11 = (f32[1,637]{1,0:T(1,128)S(1)}, f32[1,637]{1,0:T(1,128)S(1)}, u32[]{:S(2)}, u32[]{:S(2)}) collective-permute-start(f32[1,637]{1,0:T(1,128)S(1)} %get-tuple-element.61), channel_id=1, source_target_pairs={{0,2},{1,3},{2,0},{3,1},{4,6},{5,7},{6,4},{7,5},{8,10},{9,11},{10,... | collective-permute-start | bytes 7652 | tf_op jit(solution)/shard_map/ppermute | solution.py:547
  35.2 2.2 %collective-permute-start.10 = (f32[1,637]{1,0:T(1,128)S(1)}, f32[1,637]{1,0:T(1,128)S(1)}, u32[]{:S(2)}, u32[]{:S(2)}) collective-permute-start(f32[1,637]{1,0:T(1,128)S(1)} %get-tuple-element.61), channel_id=1, source_target_pairs={{0,1},{1,0},{2,3},{3,2},{4,5},{5,4},{6,7},{7,6},{8,9},{9,8},{10,11... | collective-permute-start | bytes 7652 | tf_op jit(solution)/shard_map/ppermute | solution.py:547

commit v6 on v5

--- a/solution.py
+++ b/solution.py
@@ -50,8 +50,15 @@
         self.pad_face = up16(self.face)
         self.span = up16(self.shift + self.face)
         self.l_face = 2 * self.coef
-        self.l_term = self.l_face + self.span
-        self.later = self.l_term + self.pad_face
+        self.l_term = self.l_face + self.pad_face
+        self.l_block = self.l_term + self.pad_face
+        self.later = self.l_block + self.pad_face
+        self.second = {
+            "near": self.l_term + 2 * ROWS16,
+            "over": self.l_term,
+            "far": self.coef,
+            "farther": self.l_term + ROWS16,
+        }
 
 
 def dot(a, b):
@@ -87,20 +94,14 @@
     z, center_hbm, x0_hbm, proj_hbm, x0, near, over, own0, own1, coeffs, center, proj, xs, sems
 ):
     copies = [
-        pltpu.make_async_copy(x0_hbm, x0, sems.at[0]),
+        pltpu.make_async_copy(proj_hbm, proj, sems.at[0]),
         pltpu.make_async_copy(center_hbm, center, sems.at[1]),
-        pltpu.make_async_copy(proj_hbm, proj, sems.at[2]),
+        pltpu.make_async_copy(x0_hbm, x0, sems.at[2]),
     ]
     for copy in copies:
         copy.start()
     copies[0].wait()
-    xs[...] = x0[...].astype(F32)
-    put(
-        near, over, (slice(z.m_rows, z.first), slice(None)),
-        x0[z.right_lo : z.right_lo + z.halo, :], x0[z.left_lo : z.left_lo + z.halo, :],
-    )
     copies[1].wait()
-    copies[2].wait()
     on0, on1, reach_left, reach_right = [], [], [], []
     for a in range(z.atoms):
         low = center[a] == 0
@@ -144,12 +145,21 @@
         if k == 0:
             to_right = (far_first + to_first(own_last)).astype(BF16)
         put(near, over, (slice(k * z.coef, (k + 1) * z.coef), slice(None)), to_right, to_left)
+    copies[2].wait()
+    xs[...] = x0[...].astype(F32)
+    put(
+        near, over, (slice(z.m_rows, z.first), slice(None)),
+        x0[z.right_lo : z.right_lo + z.halo, :], x0[z.left_lo : z.left_lo + z.halo, :],
+    )
     row = lax.broadcasted_iota(jnp.int32, (z.nodes, 1), 0)
     x_first, x_last = xs[: z.nodes, :], xs[z.last :, :]
-    first = dot(own0[...], x_first.astype(BF16))
-    last = dot(own1[...], x_last.astype(BF16))
-    inner_first = dot(own0[...], jnp.where(row < z.face, 0.0, x_first).astype(BF16))
-    inner_last = dot(own1[...], jnp.where(row >= z.stride, 0.0, x_last).astype(BF16))
+    states = x0.shape[1]
+    x_first = jnp.concatenate([x_first, jnp.where(row < z.face, 0.0, x_first)], axis=1)
+    x_last = jnp.concatenate([x_last, jnp.where(row >= z.stride, 0.0, x_last)], axis=1)
+    on_first = dot(own0[...], x_first.astype(BF16))
+    on_last = dot(own1[...], x_last.astype(BF16))
+    first, inner_first = on_first[:, :states], on_first[:, states:]
+    last, inner_last = on_last[:, :states], on_last[:, states:]
     coeffs[...] = inner_first + inner_last
     put(
         near, over, (slice(z.m_coef, z.m_rows), slice(None)),
@@ -177,16 +187,15 @@
     return jnp.concatenate([a, b, a, b], axis=0).astype(BF16)
 
 
-def send_part(
-    z, rows0, rows1, end0, end1, part, coeffs, near, over, far, farther, first, last
-):
+def send_part(z, rows0, rows1, part, coeffs, near, over, far, farther, faces):
     c = z.coef
-    last[...] = jnp.zeros_like(last)
-    first[...] = jnp.zeros_like(first)
-    last[: z.face, :] = part[z.end :, :]
-    first[z.shift : z.shift + z.face, :] = part[: z.face, :]
-    last_rows, first_rows = last[...].astype(BF16), first[...].astype(BF16)
-    put(near, over, (slice(z.l_face, z.l_term), slice(None)), last_rows, first_rows)
+    faces[...] = jnp.zeros_like(faces)
+    faces[0, : z.face, :] = part[: z.face, :]
+    faces[1, : z.face, :] = part[z.end :, :]
+    put(
+        near, over, (slice(z.l_face, z.l_term), slice(None)),
+        faces[1].astype(BF16), faces[0].astype(BF16),
+    )
     on0, on1 = part[: z.nodes, :].astype(BF16), part[z.last :, :].astype(BF16)
     s0, s1 = dot(rows0[...], on0), dot(rows1[...], on1)
     before, own, after = s0[c:], s0[:c] + s1[:c], s1[c:]
@@ -198,21 +207,16 @@
     over[:c, :] = own
     put(near, over, (slice(c, 2 * c), slice(None)), after, before)
     even = is_even()
-    far[...] = jnp.where(even, before, after)
-    farther[...] = jnp.where(even, after, before)
-    if end0 is None:
-        return
-    put(
-        near, over, (slice(z.l_term, z.later), slice(None)),
-        dot(end1[...], on1).astype(BF16), dot(end0[: z.pad_face, :], on0).astype(BF16),
-    )
+    far[:c, :] = jnp.where(even, before, after)
+    farther[:c, :] = jnp.where(even, after, before)
+    return on0, on1
 
 
 def whole_coeffs(z, own_ref, near, over, far, farther):
     c = z.coef
     left, right = (v.astype(F32) for v in take(near, over, (slice(0, 2 * c), slice(None))))
     even = is_even()
-    a, b = far[...], farther[...]
+    a, b = far[:c, :], farther[:c, :]
     far_left, far_right = jnp.where(even, b, a), jnp.where(even, a, b)
     before = own_ref[:c, :] + left[:c] + far_left.astype(F32)
     own = own_ref[c : 2 * c, :] + left[c:] + right[c:]
@@ -222,18 +226,25 @@
 
 def face_rows(z, near, over):
     first, last = take(near, over, (slice(z.l_face, z.l_term), slice(None)))
-    return (
-        first.astype(F32)[: z.face],
-        last.astype(F32)[z.shift : z.shift + z.face],
-    )
-
-
-def neighbour_terms(z, s, near, over, cell0, cell1, spread0, spread1):
+    return first.astype(F32)[: z.face], last.astype(F32)[: z.face]
+
+
+def at_last(z, rows, pad):
+    pad[...] = jnp.zeros_like(pad)
+    pad[z.shift : z.shift + z.face, :] = rows
+    return pad[...].astype(BF16)
+
+
+def neighbour_terms(z, s, faces, cell0, cell1, spread0, spread1, pad):
     before, own, after = s
-    first, last = take(near, over, (slice(z.l_face, z.l_term), slice(None)))
+    first, last = faces
     k_last = (z.chunks - 1) * LANES
-    term0 = dot(spread0[...], twice(own, before)) + dot(cell0[:, : z.span], first)
-    term1 = dot(spread1[...], twice(own, after)) + dot(cell1[:, k_last:], last[: z.tail])
+    pad[0, : z.face, :] = first
+    pad[0, z.face :, :] = jnp.zeros((z.span - z.face, first.shape[1]), F32)
+    first = pad[0].astype(BF16)[: z.pad_face]
+    last = at_last(z, last, pad.at[1])[: z.tail]
+    term0 = dot(spread0[...], twice(own, before)) + dot(cell0[:, : z.pad_face], first)
+    term1 = dot(spread1[...], twice(own, after)) + dot(cell1[:, k_last:], last)
     return term0, term1
 
 
@@ -270,12 +281,12 @@
 def first_kernel(
     z, gain,
     base, x0, own0, own1, own_coeffs, mine_near, mine_over, from_near, from_over,
-    cell0, mix_high, mix_low, end_rows,
+    mix_high, mix_low,
     part, coeffs, near, over, far, farther,
     rows0, rows1, spread0, spread1, inner0, inner1,
-    xs, ext, terms, first, last,
+    xs, ext, terms, faces,
 ):
-    c, k_last = z.coef, (z.chunks - 1) * LANES
+    c = z.coef
     xs[...] = x0[...].astype(F32)
     rows0[:c, :] = own0[...]
     rows1[:c, :] = own1[...]
@@ -325,15 +336,10 @@
         z, dot(inner0[...], twice(own, before)), dot(inner1[...], twice(own, after)), terms
     )
     part[...] = terms[...] * gain
-    send_part(
-        z, rows0, rows1, None, None,
-        part, coeffs, near, over, far, farther, first, last,
-    )
-    wide = jnp.zeros((z.pad_face, LANES - z.tail), BF16)
-    put(
-        near, over, (slice(z.l_term, z.later), slice(None)),
-        jnp.concatenate([end_rows[:, k_last:], wide], axis=1), cell0[: z.pad_face, :LANES],
-    )
+    send_part(z, rows0, rows1, part, coeffs, near, over, far, farther, faces)
+    for message, used in ((near, z.l_term), (over, z.l_term), (far, c), (farther, c)):
+        if message.shape[0] > used:
+            message[used:, :] = jnp.zeros((message.shape[0] - used, message.shape[1]), BF16)
 
 
 def beside_second(z, gain, back, part, x0, cell0, cell1, base):
@@ -352,23 +358,29 @@
     base, own_coeffs, from_near, from_over, from_far, from_farther,
     cell0, cell1, end_rows, rows0, rows1, inner0, inner1,
     part, coeffs, near, over, far, farther,
-    first_rows, last_rows,
+    edges, pad,
 ):
     s = whole_coeffs(z, own_coeffs, from_near, from_over, from_far, from_farther)
-    term0, term1 = neighbour_terms(z, s, from_near, from_over, cell0, cell1, inner0, inner1)
+    first, last = face_rows(z, from_near, from_over)
+    term0, term1 = neighbour_terms(z, s, (first, last), cell0, cell1, inner0, inner1, pad)
     part[...] = base[...]
     add_cells(z, gain * term0, gain * term1, part)
-    first, last = face_rows(z, from_near, from_over)
     part[: z.face, :] -= (0.5 * CENTRE * gain) * first
     part[z.end :, :] -= (0.5 * CENTRE * gain) * last
-    send_part(
-        z, rows0, rows1, cell0, end_rows,
-        part, coeffs, near, over, far, farther, first_rows, last_rows,
-    )
-
-
-def beside_third(z, gain, back, part, earlier, from_near, from_over, mine_near, mine_over,
-                 cell0, cell1, base):
+    on0, on1 = send_part(z, rows0, rows1, part, coeffs, near, over, far, farther, edges)
+    put(
+        near, over, (slice(z.l_term, z.l_block), slice(None)),
+        dot(end_rows[...], on1).astype(BF16), dot(cell0[: z.pad_face, :], on0).astype(BF16),
+    )
+    k_last = (z.chunks - 1) * LANES
+    wide = jnp.zeros((z.pad_face, LANES - z.tail), BF16)
+    put(
+        near, over, (slice(z.l_block, z.later), slice(None)),
+        jnp.concatenate([end_rows[:, k_last:], wide], axis=1), cell0[: z.pad_face, :LANES],
+    )
+
+
+def beside_third(z, gain, back, part, earlier, from_near, from_over, cell0, cell1, base):
     base[...] = (-CENTRE * gain) * part[...] - back * earlier[...]
     add_cells(
         z,
@@ -377,35 +389,41 @@
         base,
     )
     first, last = face_rows(z, from_near, from_over)
-    blocks = take(from_near, from_over, (slice(z.l_term, z.later), slice(0, z.span)))
-    mine = take(mine_near, mine_over, (slice(z.l_face, z.l_term), slice(None)))
-    base[: z.face, :] += gain * dot(blocks[0], mine[0])[: z.face] - back * first
-    base[z.end :, :] += gain * dot(blocks[1], mine[1])[: z.face] - back * last
+    base[: z.face, :] -= back * first
+    base[z.end :, :] -= back * last
 
 
 def third_kernel(
     z, gain, share,
     base, own_coeffs, from_near, from_over, from_far, from_farther,
-    cell0, cell1, spread0, spread1, occupation,
+    cell0, cell1, spread0, spread1, part, occupation,
     out, density,
+    pad, mine,
 ):
     s = whole_coeffs(z, own_coeffs, from_near, from_over, from_far, from_farther)
-    term0, term1 = neighbour_terms(z, s, from_near, from_over, cell0, cell1, spread0, spread1)
+    first, last = face_rows(z, from_near, from_over)
+    term0, term1 = neighbour_terms(z, s, (first, last), cell0, cell1, spread0, spread1, pad)
     out[...] = base[...]
     add_cells(z, gain * term0, gain * term1, out)
-    first, last = face_rows(z, from_near, from_over)
-    terms = take(from_near, from_over, (slice(z.l_term, z.later), slice(None)))
-    left, right = (v.astype(F32)[: z.face] for v in terms)
+    terms = take(from_near, from_over, (slice(z.l_term, z.l_block), slice(None)))
+    blocks = take(from_near, from_over, (slice(z.l_block, z.later), slice(None)))
+    own_first = at_last(z, part[: z.face, :], mine.at[0])
+    mine[1, : z.face, :] = part[z.end :, :]
+    mine[1, z.face :, :] = jnp.zeros((z.span - z.face, part.shape[1]), F32)
+    own_last = mine[1].astype(BF16)[: z.pad_face]
+    left = (terms[0].astype(F32) + dot(blocks[0][:, : z.span], own_first))[: z.face]
+    right = (terms[1].astype(F32) + dot(blocks[1][:, : z.pad_face], own_last))[: z.face]
     out[: z.face, :] += gain * (left - CENTRE * first)
     out[z.end :, :] += gain * (right - CENTRE * last)
     result = out[...]
-    density[...] = lax.dot_general(
-        occupation[...] * share,
-        result * result,
+    weights = jnp.concatenate(halves(occupation[...] * share), axis=0)
+    rows = lax.dot_general(
+        weights,
+        (result * result).astype(BF16),
         (((1,), (1,)), ((), ())),
         preferred_element_type=F32,
-        precision=lax.Precision.HIGHEST,
-    )
+    )
+    density[...] = rows[:1] + rows[1:]
 
 
 def call(kernel, outs, scratch, *args, hbm=0, megabytes=32, order=()):
@@ -491,18 +509,19 @@
     )
 
     coeffs = ((3 * c, states), F32)
-    messages = [((z.later, states), BF16)] * 2 + [((c, states), BF16)] * 2
-    faces = [pltpu.VMEM((z.span, states), F32)] * 2
+    second_messages = [((n, states), BF16) for n in z.second.values()]
+    third_messages = [((z.later, states), BF16)] * 2 + [((c, states), BF16)] * 2
+    faces, pad = pltpu.VMEM((2, z.pad_face, states), F32), pltpu.VMEM((2, z.span, states), F32)
     part1, own_coeffs, near, over, far, farther, rows0, rows1, spread0, spread1, inner0, inner1 = (
         call(
             functools.partial(first_kernel, z, gains[0]),
             [field, coeffs]
-            + messages
+            + second_messages
             + [((2 * c, n), BF16)] * 2
             + [((n, 4 * c), BF16)] * 4,
-            [scratch, pltpu.VMEM((2, z.chunks * LANES, states), F32), scratch] + faces,
+            [scratch, pltpu.VMEM((2, z.chunks * LANES, states), F32), scratch, faces],
             base, x0, own0, own1, own_share, near, over, from_near, from_over,
-            cell0, mix_high, mix_low, end_rows,
+            mix_high, mix_low,
             order=FIRST_ORDER,
         )
     )
@@ -515,8 +534,8 @@
     )
     part2, own_coeffs, near, over, far, farther = call(
         functools.partial(second_kernel, z, gains[1]),
-        [field, coeffs] + messages,
-        faces,
+        [field, coeffs] + third_messages,
+        [faces, pad],
         base, own_coeffs, *second,
         cell0, cell1, end_rows, rows0, rows1, inner0, inner1,
         order=ORDER,
@@ -526,14 +545,14 @@
         functools.partial(beside_third, z, gains[2], backs[2]),
         [field],
         [],
-        part2, part1, second[0], second[1], near, over, cell0, cell1,
+        part2, part1, second[0], second[1], cell0, cell1,
     )
     filtered, density = call(
         functools.partial(third_kernel, z, gains[2], 1.0 / (states * groups)),
         [field, ((1, rows), F32)],
-        [],
+        [pad, pad],
         base, own_coeffs, *third,
-        cell0, cell1, spread0, spread1, occupation[None, :],
+        cell0, cell1, spread0, spread1, part2, occupation[None, :],
         order=ORDER,
     )
     return filtered, total(density, groups)[0]

time: 38.2 us -> 37 us (0.969)
  the two profiles are of different devices: /device:TPU:5 before, /device:TPU:0 now
where the time goes in v6:
time: 37 us; the launch traced here: 36.6 us
  starting transfers between devices  20.1 us (54%)
  waiting for transfers between devices  8.18 us (22%)
  Pallas kernels  4.68 us (13%)
  matrix products  1.41 us (4%)
  local copies, waits for them, and re-layouts  0.86 us (2%)
  between operations  0.74 us (2%)
  other arithmetic  0.61 us (2%)
    ppermute x10, starting transfers between devices, exchanged(): return lax.ppermute(array, 'cells', pairs)  18.2 us
    ppermute x10, waiting for transfers between devices, exchanged(): return lax.ppermute(array, 'cells', pairs)  7.1 us
    pallas_call x7, Pallas kernels, call(): pl.pallas_call(ordered, out_shape=[pltpu.VMEM(s, t) for s, t in outs], in...  4.68 us
    ppermute x3, starting transfers between devices, partner(): return lax.ppermute(array, 'states', [(i, i ^ by) for i in range(groups)])  1.88 us
    dot_general x1, matrix products, body(): jnp.einsum('ct,tij->cij', onehot, cell_table, preferred_element_type=F32)  1.41 us
    ppermute x3, waiting for transfers between devices, partner(): return lax.ppermute(array, 'states', [(i, i ^ by) for i in range(groups)])  1.09 us
    unnamed x7, local copies, waits for them, and re-layouts  0.74 us
  transfers between devices with their start and end apart: 13, of which 7 were waited for; matrix products, arithmetic and copies ran while one was open for 6% of the time, Pallas kernels for 4%

profile of v6, /device:TPU:0, one launch (start us, length us, event | category | flops | bytes accessed | tf_op | source)
XLA Modules:
  0.0 36.6 jit_solution(7941854051950575471)
XLA Ops:
  0.6 0.0 copy-start
  0.6 1.4 %shard_map.86 = (bf16[637,128]{1,0:T(8,128)(2,1)S(1)}, bf16[560,128]{1,0:T(8,128)(2,1)S(1)}, bf16[560,128]{1,0:T(8,128)(2,1)S(1)}, bf16[64,343]{1,0:T(8,128)(2,1...) custom-call(s32[4]{0:T(128)} %refs_0_.2, bf16[637,128]{1,0:T(8,128)(2,1)} %refs_1_.1, ...), custom_call_target="tpu_custom_call" | custom-call | tf_op jit(solution)/shard_map/pallas_call | solution.py:439
  2.1 3.0 %collective-permute-start = (bf16[560,128]{1,0:T(8,128)(2,1)S(1)}, bf16[560,128]{1,0:T(8,128)(2,1)S(1)}, u32[]{:S(2)}, u32[]{:S(2)}) collective-permute-start(bf16[560,128]{1,0:T(8,128)(2,1)S(1)} %get-tuple-element.32.refs_7_), channel_id=1, source_target_pairs={{0,4},{4,0},{8,12},{12,8},{16,20},{20,16},{24,28},{28,24},{1,5},{5... | collective-permute-start | bytes 430088 | tf_op jit(solution)/shard_map/ppermute | solution.py:461
  5.1 0.0 copy-start.1
  5.1 3.5 %collective-permute-start.1 = (bf16[560,128]{1,0:T(8,128)(2,1)S(1)}, bf16[560,128]{1,0:T(8,128)(2,1)S(1)}, u32[]{:S(2)}, u32[]{:S(2)}) collective-permute-start(bf16[560,128]{1,0:T(8,128)(2,1)S(1)} %get-tuple-element.33.refs_8_), channel_id=1, source_target_pairs={{0,28},{4,8},{8,4},{12,16},{16,12},{20,24},{24,20},{28,0},{1,29},{... | collective-permute-start | bytes 430088 | tf_op jit(solution)/shard_map/ppermute | solution.py:461
  8.7 0.0 copy-done
  8.7 1.4 %fusion = bf16[2,343,343]{2,0,1:T(2,128)(2,1)S(1)} fusion(bf16[8,343,343]{2,0,1:T(8,128)(2,1)S(1)} %copy-done, s32[2]{0:T(128)} %param.9), kind=kOutput, calls=%fused_computation.4 | convolution fusion | flops 3764784 | bytes 2352988 | tf_op jit(solution)/shard_map/ct,tij->cij/dot_general | solution.py:501
  10.1 0.1 copy.11
  10.2 0.1 slice_bitcast_fusion
  10.2 0.0 copy-done.1
  10.2 0.7 %shard_map.87 = (f32[637,128]{1,0:T(8,128)S(1)}, bf16[128,128]{1,0:T(8,128)(2,1)S(1)}, bf16[128,128]{1,0:T(8,128)(2,1)S(1)}, bf16[64,343]{1,0:T(8,128)(2,1)S(1)}) custom-call(f32[16,16]{1,0:T(8,128)S(1)} %copy-done.1, bf16[637,128]{1,0:T(8,128)(2,1)S(1)} %get-tuple-element.34.refs_1_.refs_3_, bf16[343,343]{1,0:T(8,128)(2,1)S(1)} %get-tuple-element.63.refs_2_.refs_6_.refs_4_, ...), custom_call_target="tpu_custom_call" | custom-call | tf_op jit(solution)/shard_map/pallas_call | solution.py:439
  11.0 0.2 collective-permute-done.refs_0_
  11.2 1.8 %collective-permute-done.1.refs_1_ = bf16[560,128]{1,0:T(8,128)(2,1)S(1)} collective-permute-done((bf16[560,128]{1,0:T(8,128)(2,1)S(1)}, bf16[560,128]{1,0:T(8,128)(2,1)S(1)}, u32[]{:S(2)}, u32[]{:S(2)}) %collective-permute-start.1) | collective-permute-done | bytes 143392 | tf_op jit(solution)/shard_map/ppermute | solution.py:461
  13.0 0.9 %shard_map.88 = (f32[637,128]{1,0:T(8,128)S(1)}, f32[192,128]{1,0:T(8,128)S(1)}, bf16[224,128]{1,0:T(8,128)(2,1)S(1)}, bf16[192,128]{1,0:T(8,128)(2,1)S(1)}, bf1...) custom-call(bf16[560,128]{1,0:T(8,128)(2,1)S(1)} %collective-permute, ...), custom_call_target="tpu_custom_call" | custom-call | tf_op jit(solution)/shard_map/pallas_call | solution.py:439
  13.9 0.7 %collective-permute-start.3 = (bf16[224,128]{1,0:T(8,128)(2,1)S(1)}, bf16[224,128]{1,0:T(8,128)(2,1)S(1)}, u32[]{:S(2)}, u32[]{:S(2)}) collective-permute-start(bf16[224,128]{1,0:T(8,128)(2,1)S(1)} %get-tuple-element.42), channel_id=1, source_target_pairs={{0,4},{4,0},{8,12},{12,8},{16,20},{20,16},{24,28},{28,24},{1,5},{5... | collective-permute-start | bytes 172040 | tf_op jit(solution)/shard_map/ppermute | solution.py:461
  14.6 1.6 %collective-permute-start.4 = (bf16[208,128]{1,0:T(8,128)(2,1)S(1)}, bf16[208,128]{1,0:T(8,128)(2,1)S(1)}, u32[]{:S(2)}, u32[]{:S(2)}) collective-permute-start(bf16[208,128]{1,0:T(8,128)(2,1)S(1)} %get-tuple-element.43), channel_id=1, source_target_pairs={{0,8},{4,28},{8,16},{12,4},{16,24},{20,12},{24,0},{28,20},{1,9},{5... | collective-permute-start | bytes 159752 | tf_op jit(solution)/shard_map/ppermute | solution.py:461
  16.2 2.4 %collective-permute-start.2 = (bf16[192,128]{1,0:T(8,128)(2,1)S(1)}, bf16[192,128]{1,0:T(8,128)(2,1)S(1)}, u32[]{:S(2)}, u32[]{:S(2)}) collective-permute-start(bf16[192,128]{1,0:T(8,128)(2,1)S(1)} %get-tuple-element.41), channel_id=1, source_target_pairs={{0,28},{4,8},{8,4},{12,16},{16,12},{20,24},{24,20},{28,0},{1,29},{... | collective-permute-start | bytes 147464 | tf_op jit(solution)/shard_map/ppermute | solution.py:461
  18.6 0.4 %collective-permute-start.5 = (bf16[64,128]{1,0:T(8,128)(2,1)S(1)}, bf16[64,128]{1,0:T(8,128)(2,1)S(1)}, u32[]{:S(2)}, u32[]{:S(2)}) collective-permute-start(bf16[64,128]{1,0:T(8,128)(2,1)S(1)} %get-tuple-element.44), channel_id=1, source_target_pairs={{0,24},{4,12},{8,0},{12,20},{16,8},{20,28},{24,16},{28,4},{1,25},{... | collective-permute-start | bytes 49160 | tf_op jit(solution)/shard_map/ppermute | solution.py:461
  19.1 0.0 copy-start.2
  19.1 0.3 shard_map.89.refs_4_
  19.4 3.1 %collective-permute-done.5.refs_3_ = bf16[64,128]{1,0:T(8,128)(2,1)S(1)} collective-permute-done((bf16[64,128]{1,0:T(8,128)(2,1)S(1)}, bf16[64,128]{1,0:T(8,128)(2,1)S(1)}, u32[]{:S(2)}, u32[]{:S(2)}) %collective-permute-start.5) | collective-permute-done | bytes 16416 | tf_op jit(solution)/shard_map/ppermute | solution.py:461
  22.5 0.5 %collective-permute-done.2.refs_0_.refs_3_ = bf16[192,128]{1,0:T(8,128)(2,1)S(1)} collective-permute-done((bf16[192,128]{1,0:T(8,128)(2,1)S(1)}, bf16[192,128]{1,0:T(8,128)(2,1)S(1)}, u32[]{:S(2)}, u32[]{:S(2)}) %collective-permute-start.2) | collective-permute-done | bytes 49184 | tf_op jit(solution)/shard_map/ppermute | solution.py:461
  23.0 0.0 collective-permute-done.4.refs_2_
  23.0 0.0 collective-permute-done.3.refs_1_.refs_2_
  23.0 0.5 %shard_map.90 = (f32[637,128]{1,0:T(8,128)S(1)}, f32[192,128]{1,0:T(8,128)S(1)}, bf16[320,128]{1,0:T(8,128)(2,1)S(1)}, bf16[320,128]{1,0:T(8,128)(2,1)S(1)}, bf1...) custom-call(bf16[192,128]{1,0:T(8,128)(2,1)S(1)} %collective-permute-done.2.refs_0_.refs_3_, ...), custom_call_target="tpu_custom_call" | custom-call | tf_op jit(solution)/shard_map/pallas_call | solution.py:439
  23.6 2.5 %collective-permute-start.6 = (bf16[320,128]{1,0:T(8,128)(2,1)S(1)}, bf16[320,128]{1,0:T(8,128)(2,1)S(1)}, u32[]{:S(2)}, u32[]{:S(2)}) collective-permute-start(bf16[320,128]{1,0:T(8,128)(2,1)S(1)} %get-tuple-element.52), channel_id=1, source_target_pairs={{0,28},{4,8},{8,4},{12,16},{16,12},{20,24},{24,20},{28,0},{1,29},{... | collective-permute-start | bytes 245768 | tf_op jit(solution)/shard_map/ppermute | solution.py:461
  26.1 0.2 collective-permute-start.7
  26.2 0.7 %collective-permute-start.8 = (bf16[64,128]{1,0:T(8,128)(2,1)S(1)}, bf16[64,128]{1,0:T(8,128)(2,1)S(1)}, u32[]{:S(2)}, u32[]{:S(2)}) collective-permute-start(bf16[64,128]{1,0:T(8,128)(2,1)S(1)} %get-tuple-element.54), channel_id=1, source_target_pairs={{0,8},{4,28},{8,16},{12,4},{16,24},{20,12},{24,0},{28,20},{1,9},{5... | collective-permute-start | bytes 49160 | tf_op jit(solution)/shard_map/ppermute | solution.py:461
  26.9 3.2 %collective-permute-start.9 = (bf16[64,128]{1,0:T(8,128)(2,1)S(1)}, bf16[64,128]{1,0:T(8,128)(2,1)S(1)}, u32[]{:S(2)}, u32[]{:S(2)}) collective-permute-start(bf16[64,128]{1,0:T(8,128)(2,1)S(1)} %get-tuple-element.55), channel_id=1, source_target_pairs={{0,24},{4,12},{8,0},{12,20},{16,8},{20,28},{24,16},{28,4},{1,25},{... | collective-permute-start | bytes 49160 | tf_op jit(solution)/shard_map/ppermute | solution.py:461
  30.1 0.3 shard_map.91.refs_4_
  30.4 1.4 %collective-permute-done.8.refs_2_ = bf16[64,128]{1,0:T(8,128)(2,1)S(1)} collective-permute-done((bf16[64,128]{1,0:T(8,128)(2,1)S(1)}, bf16[64,128]{1,0:T(8,128)(2,1)S(1)}, u32[]{:S(2)}, u32[]{:S(2)}) %collective-permute-start.8) | collective-permute-done | bytes 16416 | tf_op jit(solution)/shard_map/ppermute | solution.py:461
  31.8 0.0 collective-permute-done.9.refs_3_
  31.8 0.0 collective-permute-done.6.refs_0_
  31.8 0.0 collective-permute-done.7.refs_1_
  31.8 0.0 copy-done.2
  31.8 0.5 %shard_map.92 = (f32[637,128]{1,0:T(8,128)S(1)}, f32[1,637]{1,0:T(1,128)S(1)}) custom-call(bf16[320,128]{1,0:T(8,128)(2,1)S(1)} %collective-permute-done.6.refs_0_, bf16[320,128]{1,0:T(8,128)(2,1)S(1)} %collective-permute-done.7.refs_1_, bf16[64,128]{1,0:T(8,128)(2,1)S(1)} %collective-permute-done.8.refs_2_, ...), custom_call_target="tpu_custom_call" | custom-call | tf_op jit(solution)/shard_map/pallas_call | solution.py:439
  32.3 0.0 collective-permute-start.12
  32.3 1.6 %collective-permute-start.11 = (f32[1,637]{1,0:T(1,128)S(1)}, f32[1,637]{1,0:T(1,128)S(1)}, u32[]{:S(2)}, u32[]{:S(2)}) collective-permute-start(f32[1,637]{1,0:T(1,128)S(1)} %get-tuple-element.61), channel_id=1, source_target_pairs={{0,2},{1,3},{2,0},{3,1},{4,6},{5,7},{6,4},{7,5},{8,10},{9,11},{10,... | collective-permute-start | bytes 7652 | tf_op jit(solution)/shard_map/ppermute | solution.py:566
  33.9 0.3 collective-permute-start.10
  34.2 0.7 %copy.12 = f32[637,128]{1,0:T(8,128)} copy(f32[637,128]{1,0:T(8,128)S(1)} %get-tuple-element.64) | data formatting | bytes 652288
  34.9 0.4 %collective-permute-done.12 = f32[1,637]{1,0:T(1,128)S(1)} collective-permute-done((f32[1,637]{1,0:T(1,128)S(1)}, f32[1,637]{1,0:T(1,128)S(1)}, u32[]{:S(2)}, u32[]{:S(2)}) %collective-permute-start.12) | collective-permute-done | bytes 2580 | tf_op jit(solution)/shard_map/ppermute | solution.py:566
  35.3 0.7 %collective-permute-done.11 = f32[1,637]{1,0:T(1,128)S(1)} collective-permute-done((f32[1,637]{1,0:T(1,128)S(1)}, f32[1,637]{1,0:T(1,128)S(1)}, u32[]{:S(2)}, u32[]{:S(2)}) %collective-permute-start.11) | collective-permute-done | bytes 2580 | tf_op jit(solution)/shard_map/ppermute | solution.py:566
  36.0 0.0 collective-permute-done.10
  36.0 0.6 %add_reduce_fusion = f32[637]{0:T(1024)} fusion(f32[1,637]{1,0:T(1,128)S(1)} %collective-permute-done.12, f32[1,637]{1,0:T(1,128)S(1)} %collective-permute-done.11, f32[1,637]{1,0:T(1,128)S(1)} %get-tuple-element.61, f32[1,637]{1,0:T(1,128)S(1)} %collective-permute-done.10), kind=kLoop, calls=%fused_computation.3 | loop fusion | flops 1911 | bytes 12740 | tf_op jit(solution)/shard_map/add | solution.py:569
Async XLA Ops:
  0.6 8.0 %copy-start = (bf16[8,343,343]{2,0,1:T(8,128)(2,1)S(1)}, bf16[8,343,343]{2,0,1:T(8,128)(2,1)}, u32[]{:S(2)}) copy-start(bf16[8,343,343]{2,0,1:T(8,128)(2,1)} %param.8) | copy-start | bytes 5647156
  2.1 9.1 %collective-permute-start = (bf16[560,128]{1,0:T(8,128)(2,1)S(1)}, bf16[560,128]{1,0:T(8,128)(2,1)S(1)}, u32[]{:S(2)}, u32[]{:S(2)}) collective-permute-start(bf16[560,128]{1,0:T(8,128)(2,1)S(1)} %get-tuple-element.32.refs_7_), channel_id=1, source_target_pairs={{0,4},{4,0},{8,12},{12,8},{16,20},{20,16},{24,28},{28,24},{1,5},{5... | collective-permute-start | bytes 430088 | tf_op jit(solution)/shard_map/ppermute | solution.py:461
  5.1 5.1 %copy-start.1 = (f32[16,16]{1,0:T(8,128)S(1)}, f32[16,16]{1,0:T(8,128)}, u32[]{:S(2)}) copy-start(f32[16,16]{1,0:T(8,128)} %refs_0_.3) | copy-start | bytes 3076
  5.1 7.9 %collective-permute-start.1 = (bf16[560,128]{1,0:T(8,128)(2,1)S(1)}, bf16[560,128]{1,0:T(8,128)(2,1)S(1)}, u32[]{:S(2)}, u32[]{:S(2)}) collective-permute-start(bf16[560,128]{1,0:T(8,128)(2,1)S(1)} %get-tuple-element.33.refs_8_), channel_id=1, source_target_pairs={{0,28},{4,8},{8,4},{12,16},{16,12},{20,24},{24,20},{28,0},{1,29},{... | collective-permute-start | bytes 430088 | tf_op jit(solution)/shard_map/ppermute | solution.py:461
  13.9 9.1 %collective-permute-start.3 = (bf16[224,128]{1,0:T(8,128)(2,1)S(1)}, bf16[224,128]{1,0:T(8,128)(2,1)S(1)}, u32[]{:S(2)}, u32[]{:S(2)}) collective-permute-start(bf16[224,128]{1,0:T(8,128)(2,1)S(1)} %get-tuple-element.42), channel_id=1, source_target_pairs={{0,4},{4,0},{8,12},{12,8},{16,20},{20,16},{24,28},{28,24},{1,5},{5... | collective-permute-start | bytes 172040 | tf_op jit(solution)/shard_map/ppermute | solution.py:461
  14.6 8.4 %collective-permute-start.4 = (bf16[208,128]{1,0:T(8,128)(2,1)S(1)}, bf16[208,128]{1,0:T(8,128)(2,1)S(1)}, u32[]{:S(2)}, u32[]{:S(2)}) collective-permute-start(bf16[208,128]{1,0:T(8,128)(2,1)S(1)} %get-tuple-element.43), channel_id=1, source_target_pairs={{0,8},{4,28},{8,16},{12,4},{16,24},{20,12},{24,0},{28,20},{1,9},{5... | collective-permute-start | bytes 159752 | tf_op jit(solution)/shard_map/ppermute | solution.py:461
  16.2 6.8 %collective-permute-start.2 = (bf16[192,128]{1,0:T(8,128)(2,1)S(1)}, bf16[192,128]{1,0:T(8,128)(2,1)S(1)}, u32[]{:S(2)}, u32[]{:S(2)}) collective-permute-start(bf16[192,128]{1,0:T(8,128)(2,1)S(1)} %get-tuple-element.41), channel_id=1, source_target_pairs={{0,28},{4,8},{8,4},{12,16},{16,12},{20,24},{24,20},{28,0},{1,29},{... | collective-permute-start | bytes 147464 | tf_op jit(solution)/shard_map/ppermute | solution.py:461
  18.6 3.8 %collective-permute-start.5 = (bf16[64,128]{1,0:T(8,128)(2,1)S(1)}, bf16[64,128]{1,0:T(8,128)(2,1)S(1)}, u32[]{:S(2)}, u32[]{:S(2)}) collective-permute-start(bf16[64,128]{1,0:T(8,128)(2,1)S(1)} %get-tuple-element.44), channel_id=1, source_target_pairs={{0,24},{4,12},{8,0},{12,20},{16,8},{20,28},{24,16},{28,4},{1,25},{... | collective-permute-start | bytes 49160 | tf_op jit(solution)/shard_map/ppermute | solution.py:461
  19.1 12.7 %copy-start.2 = (f32[128]{0:T(128)S(1)}, f32[128]{0:T(128)}, u32[]{:S(2)}) copy-start(f32[128]{0:T(128)} %param.13) | copy-start | bytes 1540
  23.6 8.2 %collective-permute-start.6 = (bf16[320,128]{1,0:T(8,128)(2,1)S(1)}, bf16[320,128]{1,0:T(8,128)(2,1)S(1)}, u32[]{:S(2)}, u32[]{:S(2)}) collective-permute-start(bf16[320,128]{1,0:T(8,128)(2,1)S(1)} %get-tuple-element.52), channel_id=1, source_target_pairs={{0,28},{4,8},{8,4},{12,16},{16,12},{20,24},{24,20},{28,0},{1,29},{... | collective-permute-start | bytes 245768 | tf_op jit(solution)/shard_map/ppermute | solution.py:461
  26.1 5.7 %collective-permute-start.7 = (bf16[320,128]{1,0:T(8,128)(2,1)S(1)}, bf16[320,128]{1,0:T(8,128)(2,1)S(1)}, u32[]{:S(2)}, u32[]{:S(2)}) collective-permute-start(bf16[320,128]{1,0:T(8,128)(2,1)S(1)} %get-tuple-element.53), channel_id=1, source_target_pairs={{0,4},{4,0},{8,12},{12,8},{16,20},{20,16},{24,28},{28,24},{1,5},{5... | collective-permute-start | bytes 245768 | tf_op jit(solution)/shard_map/ppermute | solution.py:461
  26.2 5.5 %collective-permute-start.8 = (bf16[64,128]{1,0:T(8,128)(2,1)S(1)}, bf16[64,128]{1,0:T(8,128)(2,1)S(1)}, u32[]{:S(2)}, u32[]{:S(2)}) collective-permute-start(bf16[64,128]{1,0:T(8,128)(2,1)S(1)} %get-tuple-element.54), channel_id=1, source_target_pairs={{0,8},{4,28},{8,16},{12,4},{16,24},{20,12},{24,0},{28,20},{1,9},{5... | collective-permute-start | bytes 49160 | tf_op jit(solution)/shard_map/ppermute | solution.py:461
  26.9 4.9 %collective-permute-start.9 = (bf16[64,128]{1,0:T(8,128)(2,1)S(1)}, bf16[64,128]{1,0:T(8,128)(2,1)S(1)}, u32[]{:S(2)}, u32[]{:S(2)}) collective-permute-start(bf16[64,128]{1,0:T(8,128)(2,1)S(1)} %get-tuple-element.55), channel_id=1, source_target_pairs={{0,24},{4,12},{8,0},{12,20},{16,8},{20,28},{24,16},{28,4},{1,25},{... | collective-permute-start | bytes 49160 | tf_op jit(solution)/shard_map/ppermute | solution.py:461
  32.3 3.0 %collective-permute-start.12 = (f32[1,637]{1,0:T(1,128)S(1)}, f32[1,637]{1,0:T(1,128)S(1)}, u32[]{:S(2)}, u32[]{:S(2)}) collective-permute-start(f32[1,637]{1,0:T(1,128)S(1)} %get-tuple-element.61), channel_id=1, source_target_pairs={{0,3},{1,2},{2,1},{3,0},{4,7},{5,6},{6,5},{7,4},{8,11},{9,10},{10,... | collective-permute-start | bytes 7652 | tf_op jit(solution)/shard_map/ppermute | solution.py:566
  32.3 3.7 %collective-permute-start.11 = (f32[1,637]{1,0:T(1,128)S(1)}, f32[1,637]{1,0:T(1,128)S(1)}, u32[]{:S(2)}, u32[]{:S(2)}) collective-permute-start(f32[1,637]{1,0:T(1,128)S(1)} %get-tuple-element.61), channel_id=1, source_target_pairs={{0,2},{1,3},{2,0},{3,1},{4,6},{5,7},{6,4},{7,5},{8,10},{9,11},{10,... | collective-permute-start | bytes 7652 | tf_op jit(solution)/shard_map/ppermute | solution.py:566
  33.9 2.1 %collective-permute-start.10 = (f32[1,637]{1,0:T(1,128)S(1)}, f32[1,637]{1,0:T(1,128)S(1)}, u32[]{:S(2)}, u32[]{:S(2)}) collective-permute-start(f32[1,637]{1,0:T(1,128)S(1)} %get-tuple-element.61), channel_id=1, source_target_pairs={{0,1},{1,0},{2,3},{3,2},{4,5},{5,4},{6,7},{7,6},{8,9},{9,8},{10,11... | collective-permute-start | bytes 7652 | tf_op jit(solution)/shard_map/ppermute | solution.py:566

commit v7 on v6

--- a/solution.py
+++ b/solution.py
@@ -160,7 +160,7 @@
     on_last = dot(own1[...], x_last.astype(BF16))
     first, inner_first = on_first[:, :states], on_first[:, states:]
     last, inner_last = on_last[:, :states], on_last[:, states:]
-    coeffs[...] = inner_first + inner_last
+    coeffs[...] = first + last
     put(
         near, over, (slice(z.m_coef, z.m_rows), slice(None)),
         (first + inner_last).astype(BF16), (inner_first + last).astype(BF16),
@@ -179,7 +179,7 @@
 
 CENTRE = (upper_edge + lower_edge) / 2.0
 
-FIRST_ORDER = (7, 8)
+FIRST_ORDER = (6, 7)
 ORDER = (3, 2, 5, 4)
 
 
@@ -249,7 +249,7 @@
 
 
 def beside_first(
-    z, coupling, x0, cell0, cell1, base, mix_high, mix_low, end_rows, xs
+    z, coupling, x0, cell0, cell1, mine_near, mine_over, base, mix, end_rows, outer, xs
 ):
     xs[...] = x0[...].astype(F32)
     base[...] = (-CENTRE) * (face_scale(z) * xs[...])
@@ -267,24 +267,48 @@
     )
     row = lax.broadcasted_iota(jnp.int32, (size, size), 0)
     col = lax.broadcasted_iota(jnp.int32, (size, size), 1)
-    mix = jnp.where(lax.div(row, z.proj) == lax.div(col, z.proj), wide, 0.0)
-    mix_high[...], mix_low[...] = halves(mix)
+    wide = jnp.where(lax.div(row, z.proj) == lax.div(col, z.proj), wide, 0.0)
+    mix[...] = jnp.concatenate(halves(wide), axis=1)
+    node = lax.broadcasted_iota(jnp.int32, (LANES, z.halo), 0)
+    place = lax.broadcasted_iota(jnp.int32, (LANES, z.halo), 1)
+    left, right = jnp.zeros((z.coef, z.halo), F32), jnp.zeros((z.coef, z.halo), F32)
+    for k in range(z.chunks):
+        rows = (slice(k * z.coef, (k + 1) * z.coef), slice(None))
+        to_left, to_right = take(mine_near, mine_over, rows)
+        at = node + k * LANES
+        low = (place == at + (z.last - z.right_lo)) & (at < z.stride)
+        high = (place == at - z.left_lo) & (at >= z.face) & (at < z.nodes)
+        left += dot(to_left, jnp.where(low, 1.0, 0.0).astype(BF16))
+        right += dot(to_right, jnp.where(high, 1.0, 0.0).astype(BF16))
+    outer[: z.coef, :] = left.astype(BF16)
+    outer[z.coef :, :] = right.astype(BF16)
     end_rows[...] = jnp.zeros_like(end_rows)
     end_rows[: z.face, :] = cell1[...].astype(F32)[z.stride :].astype(BF16)
 
 
-def mixed(a, mix_high, mix_low):
-    high, low = halves(dot(a, mix_high[...]) + dot(a, mix_low[...]))
-    return jnp.concatenate([high, low], axis=1)
+def mixed(a, mix):
+    width = a.shape[1]
+    product = dot(a, mix[...])
+    return jnp.concatenate(halves(product[:, :width] + product[:, width:]), axis=1)
+
+
+def leave_out(z, spread0, spread1):
+    start = down16(z.stride)
+    for ref, rows in ((spread0, slice(0, z.pad_face)), (spread1, slice(start, z.nodes))):
+        part = ref[rows, :].astype(F32)
+        node = lax.broadcasted_iota(jnp.int32, part.shape, 0) + rows.start
+        lane = lax.broadcasted_iota(jnp.int32, part.shape, 1)
+        face = (node < z.face) if rows.start == 0 else (node >= z.stride)
+        shared = face & (lax.rem(lane, 2 * z.coef) >= z.coef)
+        ref[rows, :] = jnp.where(shared, 0.0, part).astype(BF16)
 
 
 def first_kernel(
     z, gain,
-    base, x0, own0, own1, own_coeffs, mine_near, mine_over, from_near, from_over,
-    mix_high, mix_low,
+    base, x0, own0, own1, own_coeffs, outer, from_near, from_over, mix,
     part, coeffs, near, over, far, farther,
-    rows0, rows1, spread0, spread1, inner0, inner1,
-    xs, ext, terms, faces,
+    rows0, rows1,
+    xs, terms, faces, flat0, flat1,
 ):
     c = z.coef
     xs[...] = x0[...].astype(F32)
@@ -296,44 +320,25 @@
         rows0[c:, cols], rows1[c:, cols] = take(
             from_near, from_over, (slice(k * c, (k + 1) * c), slice(0, width))
         )
-    spread0[...] = mixed(rows0[...].T, mix_high, mix_low)
-    spread1[...] = mixed(rows1[...].T, mix_high, mix_low)
-    inner0[...] = spread0[...]
-    inner1[...] = spread1[...]
-    top = inner0[: z.pad_face, :]
-    row = lax.broadcasted_iota(jnp.int32, top.shape, 0)
-    lane = lax.broadcasted_iota(jnp.int32, top.shape, 1)
-    shared = (row < z.face) & (lax.rem(lane, 2 * c) >= c)
-    inner0[: z.pad_face, :] = jnp.where(shared, 0.0, top.astype(F32)).astype(BF16)
-    start = down16(z.stride)
-    top = inner1[start:, :]
-    row = lax.broadcasted_iota(jnp.int32, top.shape, 0)
-    lane = lax.broadcasted_iota(jnp.int32, top.shape, 1)
-    shared = (row >= z.stride - start) & (lax.rem(lane, 2 * c) >= c)
-    inner1[start:, :] = jnp.where(shared, 0.0, top.astype(F32)).astype(BF16)
-    chunks = [
-        take(mine_near, mine_over, (slice(k * c, (k + 1) * c), slice(None)))
-        for k in range(z.chunks)
-    ]
-    ext[:, z.nodes :, :] = jnp.zeros((2, ext.shape[1] - z.nodes, ext.shape[2]), F32)
-    halo = take(from_near, from_over, (slice(z.m_rows, z.first), slice(None)))
-    skip = z.last - z.right_lo
-    ext[0, : z.stride, :] = halo[0].astype(F32)[skip : skip + z.stride]
-    ext[0, z.stride : z.nodes, :] = xs[: z.face, :]
-    skip = z.face - z.left_lo
-    ext[1, : z.face, :] = xs[z.end :, :]
-    ext[1, z.face : z.nodes, :] = halo[1].astype(F32)[skip : skip + z.stride]
-    own = own_coeffs[...]
-    for k in range(z.chunks):
-        cols = slice(k * LANES, (k + 1) * LANES)
-        own += dot(chunks[k][0], ext[0, cols, :].astype(BF16))
-        own += dot(chunks[k][1], ext[1, cols, :].astype(BF16))
+    flat0[...], flat1[...] = rows0[...].T, rows1[...].T
+    leave_out(z, flat0, flat1)
+    left, right = take(from_near, from_over, (slice(z.m_rows, z.first), slice(None)))
+    own = own_coeffs[...] + dot(outer[:c, :], left) + dot(outer[c:, :], right)
     before, after = take(from_near, from_over, (slice(z.m_coef, z.m_rows), slice(None)))
     before = before.astype(F32) + dot(rows0[c:, :], x0[: z.nodes, :])
     after = after.astype(F32) + dot(rows1[c:, :], xs[z.last :, :].astype(BF16))
     terms[...] = base[...]
+    high, low = halves(jnp.concatenate([before, own, after], axis=1))
+    mix_high, mix_low = mix[:c, :c], mix[:c, 2 * c : 3 * c]
+    weighted = dot(mix_high, high) + dot(mix_high, low) + dot(mix_low, high)
+    weighted = weighted.astype(BF16)
+    n = before.shape[1]
+    before, own, after = (weighted[:, i * n : (i + 1) * n] for i in range(3))
     add_cells(
-        z, dot(inner0[...], twice(own, before)), dot(inner1[...], twice(own, after)), terms
+        z,
+        dot(flat0[...], jnp.concatenate([own, before], axis=0)),
+        dot(flat1[...], jnp.concatenate([own, after], axis=0)),
+        terms,
     )
     part[...] = terms[...] * gain
     send_part(z, rows0, rows1, part, coeffs, near, over, far, farther, faces)
@@ -342,7 +347,8 @@
             message[used:, :] = jnp.zeros((message.shape[0] - used, message.shape[1]), BF16)
 
 
-def beside_second(z, gain, back, part, x0, cell0, cell1, base):
+def beside_second(z, gain, back, part, x0, cell0, cell1, rows0, rows1, mix,
+                  base, spread0, spread1, inner0, inner1):
     scale = face_scale(z)
     base[...] = scale * ((-CENTRE * gain) * part[...] - back * x0[...].astype(F32))
     add_cells(
@@ -351,6 +357,10 @@
         gain * dot(cell1[...], part[z.last :, :].astype(BF16)),
         base,
     )
+    spread0[...] = mixed(rows0[...].T, mix)
+    spread1[...] = mixed(rows1[...].T, mix)
+    inner0[...], inner1[...] = spread0[...], spread1[...]
+    leave_out(z, inner0, inner1)
 
 
 def second_kernel(
@@ -501,36 +511,34 @@
     matrices = jnp.einsum("ct,tij->cij", onehot, cell_table, preferred_element_type=F32)
     matrices = matrices.astype(BF16)
     cell0, cell1 = matrices[0], matrices[-1]
-    base, mix_high, mix_low, end_rows = call(
+    base, mix, end_rows, outer = call(
         functools.partial(beside_first, z),
-        [field] + [((2 * c, 2 * c), BF16)] * 2 + [((z.pad_face, n), BF16)],
+        [field, ((2 * c, 4 * c), BF16), ((z.pad_face, n), BF16), ((2 * c, z.halo), BF16)],
         [scratch],
-        coupling, x0, cell0, cell1,
+        coupling, x0, cell0, cell1, near, over,
     )
 
     coeffs = ((3 * c, states), F32)
     second_messages = [((n, states), BF16) for n in z.second.values()]
     third_messages = [((z.later, states), BF16)] * 2 + [((c, states), BF16)] * 2
     faces, pad = pltpu.VMEM((2, z.pad_face, states), F32), pltpu.VMEM((2, z.span, states), F32)
-    part1, own_coeffs, near, over, far, farther, rows0, rows1, spread0, spread1, inner0, inner1 = (
+    part1, own_coeffs, near, over, far, farther, rows0, rows1 = (
         call(
             functools.partial(first_kernel, z, gains[0]),
             [field, coeffs]
             + second_messages
-            + [((2 * c, n), BF16)] * 2
-            + [((n, 4 * c), BF16)] * 4,
-            [scratch, pltpu.VMEM((2, z.chunks * LANES, states), F32), scratch, faces],
-            base, x0, own0, own1, own_share, near, over, from_near, from_over,
-            mix_high, mix_low,
+            + [((2 * c, n), BF16)] * 2,
+            [scratch, scratch, faces] + [pltpu.VMEM((n, 2 * c), BF16)] * 2,
+            base, x0, own0, own1, own_share, outer, from_near, from_over, mix,
             order=FIRST_ORDER,
         )
     )
     second = exchange_all(near, over, far, farther)
-    (base,) = call(
+    base, spread0, spread1, inner0, inner1 = call(
         functools.partial(beside_second, z, gains[1], backs[1]),
-        [field],
+        [field] + [((n, 4 * c), BF16)] * 4,
         [],
-        part1, x0, cell0, cell1,
+        part1, x0, cell0, cell1, rows0, rows1, mix,
     )
     part2, own_coeffs, near, over, far, farther = call(
         functools.partial(second_kernel, z, gains[1]),

time: 37 us -> 36.9 us (level)
  no operation moved by 1% of the time
where the time goes in v7:
time: 36.9 us; the launch traced here: 36.5 us
  starting transfers between devices  20.1 us (54%)
  waiting for transfers between devices  8.12 us (22%)
  Pallas kernels  4.66 us (13%)
  matrix products  1.41 us (4%)
  local copies, waits for them, and re-layouts  0.86 us (2%)
  between operations  0.74 us (2%)
  other arithmetic  0.61 us (2%)
    ppermute x10, starting transfers between devices, exchanged(): return lax.ppermute(array, 'cells', pairs)  18.2 us
    ppermute x10, waiting for transfers between devices, exchanged(): return lax.ppermute(array, 'cells', pairs)  7.03 us
    pallas_call x7, Pallas kernels, call(): pl.pallas_call(ordered, out_shape=[pltpu.VMEM(s, t) for s, t in outs], in...  4.66 us
    ppermute x3, starting transfers between devices, partner(): return lax.ppermute(array, 'states', [(i, i ^ by) for i in range(groups)])  1.88 us
    dot_general x1, matrix products, body(): jnp.einsum('ct,tij->cij', onehot, cell_table, preferred_element_type=F32)  1.41 us
    ppermute x3, waiting for transfers between devices, partner(): return lax.ppermute(array, 'states', [(i, i ^ by) for i in range(groups)])  1.09 us
    unnamed x7, local copies, waits for them, and re-layouts  0.74 us
  transfers between devices with their start and end apart: 13, of which 7 were waited for; matrix products, arithmetic and copies ran while one was open for 6% of the time, Pallas kernels for 4%

profile of v7, /device:TPU:0, one launch (start us, length us, event | category | flops | bytes accessed | tf_op | source)
XLA Modules:
  0.0 36.5 jit_solution(9727633482266859134)
XLA Ops:
  0.6 0.0 copy-start
  0.6 1.4 %shard_map.86 = (bf16[637,128]{1,0:T(8,128)(2,1)S(1)}, bf16[560,128]{1,0:T(8,128)(2,1)S(1)}, bf16[560,128]{1,0:T(8,128)(2,1)S(1)}, bf16[64,343]{1,0:T(8,128)(2,1...) custom-call(s32[4]{0:T(128)} %refs_0_.2, bf16[637,128]{1,0:T(8,128)(2,1)} %refs_1_.1, ...), custom_call_target="tpu_custom_call" | custom-call | tf_op jit(solution)/shard_map/pallas_call | solution.py:449
  2.1 3.0 %collective-permute-start = (bf16[560,128]{1,0:T(8,128)(2,1)S(1)}, bf16[560,128]{1,0:T(8,128)(2,1)S(1)}, u32[]{:S(2)}, u32[]{:S(2)}) collective-permute-start(bf16[560,128]{1,0:T(8,128)(2,1)S(1)} %get-tuple-element.33.refs_4_), channel_id=1, source_target_pairs={{0,4},{4,0},{8,12},{12,8},{16,20},{20,16},{24,28},{28,24},{1,5},{5... | collective-permute-start | bytes 430088 | tf_op jit(solution)/shard_map/ppermute | solution.py:471
  5.1 0.0 copy-start.1
  5.1 3.5 %collective-permute-start.1 = (bf16[560,128]{1,0:T(8,128)(2,1)S(1)}, bf16[560,128]{1,0:T(8,128)(2,1)S(1)}, u32[]{:S(2)}, u32[]{:S(2)}) collective-permute-start(bf16[560,128]{1,0:T(8,128)(2,1)S(1)} %get-tuple-element.34.refs_5_), channel_id=1, source_target_pairs={{0,28},{4,8},{8,4},{12,16},{16,12},{20,24},{24,20},{28,0},{1,29},{... | collective-permute-start | bytes 430088 | tf_op jit(solution)/shard_map/ppermute | solution.py:471
  8.7 0.0 copy-done
  8.7 1.4 %fusion = bf16[2,343,343]{2,0,1:T(2,128)(2,1)S(1)} fusion(bf16[8,343,343]{2,0,1:T(8,128)(2,1)S(1)} %copy-done, s32[2]{0:T(128)} %param.9), kind=kOutput, calls=%fused_computation.4 | convolution fusion | flops 3764784 | bytes 2352988 | tf_op jit(solution)/shard_map/ct,tij->cij/dot_general | solution.py:511
  10.1 0.1 copy.11
  10.2 0.1 slice_bitcast_fusion
  10.2 0.0 copy-done.1
  10.2 0.7 %shard_map.87 = (f32[637,128]{1,0:T(8,128)S(1)}, bf16[128,256]{1,0:T(8,128)(2,1)S(1)}, bf16[64,343]{1,0:T(8,128)(2,1)S(1)}, bf16[128,304]{1,0:T(8,128)(2,1)S(1)}) custom-call(f32[16,16]{1,0:T(8,128)S(1)} %copy-done.1, bf16[637,128]{1,0:T(8,128)(2,1)S(1)} %get-tuple-element.35.refs_1_.refs_3_, bf16[343,343]{1,0:T(8,128)(2,1)S(1)} %get-tuple-element.65.refs_2_.refs_6_.refs_4_, ...), custom_call_target="tpu_custom_call" | custom-call | tf_op jit(solution)/shard_map/pallas_call | solution.py:449
  11.0 0.3 collective-permute-done.refs_0_
  11.2 1.8 %collective-permute-done.1.refs_1_ = bf16[560,128]{1,0:T(8,128)(2,1)S(1)} collective-permute-done((bf16[560,128]{1,0:T(8,128)(2,1)S(1)}, bf16[560,128]{1,0:T(8,128)(2,1)S(1)}, u32[]{:S(2)}, u32[]{:S(2)}) %collective-permute-start.1) | collective-permute-done | bytes 143392 | tf_op jit(solution)/shard_map/ppermute | solution.py:471
  13.0 0.8 %shard_map.88 = (f32[637,128]{1,0:T(8,128)S(1)}, f32[192,128]{1,0:T(8,128)S(1)}, bf16[224,128]{1,0:T(8,128)(2,1)S(1)}, bf16[192,128]{1,0:T(8,128)(2,1)S(1)}, bf1...) custom-call(bf16[560,128]{1,0:T(8,128)(2,1)S(1)} %collective-permute, ...), custom_call_target="tpu_custom_call" | custom-call | tf_op jit(solution)/shard_map/pallas_call | solution.py:449
  13.8 0.7 %collective-permute-start.3 = (bf16[224,128]{1,0:T(8,128)(2,1)S(1)}, bf16[224,128]{1,0:T(8,128)(2,1)S(1)}, u32[]{:S(2)}, u32[]{:S(2)}) collective-permute-start(bf16[224,128]{1,0:T(8,128)(2,1)S(1)} %get-tuple-element.43), channel_id=1, source_target_pairs={{0,4},{4,0},{8,12},{12,8},{16,20},{20,16},{24,28},{28,24},{1,5},{5... | collective-permute-start | bytes 172040 | tf_op jit(solution)/shard_map/ppermute | solution.py:471
  14.6 1.6 %collective-permute-start.4 = (bf16[208,128]{1,0:T(8,128)(2,1)S(1)}, bf16[208,128]{1,0:T(8,128)(2,1)S(1)}, u32[]{:S(2)}, u32[]{:S(2)}) collective-permute-start(bf16[208,128]{1,0:T(8,128)(2,1)S(1)} %get-tuple-element.44), channel_id=1, source_target_pairs={{0,8},{4,28},{8,16},{12,4},{16,24},{20,12},{24,0},{28,20},{1,9},{5... | collective-permute-start | bytes 159752 | tf_op jit(solution)/shard_map/ppermute | solution.py:471
  16.1 2.4 %collective-permute-start.2 = (bf16[192,128]{1,0:T(8,128)(2,1)S(1)}, bf16[192,128]{1,0:T(8,128)(2,1)S(1)}, u32[]{:S(2)}, u32[]{:S(2)}) collective-permute-start(bf16[192,128]{1,0:T(8,128)(2,1)S(1)} %get-tuple-element.42), channel_id=1, source_target_pairs={{0,28},{4,8},{8,4},{12,16},{16,12},{20,24},{24,20},{28,0},{1,29},{... | collective-permute-start | bytes 147464 | tf_op jit(solution)/shard_map/ppermute | solution.py:471
  18.5 0.5 %collective-permute-start.5 = (bf16[64,128]{1,0:T(8,128)(2,1)S(1)}, bf16[64,128]{1,0:T(8,128)(2,1)S(1)}, u32[]{:S(2)}, u32[]{:S(2)}) collective-permute-start(bf16[64,128]{1,0:T(8,128)(2,1)S(1)} %get-tuple-element.45), channel_id=1, source_target_pairs={{0,24},{4,12},{8,0},{12,20},{16,8},{20,28},{24,16},{28,4},{1,25},{... | collective-permute-start | bytes 49160 | tf_op jit(solution)/shard_map/ppermute | solution.py:471
  19.0 0.0 copy-start.2
  19.0 0.4 %shard_map.89 = (f32[637,128]{1,0:T(8,128)S(1)}, bf16[343,256]{1,0:T(8,128)(2,1)S(1)}, bf16[343,256]{1,0:T(8,128)(2,1)S(1)}, bf16[343,256]{1,0:T(8,128)(2,1)S(1)}, bf16[343,256]{1,0:T(8,128)(2,1)S(1)}) custom-call(f32[637,128]{1,0:T(8,128)S(1)} %get-tuple-element.46.refs_0_.refs_1_, bf16[637,128]{1,0:T(8,128)(2,1)S(1)} %get-tuple-element.35.refs_1_.refs_3_, ...), custom_call_target="tpu_custom_call" | custom-call | tf_op jit(solution)/shard_map/pallas_call | solution.py:449
  19.4 3.0 %collective-permute-done.5.refs_3_ = bf16[64,128]{1,0:T(8,128)(2,1)S(1)} collective-permute-done((bf16[64,128]{1,0:T(8,128)(2,1)S(1)}, bf16[64,128]{1,0:T(8,128)(2,1)S(1)}, u32[]{:S(2)}, u32[]{:S(2)}) %collective-permute-start.5) | collective-permute-done | bytes 16416 | tf_op jit(solution)/shard_map/ppermute | solution.py:471
  22.4 0.6 %collective-permute-done.2.refs_0_.refs_3_ = bf16[192,128]{1,0:T(8,128)(2,1)S(1)} collective-permute-done((bf16[192,128]{1,0:T(8,128)(2,1)S(1)}, bf16[192,128]{1,0:T(8,128)(2,1)S(1)}, u32[]{:S(2)}, u32[]{:S(2)}) %collective-permute-start.2) | collective-permute-done | bytes 49184 | tf_op jit(solution)/shard_map/ppermute | solution.py:471
  22.9 0.0 collective-permute-done.4.refs_2_
  22.9 0.0 collective-permute-done.3.refs_1_.refs_2_
  22.9 0.5 %shard_map.90 = (f32[637,128]{1,0:T(8,128)S(1)}, f32[192,128]{1,0:T(8,128)S(1)}, bf16[320,128]{1,0:T(8,128)(2,1)S(1)}, bf16[320,128]{1,0:T(8,128)(2,1)S(1)}, bf1...) custom-call(bf16[192,128]{1,0:T(8,128)(2,1)S(1)} %collective-permute-done.2.refs_0_.refs_3_, ...), custom_call_target="tpu_custom_call" | custom-call | tf_op jit(solution)/shard_map/pallas_call | solution.py:449
  23.5 2.5 %collective-permute-start.6 = (bf16[320,128]{1,0:T(8,128)(2,1)S(1)}, bf16[320,128]{1,0:T(8,128)(2,1)S(1)}, u32[]{:S(2)}, u32[]{:S(2)}) collective-permute-start(bf16[320,128]{1,0:T(8,128)(2,1)S(1)} %get-tuple-element.54), channel_id=1, source_target_pairs={{0,28},{4,8},{8,4},{12,16},{16,12},{20,24},{24,20},{28,0},{1,29},{... | collective-permute-start | bytes 245768 | tf_op jit(solution)/shard_map/ppermute | solution.py:471
  26.0 0.2 collective-permute-start.7
  26.1 0.7 %collective-permute-start.8 = (bf16[64,128]{1,0:T(8,128)(2,1)S(1)}, bf16[64,128]{1,0:T(8,128)(2,1)S(1)}, u32[]{:S(2)}, u32[]{:S(2)}) collective-permute-start(bf16[64,128]{1,0:T(8,128)(2,1)S(1)} %get-tuple-element.56), channel_id=1, source_target_pairs={{0,8},{4,28},{8,16},{12,4},{16,24},{20,12},{24,0},{28,20},{1,9},{5... | collective-permute-start | bytes 49160 | tf_op jit(solution)/shard_map/ppermute | solution.py:471
  26.8 3.1 %collective-permute-start.9 = (bf16[64,128]{1,0:T(8,128)(2,1)S(1)}, bf16[64,128]{1,0:T(8,128)(2,1)S(1)}, u32[]{:S(2)}, u32[]{:S(2)}) collective-permute-start(bf16[64,128]{1,0:T(8,128)(2,1)S(1)} %get-tuple-element.57), channel_id=1, source_target_pairs={{0,24},{4,12},{8,0},{12,20},{16,8},{20,28},{24,16},{28,4},{1,25},{... | collective-permute-start | bytes 49160 | tf_op jit(solution)/shard_map/ppermute | solution.py:471
  30.0 0.3 shard_map.91.refs_4_
  30.3 1.4 %collective-permute-done.8.refs_2_ = bf16[64,128]{1,0:T(8,128)(2,1)S(1)} collective-permute-done((bf16[64,128]{1,0:T(8,128)(2,1)S(1)}, bf16[64,128]{1,0:T(8,128)(2,1)S(1)}, u32[]{:S(2)}, u32[]{:S(2)}) %collective-permute-start.8) | collective-permute-done | bytes 16416 | tf_op jit(solution)/shard_map/ppermute | solution.py:471
  31.7 0.0 collective-permute-done.9.refs_3_
  31.7 0.0 collective-permute-done.6.refs_0_
  31.7 0.0 collective-permute-done.7.refs_1_
  31.7 0.0 copy-done.2
  31.7 0.5 %shard_map.92 = (f32[637,128]{1,0:T(8,128)S(1)}, f32[1,637]{1,0:T(1,128)S(1)}) custom-call(bf16[320,128]{1,0:T(8,128)(2,1)S(1)} %collective-permute-done.6.refs_0_, bf16[320,128]{1,0:T(8,128)(2,1)S(1)} %collective-permute-done.7.refs_1_, bf16[64,128]{1,0:T(8,128)(2,1)S(1)} %collective-permute-done.8.refs_2_, ...), custom_call_target="tpu_custom_call" | custom-call | tf_op jit(solution)/shard_map/pallas_call | solution.py:449
  32.2 0.0 collective-permute-start.12
  32.2 1.6 %collective-permute-start.11 = (f32[1,637]{1,0:T(1,128)S(1)}, f32[1,637]{1,0:T(1,128)S(1)}, u32[]{:S(2)}, u32[]{:S(2)}) collective-permute-start(f32[1,637]{1,0:T(1,128)S(1)} %get-tuple-element.63), channel_id=1, source_target_pairs={{0,2},{1,3},{2,0},{3,1},{4,6},{5,7},{6,4},{7,5},{8,10},{9,11},{10,... | collective-permute-start | bytes 7652 | tf_op jit(solution)/shard_map/ppermute | solution.py:574
  33.8 0.3 collective-permute-start.10
  34.1 0.7 %copy.12 = f32[637,128]{1,0:T(8,128)} copy(f32[637,128]{1,0:T(8,128)S(1)} %get-tuple-element.66) | data formatting | bytes 652288
  34.8 0.4 %collective-permute-done.12 = f32[1,637]{1,0:T(1,128)S(1)} collective-permute-done((f32[1,637]{1,0:T(1,128)S(1)}, f32[1,637]{1,0:T(1,128)S(1)}, u32[]{:S(2)}, u32[]{:S(2)}) %collective-permute-start.12) | collective-permute-done | bytes 2580 | tf_op jit(solution)/shard_map/ppermute | solution.py:574
  35.2 0.7 %collective-permute-done.11 = f32[1,637]{1,0:T(1,128)S(1)} collective-permute-done((f32[1,637]{1,0:T(1,128)S(1)}, f32[1,637]{1,0:T(1,128)S(1)}, u32[]{:S(2)}, u32[]{:S(2)}) %collective-permute-start.11) | collective-permute-done | bytes 2580 | tf_op jit(solution)/shard_map/ppermute | solution.py:574
  35.9 0.0 collective-permute-done.10
  35.9 0.6 %add_reduce_fusion = f32[637]{0:T(1024)} fusion(f32[1,637]{1,0:T(1,128)S(1)} %collective-permute-done.12, f32[1,637]{1,0:T(1,128)S(1)} %collective-permute-done.11, f32[1,637]{1,0:T(1,128)S(1)} %get-tuple-element.63, f32[1,637]{1,0:T(1,128)S(1)} %collective-permute-done.10), kind=kLoop, calls=%fused_computation.3 | loop fusion | flops 1911 | bytes 12740 | tf_op jit(solution)/shard_map/add | solution.py:577
Async XLA Ops:
  0.6 8.0 %copy-start = (bf16[8,343,343]{2,0,1:T(8,128)(2,1)S(1)}, bf16[8,343,343]{2,0,1:T(8,128)(2,1)}, u32[]{:S(2)}) copy-start(bf16[8,343,343]{2,0,1:T(8,128)(2,1)} %param.8) | copy-start | bytes 5647156
  2.1 9.1 %collective-permute-start = (bf16[560,128]{1,0:T(8,128)(2,1)S(1)}, bf16[560,128]{1,0:T(8,128)(2,1)S(1)}, u32[]{:S(2)}, u32[]{:S(2)}) collective-permute-start(bf16[560,128]{1,0:T(8,128)(2,1)S(1)} %get-tuple-element.33.refs_4_), channel_id=1, source_target_pairs={{0,4},{4,0},{8,12},{12,8},{16,20},{20,16},{24,28},{28,24},{1,5},{5... | collective-permute-start | bytes 430088 | tf_op jit(solution)/shard_map/ppermute | solution.py:471
  5.1 5.1 %copy-start.1 = (f32[16,16]{1,0:T(8,128)S(1)}, f32[16,16]{1,0:T(8,128)}, u32[]{:S(2)}) copy-start(f32[16,16]{1,0:T(8,128)} %refs_0_.3) | copy-start | bytes 3076
  5.1 7.9 %collective-permute-start.1 = (bf16[560,128]{1,0:T(8,128)(2,1)S(1)}, bf16[560,128]{1,0:T(8,128)(2,1)S(1)}, u32[]{:S(2)}, u32[]{:S(2)}) collective-permute-start(bf16[560,128]{1,0:T(8,128)(2,1)S(1)} %get-tuple-element.34.refs_5_), channel_id=1, source_target_pairs={{0,28},{4,8},{8,4},{12,16},{16,12},{20,24},{24,20},{28,0},{1,29},{... | collective-permute-start | bytes 430088 | tf_op jit(solution)/shard_map/ppermute | solution.py:471
  13.8 9.1 %collective-permute-start.3 = (bf16[224,128]{1,0:T(8,128)(2,1)S(1)}, bf16[224,128]{1,0:T(8,128)(2,1)S(1)}, u32[]{:S(2)}, u32[]{:S(2)}) collective-permute-start(bf16[224,128]{1,0:T(8,128)(2,1)S(1)} %get-tuple-element.43), channel_id=1, source_target_pairs={{0,4},{4,0},{8,12},{12,8},{16,20},{20,16},{24,28},{28,24},{1,5},{5... | collective-permute-start | bytes 172040 | tf_op jit(solution)/shard_map/ppermute | solution.py:471
  14.6 8.4 %collective-permute-start.4 = (bf16[208,128]{1,0:T(8,128)(2,1)S(1)}, bf16[208,128]{1,0:T(8,128)(2,1)S(1)}, u32[]{:S(2)}, u32[]{:S(2)}) collective-permute-start(bf16[208,128]{1,0:T(8,128)(2,1)S(1)} %get-tuple-element.44), channel_id=1, source_target_pairs={{0,8},{4,28},{8,16},{12,4},{16,24},{20,12},{24,0},{28,20},{1,9},{5... | collective-permute-start | bytes 159752 | tf_op jit(solution)/shard_map/ppermute | solution.py:471
  16.1 6.8 %collective-permute-start.2 = (bf16[192,128]{1,0:T(8,128)(2,1)S(1)}, bf16[192,128]{1,0:T(8,128)(2,1)S(1)}, u32[]{:S(2)}, u32[]{:S(2)}) collective-permute-start(bf16[192,128]{1,0:T(8,128)(2,1)S(1)} %get-tuple-element.42), channel_id=1, source_target_pairs={{0,28},{4,8},{8,4},{12,16},{16,12},{20,24},{24,20},{28,0},{1,29},{... | collective-permute-start | bytes 147464 | tf_op jit(solution)/shard_map/ppermute | solution.py:471
  18.5 3.8 %collective-permute-start.5 = (bf16[64,128]{1,0:T(8,128)(2,1)S(1)}, bf16[64,128]{1,0:T(8,128)(2,1)S(1)}, u32[]{:S(2)}, u32[]{:S(2)}) collective-permute-start(bf16[64,128]{1,0:T(8,128)(2,1)S(1)} %get-tuple-element.45), channel_id=1, source_target_pairs={{0,24},{4,12},{8,0},{12,20},{16,8},{20,28},{24,16},{28,4},{1,25},{... | collective-permute-start | bytes 49160 | tf_op jit(solution)/shard_map/ppermute | solution.py:471
  19.0 12.7 %copy-start.2 = (f32[128]{0:T(128)S(1)}, f32[128]{0:T(128)}, u32[]{:S(2)}) copy-start(f32[128]{0:T(128)} %param.13) | copy-start | bytes 1540
  23.5 8.2 %collective-permute-start.6 = (bf16[320,128]{1,0:T(8,128)(2,1)S(1)}, bf16[320,128]{1,0:T(8,128)(2,1)S(1)}, u32[]{:S(2)}, u32[]{:S(2)}) collective-permute-start(bf16[320,128]{1,0:T(8,128)(2,1)S(1)} %get-tuple-element.54), channel_id=1, source_target_pairs={{0,28},{4,8},{8,4},{12,16},{16,12},{20,24},{24,20},{28,0},{1,29},{... | collective-permute-start | bytes 245768 | tf_op jit(solution)/shard_map/ppermute | solution.py:471
  26.0 5.7 %collective-permute-start.7 = (bf16[320,128]{1,0:T(8,128)(2,1)S(1)}, bf16[320,128]{1,0:T(8,128)(2,1)S(1)}, u32[]{:S(2)}, u32[]{:S(2)}) collective-permute-start(bf16[320,128]{1,0:T(8,128)(2,1)S(1)} %get-tuple-element.55), channel_id=1, source_target_pairs={{0,4},{4,0},{8,12},{12,8},{16,20},{20,16},{24,28},{28,24},{1,5},{5... | collective-permute-start | bytes 245768 | tf_op jit(solution)/shard_map/ppermute | solution.py:471
  26.1 5.5 %collective-permute-start.8 = (bf16[64,128]{1,0:T(8,128)(2,1)S(1)}, bf16[64,128]{1,0:T(8,128)(2,1)S(1)}, u32[]{:S(2)}, u32[]{:S(2)}) collective-permute-start(bf16[64,128]{1,0:T(8,128)(2,1)S(1)} %get-tuple-element.56), channel_id=1, source_target_pairs={{0,8},{4,28},{8,16},{12,4},{16,24},{20,12},{24,0},{28,20},{1,9},{5... | collective-permute-start | bytes 49160 | tf_op jit(solution)/shard_map/ppermute | solution.py:471
  26.8 4.9 %collective-permute-start.9 = (bf16[64,128]{1,0:T(8,128)(2,1)S(1)}, bf16[64,128]{1,0:T(8,128)(2,1)S(1)}, u32[]{:S(2)}, u32[]{:S(2)}) collective-permute-start(bf16[64,128]{1,0:T(8,128)(2,1)S(1)} %get-tuple-element.57), channel_id=1, source_target_pairs={{0,24},{4,12},{8,0},{12,20},{16,8},{20,28},{24,16},{28,4},{1,25},{... | collective-permute-start | bytes 49160 | tf_op jit(solution)/shard_map/ppermute | solution.py:471
  32.2 3.0 %collective-permute-start.12 = (f32[1,637]{1,0:T(1,128)S(1)}, f32[1,637]{1,0:T(1,128)S(1)}, u32[]{:S(2)}, u32[]{:S(2)}) collective-permute-start(f32[1,637]{1,0:T(1,128)S(1)} %get-tuple-element.63), channel_id=1, source_target_pairs={{0,3},{1,2},{2,1},{3,0},{4,7},{5,6},{6,5},{7,4},{8,11},{9,10},{10,... | collective-permute-start | bytes 7652 | tf_op jit(solution)/shard_map/ppermute | solution.py:574
  32.2 3.7 %collective-permute-start.11 = (f32[1,637]{1,0:T(1,128)S(1)}, f32[1,637]{1,0:T(1,128)S(1)}, u32[]{:S(2)}, u32[]{:S(2)}) collective-permute-start(f32[1,637]{1,0:T(1,128)S(1)} %get-tuple-element.63), channel_id=1, source_target_pairs={{0,2},{1,3},{2,0},{3,1},{4,6},{5,7},{6,4},{7,5},{8,10},{9,11},{10,... | collective-permute-start | bytes 7652 | tf_op jit(solution)/shard_map/ppermute | solution.py:574
  33.8 2.1 %collective-permute-start.10 = (f32[1,637]{1,0:T(1,128)S(1)}, f32[1,637]{1,0:T(1,128)S(1)}, u32[]{:S(2)}, u32[]{:S(2)}) collective-permute-start(f32[1,637]{1,0:T(1,128)S(1)} %get-tuple-element.63), channel_id=1, source_target_pairs={{0,1},{1,0},{2,3},{3,2},{4,5},{5,4},{6,7},{7,6},{8,9},{9,8},{10,11... | collective-permute-start | bytes 7652 | tf_op jit(solution)/shard_map/ppermute | solution.py:574

commit v8 on v7

--- a/solution.py
+++ b/solution.py
@@ -91,7 +91,7 @@
 
 
 def pack_kernel(
-    z, center_hbm, x0_hbm, proj_hbm, x0, near, over, own0, own1, coeffs, center, proj, xs, sems
+    z, center_hbm, x0_hbm, proj_hbm, x0, near, over, own0, own1, center, proj, xs, sems
 ):
     copies = [
         pltpu.make_async_copy(proj_hbm, proj, sems.at[0]),
@@ -102,7 +102,7 @@
         copy.start()
     copies[0].wait()
     copies[1].wait()
-    on0, on1, reach_left, reach_right = [], [], [], []
+    on0, on1, reach_left, reach_right, is_low = [], [], [], [], []
     for a in range(z.atoms):
         low = center[a] == 0
         before, here, after = proj[a, 0], proj[a, 1], proj[a, 2]
@@ -111,8 +111,9 @@
         on1.append(jnp.where(low, after, here))
         reach_left.append(jnp.where(low, before, none))
         reach_right.append(jnp.where(low, none, after))
-    on0, on1, reach_left, reach_right = (
-        jnp.concatenate(v, axis=0) for v in (on0, on1, reach_left, reach_right)
+        is_low.append(jnp.full((z.proj, LANES), jnp.where(low, 1.0, 0.0), F32))
+    on0, on1, reach_left, reach_right, is_low = (
+        jnp.concatenate(v, axis=0) for v in (on0, on1, reach_left, reach_right, is_low)
     )
     k_last = (z.chunks - 1) * LANES
 
@@ -145,26 +146,20 @@
         if k == 0:
             to_right = (far_first + to_first(own_last)).astype(BF16)
         put(near, over, (slice(k * z.coef, (k + 1) * z.coef), slice(None)), to_right, to_left)
+    left_out = jnp.where(on_first & (is_low > 0.5), 0.0, own_first).astype(BF16)
+    sent0 = jnp.concatenate([left_out, on0[:, LANES:]], axis=1)
+    left_out = jnp.where(on_last & (is_low < 0.5), 0.0, own_last).astype(BF16)
+    sent1 = jnp.concatenate([on1[:, :k_last], left_out[:, : z.tail]], axis=1)
     copies[2].wait()
-    xs[...] = x0[...].astype(F32)
     put(
         near, over, (slice(z.m_rows, z.first), slice(None)),
         x0[z.right_lo : z.right_lo + z.halo, :], x0[z.left_lo : z.left_lo + z.halo, :],
     )
-    row = lax.broadcasted_iota(jnp.int32, (z.nodes, 1), 0)
-    x_first, x_last = xs[: z.nodes, :], xs[z.last :, :]
-    states = x0.shape[1]
-    x_first = jnp.concatenate([x_first, jnp.where(row < z.face, 0.0, x_first)], axis=1)
-    x_last = jnp.concatenate([x_last, jnp.where(row >= z.stride, 0.0, x_last)], axis=1)
-    on_first = dot(own0[...], x_first.astype(BF16))
-    on_last = dot(own1[...], x_last.astype(BF16))
-    first, inner_first = on_first[:, :states], on_first[:, states:]
-    last, inner_last = on_last[:, :states], on_last[:, states:]
-    coeffs[...] = first + last
-    put(
-        near, over, (slice(z.m_coef, z.m_rows), slice(None)),
-        (first + inner_last).astype(BF16), (inner_first + last).astype(BF16),
-    )
+    xs[z.right_lo :, :] = x0[z.right_lo :, :].astype(F32)
+    sent = dot(sent0, x0[: z.nodes, :]) + dot(sent1, xs[z.last :, :].astype(BF16))
+    sent = sent.astype(BF16)
+    near[z.m_coef : z.m_rows, :] = sent
+    over[z.m_coef : z.m_rows, :] = sent
 
 
 def add_cells(z, term0, term1, out):
@@ -249,9 +244,11 @@
 
 
 def beside_first(
-    z, coupling, x0, cell0, cell1, mine_near, mine_over, base, mix, end_rows, outer, xs
+    z, coupling, x0, cell0, cell1, mine_near, mine_over, own0, own1,
+    base, mix, end_rows, outer, coeffs, xs,
 ):
     xs[...] = x0[...].astype(F32)
+    coeffs[...] = dot(own0[...], x0[: z.nodes, :]) + dot(own1[...], xs[z.last :, :].astype(BF16))
     base[...] = (-CENTRE) * (face_scale(z) * xs[...])
     add_cells(
         z, dot(cell0[...], x0[: z.nodes, :]), dot(cell1[...], xs[z.last :, :].astype(BF16)), base
@@ -489,12 +486,11 @@
 
     field, share = ((rows, states), F32), ((c, states), F32)
     scratch = pltpu.VMEM(*field)
-    x0, near, over, own0, own1, own_share = call(
+    x0, near, over, own0, own1 = call(
         functools.partial(pack_kernel, z),
         [((rows, states), BF16)]
         + [((z.first, states), BF16)] * 2
-        + [((c, n), BF16)] * 2
-        + [share],
+        + [((c, n), BF16)] * 2,
         [
             pltpu.SMEM(atom_center.shape, jnp.int32),
             pltpu.VMEM(proj_values.shape, BF16),
@@ -511,11 +507,11 @@
     matrices = jnp.einsum("ct,tij->cij", onehot, cell_table, preferred_element_type=F32)
     matrices = matrices.astype(BF16)
     cell0, cell1 = matrices[0], matrices[-1]
-    base, mix, end_rows, outer = call(
+    base, mix, end_rows, outer, own_share = call(
         functools.partial(beside_first, z),
-        [field, ((2 * c, 4 * c), BF16), ((z.pad_face, n), BF16), ((2 * c, z.halo), BF16)],
+        [field, ((2 * c, 4 * c), BF16), ((z.pad_face, n), BF16), ((2 * c, z.halo), BF16), share],
         [scratch],
-        coupling, x0, cell0, cell1, near, over,
+        coupling, x0, cell0, cell1, near, over, own0, own1,
     )
 
     coeffs = ((3 * c, states), F32)

time: 36.9 us -> 36.9 us (level)
  no operation moved by 1% of the time
where the time goes in v8:
time: 36.9 us; the launch traced here: 36.5 us
  starting transfers between devices  20.1 us (54%)
  waiting for transfers between devices  8.06 us (22%)
  Pallas kernels  4.69 us (13%)
  matrix products  1.41 us (4%)
  local copies, waits for them, and re-layouts  0.86 us (2%)
  between operations  0.74 us (2%)
  other arithmetic  0.61 us (2%)
    ppermute x10, starting transfers between devices, exchanged(): return lax.ppermute(array, 'cells', pairs)  18.2 us
    ppermute x10, waiting for transfers between devices, exchanged(): return lax.ppermute(array, 'cells', pairs)  6.98 us
    pallas_call x7, Pallas kernels, call(): pl.pallas_call(ordered, out_shape=[pltpu.VMEM(s, t) for s, t in outs], in...  4.69 us
    ppermute x3, starting transfers between devices, partner(): return lax.ppermute(array, 'states', [(i, i ^ by) for i in range(groups)])  1.88 us
    dot_general x1, matrix products, body(): jnp.einsum('ct,tij->cij', onehot, cell_table, preferred_element_type=F32)  1.41 us
    ppermute x3, waiting for transfers between devices, partner(): return lax.ppermute(array, 'states', [(i, i ^ by) for i in range(groups)])  1.09 us
    unnamed x7, local copies, waits for them, and re-layouts  0.74 us
  transfers between devices with their start and end apart: 13, of which 7 were waited for; matrix products, arithmetic and copies ran while one was open for 6% of the time, Pallas kernels for 4%

profile of v8, /device:TPU:0, one launch (start us, length us, event | category | flops | bytes accessed | tf_op | source)
XLA Modules:
  0.0 36.5 jit_solution(2372440599954401439)
XLA Ops:
  0.6 0.0 copy-start
  0.6 1.4 %shard_map.86 = (bf16[637,128]{1,0:T(8,128)(2,1)S(1)}, bf16[560,128]{1,0:T(8,128)(2,1)S(1)}, bf16[560,128]{1,0:T(8,128)(2,1)S(1)}, bf16[64,343]{1,0:T(8,128)(2,1)S(1)}, bf16[64,343]{1,0:T(8,128)(2,1)S(1)}) custom-call(s32[4]{0:T(128)} %refs_0_.2, bf16[637,128]{1,0:T(8,128)(2,1)} %refs_1_.1, bf16[4,3,16,343]{3,2,1,0:T(8,128)(2,1)} %refs_2_.1), custom_call_target="tpu_custom_call" | custom-call | tf_op jit(solution)/shard_map/pallas_call | solution.py:446
  2.1 3.0 %collective-permute-start = (bf16[560,128]{1,0:T(8,128)(2,1)S(1)}, bf16[560,128]{1,0:T(8,128)(2,1)S(1)}, u32[]{:S(2)}, u32[]{:S(2)}) collective-permute-start(bf16[560,128]{1,0:T(8,128)(2,1)S(1)} %get-tuple-element.33.refs_4_), channel_id=1, source_target_pairs={{0,4},{4,0},{8,12},{12,8},{16,20},{20,16},{24,28},{28,24},{1,5},{5... | collective-permute-start | bytes 430088 | tf_op jit(solution)/shard_map/ppermute | solution.py:468
  5.1 0.0 copy-start.1
  5.1 3.5 %collective-permute-start.1 = (bf16[560,128]{1,0:T(8,128)(2,1)S(1)}, bf16[560,128]{1,0:T(8,128)(2,1)S(1)}, u32[]{:S(2)}, u32[]{:S(2)}) collective-permute-start(bf16[560,128]{1,0:T(8,128)(2,1)S(1)} %get-tuple-element.34.refs_5_), channel_id=1, source_target_pairs={{0,28},{4,8},{8,4},{12,16},{16,12},{20,24},{24,20},{28,0},{1,29},{... | collective-permute-start | bytes 430088 | tf_op jit(solution)/shard_map/ppermute | solution.py:468
  8.6 0.0 copy-done
  8.7 1.4 %fusion = bf16[2,343,343]{2,0,1:T(2,128)(2,1)S(1)} fusion(bf16[8,343,343]{2,0,1:T(8,128)(2,1)S(1)} %copy-done, s32[2]{0:T(128)} %param.9), kind=kOutput, calls=%fused_computation.4 | convolution fusion | flops 3764784 | bytes 2352988 | tf_op jit(solution)/shard_map/ct,tij->cij/dot_general | solution.py:507
  10.1 0.1 copy.11
  10.1 0.1 slice_bitcast_fusion
  10.2 0.0 copy-done.1
  10.2 0.8 %shard_map.87 = (f32[637,128]{1,0:T(8,128)S(1)}, bf16[128,256]{1,0:T(8,128)(2,1)S(1)}, bf16[64,343]{1,0:T(8,128)(2,1)S(1)}, bf16[128,304]{1,0:T(8,128)(2,1)S(1)}, f32[64,128]{1,0:T(8,128)S(1)}) custom-call(f32[16,16]{1,0:T(8,128)S(1)} %copy-done.1, bf16[637,128]{1,0:T(8,128)(2,1)S(1)} %get-tuple-element.35.refs_1_.refs_3_, ...), custom_call_target="tpu_custom_call" | custom-call | tf_op jit(solution)/shard_map/pallas_call | solution.py:446
  11.0 0.2 collective-permute-done.refs_0_
  11.2 1.8 %collective-permute-done.1.refs_1_ = bf16[560,128]{1,0:T(8,128)(2,1)S(1)} collective-permute-done((bf16[560,128]{1,0:T(8,128)(2,1)S(1)}, bf16[560,128]{1,0:T(8,128)(2,1)S(1)}, u32[]{:S(2)}, u32[]{:S(2)}) %collective-permute-start.1) | collective-permute-done | bytes 143392 | tf_op jit(solution)/shard_map/ppermute | solution.py:468
  13.0 0.8 %shard_map.88 = (f32[637,128]{1,0:T(8,128)S(1)}, f32[192,128]{1,0:T(8,128)S(1)}, bf16[224,128]{1,0:T(8,128)(2,1)S(1)}, bf16[192,128]{1,0:T(8,128)(2,1)S(1)}, bf1...) custom-call(bf16[560,128]{1,0:T(8,128)(2,1)S(1)} %collective-permute, ...), custom_call_target="tpu_custom_call" | custom-call | tf_op jit(solution)/shard_map/pallas_call | solution.py:446
  13.8 0.7 %collective-permute-start.3 = (bf16[224,128]{1,0:T(8,128)(2,1)S(1)}, bf16[224,128]{1,0:T(8,128)(2,1)S(1)}, u32[]{:S(2)}, u32[]{:S(2)}) collective-permute-start(bf16[224,128]{1,0:T(8,128)(2,1)S(1)} %get-tuple-element.43), channel_id=1, source_target_pairs={{0,4},{4,0},{8,12},{12,8},{16,20},{20,16},{24,28},{28,24},{1,5},{5... | collective-permute-start | bytes 172040 | tf_op jit(solution)/shard_map/ppermute | solution.py:468
  14.5 1.6 %collective-permute-start.4 = (bf16[208,128]{1,0:T(8,128)(2,1)S(1)}, bf16[208,128]{1,0:T(8,128)(2,1)S(1)}, u32[]{:S(2)}, u32[]{:S(2)}) collective-permute-start(bf16[208,128]{1,0:T(8,128)(2,1)S(1)} %get-tuple-element.44), channel_id=1, source_target_pairs={{0,8},{4,28},{8,16},{12,4},{16,24},{20,12},{24,0},{28,20},{1,9},{5... | collective-permute-start | bytes 159752 | tf_op jit(solution)/shard_map/ppermute | solution.py:468
  16.1 2.4 %collective-permute-start.2 = (bf16[192,128]{1,0:T(8,128)(2,1)S(1)}, bf16[192,128]{1,0:T(8,128)(2,1)S(1)}, u32[]{:S(2)}, u32[]{:S(2)}) collective-permute-start(bf16[192,128]{1,0:T(8,128)(2,1)S(1)} %get-tuple-element.42), channel_id=1, source_target_pairs={{0,28},{4,8},{8,4},{12,16},{16,12},{20,24},{24,20},{28,0},{1,29},{... | collective-permute-start | bytes 147464 | tf_op jit(solution)/shard_map/ppermute | solution.py:468
  18.5 0.5 %collective-permute-start.5 = (bf16[64,128]{1,0:T(8,128)(2,1)S(1)}, bf16[64,128]{1,0:T(8,128)(2,1)S(1)}, u32[]{:S(2)}, u32[]{:S(2)}) collective-permute-start(bf16[64,128]{1,0:T(8,128)(2,1)S(1)} %get-tuple-element.45), channel_id=1, source_target_pairs={{0,24},{4,12},{8,0},{12,20},{16,8},{20,28},{24,16},{28,4},{1,25},{... | collective-permute-start | bytes 49160 | tf_op jit(solution)/shard_map/ppermute | solution.py:468
  19.0 0.0 copy-start.2
  19.0 0.4 %shard_map.89 = (f32[637,128]{1,0:T(8,128)S(1)}, bf16[343,256]{1,0:T(8,128)(2,1)S(1)}, bf16[343,256]{1,0:T(8,128)(2,1)S(1)}, bf16[343,256]{1,0:T(8,128)(2,1)S(1)}, bf16[343,256]{1,0:T(8,128)(2,1)S(1)}) custom-call(f32[637,128]{1,0:T(8,128)S(1)} %get-tuple-element.46.refs_0_.refs_1_, bf16[637,128]{1,0:T(8,128)(2,1)S(1)} %get-tuple-element.35.refs_1_.refs_3_, ...), custom_call_target="tpu_custom_call" | custom-call | tf_op jit(solution)/shard_map/pallas_call | solution.py:446
  19.4 3.0 %collective-permute-done.5.refs_3_ = bf16[64,128]{1,0:T(8,128)(2,1)S(1)} collective-permute-done((bf16[64,128]{1,0:T(8,128)(2,1)S(1)}, bf16[64,128]{1,0:T(8,128)(2,1)S(1)}, u32[]{:S(2)}, u32[]{:S(2)}) %collective-permute-start.5) | collective-permute-done | bytes 16416 | tf_op jit(solution)/shard_map/ppermute | solution.py:468
  22.3 0.6 %collective-permute-done.2.refs_0_.refs_3_ = bf16[192,128]{1,0:T(8,128)(2,1)S(1)} collective-permute-done((bf16[192,128]{1,0:T(8,128)(2,1)S(1)}, bf16[192,128]{1,0:T(8,128)(2,1)S(1)}, u32[]{:S(2)}, u32[]{:S(2)}) %collective-permute-start.2) | collective-permute-done | bytes 49184 | tf_op jit(solution)/shard_map/ppermute | solution.py:468
  22.9 0.0 collective-permute-done.4.refs_2_
  22.9 0.0 collective-permute-done.3.refs_1_.refs_2_
  22.9 0.5 %shard_map.90 = (f32[637,128]{1,0:T(8,128)S(1)}, f32[192,128]{1,0:T(8,128)S(1)}, bf16[320,128]{1,0:T(8,128)(2,1)S(1)}, bf16[320,128]{1,0:T(8,128)(2,1)S(1)}, bf1...) custom-call(bf16[192,128]{1,0:T(8,128)(2,1)S(1)} %collective-permute-done.2.refs_0_.refs_3_, ...), custom_call_target="tpu_custom_call" | custom-call | tf_op jit(solution)/shard_map/pallas_call | solution.py:446
  23.5 2.5 %collective-permute-start.6 = (bf16[320,128]{1,0:T(8,128)(2,1)S(1)}, bf16[320,128]{1,0:T(8,128)(2,1)S(1)}, u32[]{:S(2)}, u32[]{:S(2)}) collective-permute-start(bf16[320,128]{1,0:T(8,128)(2,1)S(1)} %get-tuple-element.54), channel_id=1, source_target_pairs={{0,28},{4,8},{8,4},{12,16},{16,12},{20,24},{24,20},{28,0},{1,29},{... | collective-permute-start | bytes 245768 | tf_op jit(solution)/shard_map/ppermute | solution.py:468
  25.9 0.2 collective-permute-start.7
  26.1 0.7 %collective-permute-start.8 = (bf16[64,128]{1,0:T(8,128)(2,1)S(1)}, bf16[64,128]{1,0:T(8,128)(2,1)S(1)}, u32[]{:S(2)}, u32[]{:S(2)}) collective-permute-start(bf16[64,128]{1,0:T(8,128)(2,1)S(1)} %get-tuple-element.56), channel_id=1, source_target_pairs={{0,8},{4,28},{8,16},{12,4},{16,24},{20,12},{24,0},{28,20},{1,9},{5... | collective-permute-start | bytes 49160 | tf_op jit(solution)/shard_map/ppermute | solution.py:468
  26.8 3.2 %collective-permute-start.9 = (bf16[64,128]{1,0:T(8,128)(2,1)S(1)}, bf16[64,128]{1,0:T(8,128)(2,1)S(1)}, u32[]{:S(2)}, u32[]{:S(2)}) collective-permute-start(bf16[64,128]{1,0:T(8,128)(2,1)S(1)} %get-tuple-element.57), channel_id=1, source_target_pairs={{0,24},{4,12},{8,0},{12,20},{16,8},{20,28},{24,16},{28,4},{1,25},{... | collective-permute-start | bytes 49160 | tf_op jit(solution)/shard_map/ppermute | solution.py:468
  29.9 0.3 shard_map.91.refs_4_
  30.2 1.4 %collective-permute-done.8.refs_2_ = bf16[64,128]{1,0:T(8,128)(2,1)S(1)} collective-permute-done((bf16[64,128]{1,0:T(8,128)(2,1)S(1)}, bf16[64,128]{1,0:T(8,128)(2,1)S(1)}, u32[]{:S(2)}, u32[]{:S(2)}) %collective-permute-start.8) | collective-permute-done | bytes 16416 | tf_op jit(solution)/shard_map/ppermute | solution.py:468
  31.7 0.0 collective-permute-done.9.refs_3_
  31.7 0.0 collective-permute-done.6.refs_0_
  31.7 0.0 collective-permute-done.7.refs_1_
  31.7 0.0 copy-done.2
  31.7 0.5 %shard_map.92 = (f32[637,128]{1,0:T(8,128)S(1)}, f32[1,637]{1,0:T(1,128)S(1)}) custom-call(bf16[320,128]{1,0:T(8,128)(2,1)S(1)} %collective-permute-done.6.refs_0_, bf16[320,128]{1,0:T(8,128)(2,1)S(1)} %collective-permute-done.7.refs_1_, bf16[64,128]{1,0:T(8,128)(2,1)S(1)} %collective-permute-done.8.refs_2_, ...), custom_call_target="tpu_custom_call" | custom-call | tf_op jit(solution)/shard_map/pallas_call | solution.py:446
  32.2 0.0 collective-permute-start.12
  32.2 1.6 %collective-permute-start.11 = (f32[1,637]{1,0:T(1,128)S(1)}, f32[1,637]{1,0:T(1,128)S(1)}, u32[]{:S(2)}, u32[]{:S(2)}) collective-permute-start(f32[1,637]{1,0:T(1,128)S(1)} %get-tuple-element.63), channel_id=1, source_target_pairs={{0,2},{1,3},{2,0},{3,1},{4,6},{5,7},{6,4},{7,5},{8,10},{9,11},{10,... | collective-permute-start | bytes 7652 | tf_op jit(solution)/shard_map/ppermute | solution.py:570
  33.8 0.3 collective-permute-start.10
  34.1 0.7 %copy.12 = f32[637,128]{1,0:T(8,128)} copy(f32[637,128]{1,0:T(8,128)S(1)} %get-tuple-element.66) | data formatting | bytes 652288
  34.8 0.4 %collective-permute-done.12 = f32[1,637]{1,0:T(1,128)S(1)} collective-permute-done((f32[1,637]{1,0:T(1,128)S(1)}, f32[1,637]{1,0:T(1,128)S(1)}, u32[]{:S(2)}, u32[]{:S(2)}) %collective-permute-start.12) | collective-permute-done | bytes 2580 | tf_op jit(solution)/shard_map/ppermute | solution.py:570
  35.2 0.7 %collective-permute-done.11 = f32[1,637]{1,0:T(1,128)S(1)} collective-permute-done((f32[1,637]{1,0:T(1,128)S(1)}, f32[1,637]{1,0:T(1,128)S(1)}, u32[]{:S(2)}, u32[]{:S(2)}) %collective-permute-start.11) | collective-permute-done | bytes 2580 | tf_op jit(solution)/shard_map/ppermute | solution.py:570
  35.9 0.0 collective-permute-done.10
  35.9 0.6 %add_reduce_fusion = f32[637]{0:T(1024)} fusion(f32[1,637]{1,0:T(1,128)S(1)} %collective-permute-done.12, f32[1,637]{1,0:T(1,128)S(1)} %collective-permute-done.11, f32[1,637]{1,0:T(1,128)S(1)} %get-tuple-element.63, f32[1,637]{1,0:T(1,128)S(1)} %collective-permute-done.10), kind=kLoop, calls=%fused_computation.3 | loop fusion | flops 1911 | bytes 12740 | tf_op jit(solution)/shard_map/add | solution.py:573
Async XLA Ops:
  0.6 8.0 %copy-start = (bf16[8,343,343]{2,0,1:T(8,128)(2,1)S(1)}, bf16[8,343,343]{2,0,1:T(8,128)(2,1)}, u32[]{:S(2)}) copy-start(bf16[8,343,343]{2,0,1:T(8,128)(2,1)} %param.8) | copy-start | bytes 5647156
  2.1 9.1 %collective-permute-start = (bf16[560,128]{1,0:T(8,128)(2,1)S(1)}, bf16[560,128]{1,0:T(8,128)(2,1)S(1)}, u32[]{:S(2)}, u32[]{:S(2)}) collective-permute-start(bf16[560,128]{1,0:T(8,128)(2,1)S(1)} %get-tuple-element.33.refs_4_), channel_id=1, source_target_pairs={{0,4},{4,0},{8,12},{12,8},{16,20},{20,16},{24,28},{28,24},{1,5},{5... | collective-permute-start | bytes 430088 | tf_op jit(solution)/shard_map/ppermute | solution.py:468
  5.1 5.1 %copy-start.1 = (f32[16,16]{1,0:T(8,128)S(1)}, f32[16,16]{1,0:T(8,128)}, u32[]{:S(2)}) copy-start(f32[16,16]{1,0:T(8,128)} %refs_0_.3) | copy-start | bytes 3076
  5.1 7.9 %collective-permute-start.1 = (bf16[560,128]{1,0:T(8,128)(2,1)S(1)}, bf16[560,128]{1,0:T(8,128)(2,1)S(1)}, u32[]{:S(2)}, u32[]{:S(2)}) collective-permute-start(bf16[560,128]{1,0:T(8,128)(2,1)S(1)} %get-tuple-element.34.refs_5_), channel_id=1, source_target_pairs={{0,28},{4,8},{8,4},{12,16},{16,12},{20,24},{24,20},{28,0},{1,29},{... | collective-permute-start | bytes 430088 | tf_op jit(solution)/shard_map/ppermute | solution.py:468
  13.8 9.1 %collective-permute-start.3 = (bf16[224,128]{1,0:T(8,128)(2,1)S(1)}, bf16[224,128]{1,0:T(8,128)(2,1)S(1)}, u32[]{:S(2)}, u32[]{:S(2)}) collective-permute-start(bf16[224,128]{1,0:T(8,128)(2,1)S(1)} %get-tuple-element.43), channel_id=1, source_target_pairs={{0,4},{4,0},{8,12},{12,8},{16,20},{20,16},{24,28},{28,24},{1,5},{5... | collective-permute-start | bytes 172040 | tf_op jit(solution)/shard_map/ppermute | solution.py:468
  14.5 8.4 %collective-permute-start.4 = (bf16[208,128]{1,0:T(8,128)(2,1)S(1)}, bf16[208,128]{1,0:T(8,128)(2,1)S(1)}, u32[]{:S(2)}, u32[]{:S(2)}) collective-permute-start(bf16[208,128]{1,0:T(8,128)(2,1)S(1)} %get-tuple-element.44), channel_id=1, source_target_pairs={{0,8},{4,28},{8,16},{12,4},{16,24},{20,12},{24,0},{28,20},{1,9},{5... | collective-permute-start | bytes 159752 | tf_op jit(solution)/shard_map/ppermute | solution.py:468
  16.1 6.8 %collective-permute-start.2 = (bf16[192,128]{1,0:T(8,128)(2,1)S(1)}, bf16[192,128]{1,0:T(8,128)(2,1)S(1)}, u32[]{:S(2)}, u32[]{:S(2)}) collective-permute-start(bf16[192,128]{1,0:T(8,128)(2,1)S(1)} %get-tuple-element.42), channel_id=1, source_target_pairs={{0,28},{4,8},{8,4},{12,16},{16,12},{20,24},{24,20},{28,0},{1,29},{... | collective-permute-start | bytes 147464 | tf_op jit(solution)/shard_map/ppermute | solution.py:468
  18.5 3.8 %collective-permute-start.5 = (bf16[64,128]{1,0:T(8,128)(2,1)S(1)}, bf16[64,128]{1,0:T(8,128)(2,1)S(1)}, u32[]{:S(2)}, u32[]{:S(2)}) collective-permute-start(bf16[64,128]{1,0:T(8,128)(2,1)S(1)} %get-tuple-element.45), channel_id=1, source_target_pairs={{0,24},{4,12},{8,0},{12,20},{16,8},{20,28},{24,16},{28,4},{1,25},{... | collective-permute-start | bytes 49160 | tf_op jit(solution)/shard_map/ppermute | solution.py:468
  19.0 12.7 %copy-start.2 = (f32[128]{0:T(128)S(1)}, f32[128]{0:T(128)}, u32[]{:S(2)}) copy-start(f32[128]{0:T(128)} %param.13) | copy-start | bytes 1540
  23.5 8.2 %collective-permute-start.6 = (bf16[320,128]{1,0:T(8,128)(2,1)S(1)}, bf16[320,128]{1,0:T(8,128)(2,1)S(1)}, u32[]{:S(2)}, u32[]{:S(2)}) collective-permute-start(bf16[320,128]{1,0:T(8,128)(2,1)S(1)} %get-tuple-element.54), channel_id=1, source_target_pairs={{0,28},{4,8},{8,4},{12,16},{16,12},{20,24},{24,20},{28,0},{1,29},{... | collective-permute-start | bytes 245768 | tf_op jit(solution)/shard_map/ppermute | solution.py:468
  25.9 5.7 %collective-permute-start.7 = (bf16[320,128]{1,0:T(8,128)(2,1)S(1)}, bf16[320,128]{1,0:T(8,128)(2,1)S(1)}, u32[]{:S(2)}, u32[]{:S(2)}) collective-permute-start(bf16[320,128]{1,0:T(8,128)(2,1)S(1)} %get-tuple-element.55), channel_id=1, source_target_pairs={{0,4},{4,0},{8,12},{12,8},{16,20},{20,16},{24,28},{28,24},{1,5},{5... | collective-permute-start | bytes 245768 | tf_op jit(solution)/shard_map/ppermute | solution.py:468
  26.1 5.5 %collective-permute-start.8 = (bf16[64,128]{1,0:T(8,128)(2,1)S(1)}, bf16[64,128]{1,0:T(8,128)(2,1)S(1)}, u32[]{:S(2)}, u32[]{:S(2)}) collective-permute-start(bf16[64,128]{1,0:T(8,128)(2,1)S(1)} %get-tuple-element.56), channel_id=1, source_target_pairs={{0,8},{4,28},{8,16},{12,4},{16,24},{20,12},{24,0},{28,20},{1,9},{5... | collective-permute-start | bytes 49160 | tf_op jit(solution)/shard_map/ppermute | solution.py:468
  26.8 4.9 %collective-permute-start.9 = (bf16[64,128]{1,0:T(8,128)(2,1)S(1)}, bf16[64,128]{1,0:T(8,128)(2,1)S(1)}, u32[]{:S(2)}, u32[]{:S(2)}) collective-permute-start(bf16[64,128]{1,0:T(8,128)(2,1)S(1)} %get-tuple-element.57), channel_id=1, source_target_pairs={{0,24},{4,12},{8,0},{12,20},{16,8},{20,28},{24,16},{28,4},{1,25},{... | collective-permute-start | bytes 49160 | tf_op jit(solution)/shard_map/ppermute | solution.py:468
  32.2 3.0 %collective-permute-start.12 = (f32[1,637]{1,0:T(1,128)S(1)}, f32[1,637]{1,0:T(1,128)S(1)}, u32[]{:S(2)}, u32[]{:S(2)}) collective-permute-start(f32[1,637]{1,0:T(1,128)S(1)} %get-tuple-element.63), channel_id=1, source_target_pairs={{0,3},{1,2},{2,1},{3,0},{4,7},{5,6},{6,5},{7,4},{8,11},{9,10},{10,... | collective-permute-start | bytes 7652 | tf_op jit(solution)/shard_map/ppermute | solution.py:570
  32.2 3.7 %collective-permute-start.11 = (f32[1,637]{1,0:T(1,128)S(1)}, f32[1,637]{1,0:T(1,128)S(1)}, u32[]{:S(2)}, u32[]{:S(2)}) collective-permute-start(f32[1,637]{1,0:T(1,128)S(1)} %get-tuple-element.63), channel_id=1, source_target_pairs={{0,2},{1,3},{2,0},{3,1},{4,6},{5,7},{6,4},{7,5},{8,10},{9,11},{10,... | collective-permute-start | bytes 7652 | tf_op jit(solution)/shard_map/ppermute | solution.py:570
  33.8 2.1 %collective-permute-start.10 = (f32[1,637]{1,0:T(1,128)S(1)}, f32[1,637]{1,0:T(1,128)S(1)}, u32[]{:S(2)}, u32[]{:S(2)}) collective-permute-start(f32[1,637]{1,0:T(1,128)S(1)} %get-tuple-element.63), channel_id=1, source_target_pairs={{0,1},{1,0},{2,3},{3,2},{4,5},{5,4},{6,7},{7,6},{8,9},{9,8},{10,11... | collective-permute-start | bytes 7652 | tf_op jit(solution)/shard_map/ppermute | solution.py:570

commit v9 on v7

--- a/solution.py
+++ b/solution.py
@@ -249,12 +249,15 @@
 
 
 def beside_first(
-    z, coupling, x0, cell0, cell1, mine_near, mine_over, base, mix, end_rows, outer, xs
+    z, gain, coupling, x0, cell0, cell1, mine_near, mine_over, base, mix, end_rows, outer, xs
 ):
     xs[...] = x0[...].astype(F32)
-    base[...] = (-CENTRE) * (face_scale(z) * xs[...])
+    base[...] = (-CENTRE * gain) * (face_scale(z) * xs[...])
     add_cells(
-        z, dot(cell0[...], x0[: z.nodes, :]), dot(cell1[...], xs[z.last :, :].astype(BF16)), base
+        z,
+        gain * dot(cell0[...], x0[: z.nodes, :]),
+        gain * dot(cell1[...], xs[z.last :, :].astype(BF16)),
+        base,
     )
     size = 2 * z.coef
     row = lax.broadcasted_iota(jnp.int32, (size, z.proj), 0)
@@ -308,10 +311,10 @@
     base, x0, own0, own1, own_coeffs, outer, from_near, from_over, mix,
     part, coeffs, near, over, far, farther,
     rows0, rows1,
-    xs, terms, faces, flat0, flat1,
+    xs, faces, flat0, flat1,
 ):
     c = z.coef
-    xs[...] = x0[...].astype(F32)
+    xs[z.right_lo :, :] = x0[z.right_lo :, :].astype(F32)
     rows0[:c, :] = own0[...]
     rows1[:c, :] = own1[...]
     for k in range(z.chunks):
@@ -327,20 +330,19 @@
     before, after = take(from_near, from_over, (slice(z.m_coef, z.m_rows), slice(None)))
     before = before.astype(F32) + dot(rows0[c:, :], x0[: z.nodes, :])
     after = after.astype(F32) + dot(rows1[c:, :], xs[z.last :, :].astype(BF16))
-    terms[...] = base[...]
     high, low = halves(jnp.concatenate([before, own, after], axis=1))
     mix_high, mix_low = mix[:c, :c], mix[:c, 2 * c : 3 * c]
     weighted = dot(mix_high, high) + dot(mix_high, low) + dot(mix_low, high)
     weighted = weighted.astype(BF16)
     n = before.shape[1]
     before, own, after = (weighted[:, i * n : (i + 1) * n] for i in range(3))
+    part[...] = base[...]
     add_cells(
         z,
-        dot(flat0[...], jnp.concatenate([own, before], axis=0)),
-        dot(flat1[...], jnp.concatenate([own, after], axis=0)),
-        terms,
-    )
-    part[...] = terms[...] * gain
+        gain * dot(flat0[...], jnp.concatenate([own, before], axis=0)),
+        gain * dot(flat1[...], jnp.concatenate([own, after], axis=0)),
+        part,
+    )
     send_part(z, rows0, rows1, part, coeffs, near, over, far, farther, faces)
     for message, used in ((near, z.l_term), (over, z.l_term), (far, c), (farther, c)):
         if message.shape[0] > used:
@@ -512,7 +514,7 @@
     matrices = matrices.astype(BF16)
     cell0, cell1 = matrices[0], matrices[-1]
     base, mix, end_rows, outer = call(
-        functools.partial(beside_first, z),
+        functools.partial(beside_first, z, gains[0]),
         [field, ((2 * c, 4 * c), BF16), ((z.pad_face, n), BF16), ((2 * c, z.halo), BF16)],
         [scratch],
         coupling, x0, cell0, cell1, near, over,
@@ -528,7 +530,7 @@
             [field, coeffs]
             + second_messages
             + [((2 * c, n), BF16)] * 2,
-            [scratch, scratch, faces] + [pltpu.VMEM((n, 2 * c), BF16)] * 2,
+            [scratch, faces] + [pltpu.VMEM((n, 2 * c), BF16)] * 2,
             base, x0, own0, own1, own_share, outer, from_near, from_over, mix,
             order=FIRST_ORDER,
         )

time: 36.9 us -> 36.9 us (level)
  no operation moved by 1% of the time
where the time goes in v9:
time: 36.9 us; the launch traced here: 36.5 us
  starting transfers between devices  20.1 us (54%)
  waiting for transfers between devices  8.12 us (22%)
  Pallas kernels  4.64 us (13%)
  matrix products  1.41 us (4%)
  local copies, waits for them, and re-layouts  0.86 us (2%)
  between operations  0.74 us (2%)
  other arithmetic  0.61 us (2%)
    ppermute x10, starting transfers between devices, exchanged(): return lax.ppermute(array, 'cells', pairs)  18.2 us
    ppermute x10, waiting for transfers between devices, exchanged(): return lax.ppermute(array, 'cells', pairs)  7.03 us
    pallas_call x7, Pallas kernels, call(): pl.pallas_call(ordered, out_shape=[pltpu.VMEM(s, t) for s, t in outs], in...  4.64 us
    ppermute x3, starting transfers between devices, partner(): return lax.ppermute(array, 'states', [(i, i ^ by) for i in range(groups)])  1.88 us
    dot_general x1, matrix products, body(): jnp.einsum('ct,tij->cij', onehot, cell_table, preferred_element_type=F32)  1.41 us
    ppermute x3, waiting for transfers between devices, partner(): return lax.ppermute(array, 'states', [(i, i ^ by) for i in range(groups)])  1.09 us
    unnamed x7, local copies, waits for them, and re-layouts  0.74 us
  transfers between devices with their start and end apart: 13, of which 7 were waited for; matrix products, arithmetic and copies ran while one was open for 6% of the time, Pallas kernels for 4%

profile of v9, /device:TPU:0, one launch (start us, length us, event | category | flops | bytes accessed | tf_op | source)
XLA Modules:
  0.0 36.5 jit_solution(13300901247812265095)
XLA Ops:
  0.6 0.0 copy-start
  0.6 1.4 %shard_map.86 = (bf16[637,128]{1,0:T(8,128)(2,1)S(1)}, bf16[560,128]{1,0:T(8,128)(2,1)S(1)}, bf16[560,128]{1,0:T(8,128)(2,1)S(1)}, bf16[64,343]{1,0:T(8,128)(2,1...) custom-call(s32[4]{0:T(128)} %refs_0_.2, bf16[637,128]{1,0:T(8,128)(2,1)} %refs_1_.1, ...), custom_call_target="tpu_custom_call" | custom-call | tf_op jit(solution)/shard_map/pallas_call | solution.py:451
  2.1 3.0 %collective-permute-start = (bf16[560,128]{1,0:T(8,128)(2,1)S(1)}, bf16[560,128]{1,0:T(8,128)(2,1)S(1)}, u32[]{:S(2)}, u32[]{:S(2)}) collective-permute-start(bf16[560,128]{1,0:T(8,128)(2,1)S(1)} %get-tuple-element.33.refs_4_), channel_id=1, source_target_pairs={{0,4},{4,0},{8,12},{12,8},{16,20},{20,16},{24,28},{28,24},{1,5},{5... | collective-permute-start | bytes 430088 | tf_op jit(solution)/shard_map/ppermute | solution.py:473
  5.1 0.0 copy-start.1
  5.1 3.5 %collective-permute-start.1 = (bf16[560,128]{1,0:T(8,128)(2,1)S(1)}, bf16[560,128]{1,0:T(8,128)(2,1)S(1)}, u32[]{:S(2)}, u32[]{:S(2)}) collective-permute-start(bf16[560,128]{1,0:T(8,128)(2,1)S(1)} %get-tuple-element.34.refs_5_), channel_id=1, source_target_pairs={{0,28},{4,8},{8,4},{12,16},{16,12},{20,24},{24,20},{28,0},{1,29},{... | collective-permute-start | bytes 430088 | tf_op jit(solution)/shard_map/ppermute | solution.py:473
  8.7 0.0 copy-done
  8.7 1.4 %fusion = bf16[2,343,343]{2,0,1:T(2,128)(2,1)S(1)} fusion(bf16[8,343,343]{2,0,1:T(8,128)(2,1)S(1)} %copy-done, s32[2]{0:T(128)} %param.9), kind=kOutput, calls=%fused_computation.4 | convolution fusion | flops 3764784 | bytes 2352988 | tf_op jit(solution)/shard_map/ct,tij->cij/dot_general | solution.py:513
  10.1 0.1 copy.11
  10.2 0.1 slice_bitcast_fusion
  10.2 0.0 copy-done.1
  10.2 0.7 %shard_map.87 = (f32[637,128]{1,0:T(8,128)S(1)}, bf16[128,256]{1,0:T(8,128)(2,1)S(1)}, bf16[64,343]{1,0:T(8,128)(2,1)S(1)}, bf16[128,304]{1,0:T(8,128)(2,1)S(1)}) custom-call(f32[16,16]{1,0:T(8,128)S(1)} %copy-done.1, bf16[637,128]{1,0:T(8,128)(2,1)S(1)} %get-tuple-element.35.refs_1_.refs_3_, bf16[343,343]{1,0:T(8,128)(2,1)S(1)} %get-tuple-element.65.refs_2_.refs_6_.refs_4_, ...), custom_call_target="tpu_custom_call" | custom-call | tf_op jit(solution)/shard_map/pallas_call | solution.py:451
  11.0 0.3 collective-permute-done.refs_0_
  11.2 1.8 %collective-permute-done.1.refs_1_ = bf16[560,128]{1,0:T(8,128)(2,1)S(1)} collective-permute-done((bf16[560,128]{1,0:T(8,128)(2,1)S(1)}, bf16[560,128]{1,0:T(8,128)(2,1)S(1)}, u32[]{:S(2)}, u32[]{:S(2)}) %collective-permute-start.1) | collective-permute-done | bytes 143392 | tf_op jit(solution)/shard_map/ppermute | solution.py:473
  13.0 0.8 %shard_map.88 = (f32[637,128]{1,0:T(8,128)S(1)}, f32[192,128]{1,0:T(8,128)S(1)}, bf16[224,128]{1,0:T(8,128)(2,1)S(1)}, bf16[192,128]{1,0:T(8,128)(2,1)S(1)}, bf1...) custom-call(bf16[560,128]{1,0:T(8,128)(2,1)S(1)} %collective-permute, ...), custom_call_target="tpu_custom_call" | custom-call | tf_op jit(solution)/shard_map/pallas_call | solution.py:451
  13.8 0.7 %collective-permute-start.3 = (bf16[224,128]{1,0:T(8,128)(2,1)S(1)}, bf16[224,128]{1,0:T(8,128)(2,1)S(1)}, u32[]{:S(2)}, u32[]{:S(2)}) collective-permute-start(bf16[224,128]{1,0:T(8,128)(2,1)S(1)} %get-tuple-element.43), channel_id=1, source_target_pairs={{0,4},{4,0},{8,12},{12,8},{16,20},{20,16},{24,28},{28,24},{1,5},{5... | collective-permute-start | bytes 172040 | tf_op jit(solution)/shard_map/ppermute | solution.py:473
  14.5 1.6 %collective-permute-start.4 = (bf16[208,128]{1,0:T(8,128)(2,1)S(1)}, bf16[208,128]{1,0:T(8,128)(2,1)S(1)}, u32[]{:S(2)}, u32[]{:S(2)}) collective-permute-start(bf16[208,128]{1,0:T(8,128)(2,1)S(1)} %get-tuple-element.44), channel_id=1, source_target_pairs={{0,8},{4,28},{8,16},{12,4},{16,24},{20,12},{24,0},{28,20},{1,9},{5... | collective-permute-start | bytes 159752 | tf_op jit(solution)/shard_map/ppermute | solution.py:473
  16.1 2.4 %collective-permute-start.2 = (bf16[192,128]{1,0:T(8,128)(2,1)S(1)}, bf16[192,128]{1,0:T(8,128)(2,1)S(1)}, u32[]{:S(2)}, u32[]{:S(2)}) collective-permute-start(bf16[192,128]{1,0:T(8,128)(2,1)S(1)} %get-tuple-element.42), channel_id=1, source_target_pairs={{0,28},{4,8},{8,4},{12,16},{16,12},{20,24},{24,20},{28,0},{1,29},{... | collective-permute-start | bytes 147464 | tf_op jit(solution)/shard_map/ppermute | solution.py:473
  18.5 0.5 %collective-permute-start.5 = (bf16[64,128]{1,0:T(8,128)(2,1)S(1)}, bf16[64,128]{1,0:T(8,128)(2,1)S(1)}, u32[]{:S(2)}, u32[]{:S(2)}) collective-permute-start(bf16[64,128]{1,0:T(8,128)(2,1)S(1)} %get-tuple-element.45), channel_id=1, source_target_pairs={{0,24},{4,12},{8,0},{12,20},{16,8},{20,28},{24,16},{28,4},{1,25},{... | collective-permute-start | bytes 49160 | tf_op jit(solution)/shard_map/ppermute | solution.py:473
  19.0 0.0 copy-start.2
  19.0 0.4 %shard_map.89 = (f32[637,128]{1,0:T(8,128)S(1)}, bf16[343,256]{1,0:T(8,128)(2,1)S(1)}, bf16[343,256]{1,0:T(8,128)(2,1)S(1)}, bf16[343,256]{1,0:T(8,128)(2,1)S(1)}, bf16[343,256]{1,0:T(8,128)(2,1)S(1)}) custom-call(f32[637,128]{1,0:T(8,128)S(1)} %get-tuple-element.46.refs_0_.refs_1_, bf16[637,128]{1,0:T(8,128)(2,1)S(1)} %get-tuple-element.35.refs_1_.refs_3_, ...), custom_call_target="tpu_custom_call" | custom-call | tf_op jit(solution)/shard_map/pallas_call | solution.py:451
  19.4 3.0 %collective-permute-done.5.refs_3_ = bf16[64,128]{1,0:T(8,128)(2,1)S(1)} collective-permute-done((bf16[64,128]{1,0:T(8,128)(2,1)S(1)}, bf16[64,128]{1,0:T(8,128)(2,1)S(1)}, u32[]{:S(2)}, u32[]{:S(2)}) %collective-permute-start.5) | collective-permute-done | bytes 16416 | tf_op jit(solution)/shard_map/ppermute | solution.py:473
  22.4 0.6 %collective-permute-done.2.refs_0_.refs_3_ = bf16[192,128]{1,0:T(8,128)(2,1)S(1)} collective-permute-done((bf16[192,128]{1,0:T(8,128)(2,1)S(1)}, bf16[192,128]{1,0:T(8,128)(2,1)S(1)}, u32[]{:S(2)}, u32[]{:S(2)}) %collective-permute-start.2) | collective-permute-done | bytes 49184 | tf_op jit(solution)/shard_map/ppermute | solution.py:473
  22.9 0.0 collective-permute-done.4.refs_2_
  22.9 0.0 collective-permute-done.3.refs_1_.refs_2_
  22.9 0.5 %shard_map.90 = (f32[637,128]{1,0:T(8,128)S(1)}, f32[192,128]{1,0:T(8,128)S(1)}, bf16[320,128]{1,0:T(8,128)(2,1)S(1)}, bf16[320,128]{1,0:T(8,128)(2,1)S(1)}, bf1...) custom-call(bf16[192,128]{1,0:T(8,128)(2,1)S(1)} %collective-permute-done.2.refs_0_.refs_3_, ...), custom_call_target="tpu_custom_call" | custom-call | tf_op jit(solution)/shard_map/pallas_call | solution.py:451
  23.5 2.5 %collective-permute-start.6 = (bf16[320,128]{1,0:T(8,128)(2,1)S(1)}, bf16[320,128]{1,0:T(8,128)(2,1)S(1)}, u32[]{:S(2)}, u32[]{:S(2)}) collective-permute-start(bf16[320,128]{1,0:T(8,128)(2,1)S(1)} %get-tuple-element.54), channel_id=1, source_target_pairs={{0,28},{4,8},{8,4},{12,16},{16,12},{20,24},{24,20},{28,0},{1,29},{... | collective-permute-start | bytes 245768 | tf_op jit(solution)/shard_map/ppermute | solution.py:473
  25.9 0.2 collective-permute-start.7
  26.1 0.7 %collective-permute-start.8 = (bf16[64,128]{1,0:T(8,128)(2,1)S(1)}, bf16[64,128]{1,0:T(8,128)(2,1)S(1)}, u32[]{:S(2)}, u32[]{:S(2)}) collective-permute-start(bf16[64,128]{1,0:T(8,128)(2,1)S(1)} %get-tuple-element.56), channel_id=1, source_target_pairs={{0,8},{4,28},{8,16},{12,4},{16,24},{20,12},{24,0},{28,20},{1,9},{5... | collective-permute-start | bytes 49160 | tf_op jit(solution)/shard_map/ppermute | solution.py:473
  26.8 3.2 %collective-permute-start.9 = (bf16[64,128]{1,0:T(8,128)(2,1)S(1)}, bf16[64,128]{1,0:T(8,128)(2,1)S(1)}, u32[]{:S(2)}, u32[]{:S(2)}) collective-permute-start(bf16[64,128]{1,0:T(8,128)(2,1)S(1)} %get-tuple-element.57), channel_id=1, source_target_pairs={{0,24},{4,12},{8,0},{12,20},{16,8},{20,28},{24,16},{28,4},{1,25},{... | collective-permute-start | bytes 49160 | tf_op jit(solution)/shard_map/ppermute | solution.py:473
  29.9 0.3 shard_map.91.refs_4_
  30.2 1.4 %collective-permute-done.8.refs_2_ = bf16[64,128]{1,0:T(8,128)(2,1)S(1)} collective-permute-done((bf16[64,128]{1,0:T(8,128)(2,1)S(1)}, bf16[64,128]{1,0:T(8,128)(2,1)S(1)}, u32[]{:S(2)}, u32[]{:S(2)}) %collective-permute-start.8) | collective-permute-done | bytes 16416 | tf_op jit(solution)/shard_map/ppermute | solution.py:473
  31.7 0.0 collective-permute-done.9.refs_3_
  31.7 0.0 collective-permute-done.6.refs_0_
  31.7 0.0 collective-permute-done.7.refs_1_
  31.7 0.0 copy-done.2
  31.7 0.5 %shard_map.92 = (f32[637,128]{1,0:T(8,128)S(1)}, f32[1,637]{1,0:T(1,128)S(1)}) custom-call(bf16[320,128]{1,0:T(8,128)(2,1)S(1)} %collective-permute-done.6.refs_0_, bf16[320,128]{1,0:T(8,128)(2,1)S(1)} %collective-permute-done.7.refs_1_, bf16[64,128]{1,0:T(8,128)(2,1)S(1)} %collective-permute-done.8.refs_2_, ...), custom_call_target="tpu_custom_call" | custom-call | tf_op jit(solution)/shard_map/pallas_call | solution.py:451
  32.2 0.0 collective-permute-start.12
  32.2 1.6 %collective-permute-start.11 = (f32[1,637]{1,0:T(1,128)S(1)}, f32[1,637]{1,0:T(1,128)S(1)}, u32[]{:S(2)}, u32[]{:S(2)}) collective-permute-start(f32[1,637]{1,0:T(1,128)S(1)} %get-tuple-element.63), channel_id=1, source_target_pairs={{0,2},{1,3},{2,0},{3,1},{4,6},{5,7},{6,4},{7,5},{8,10},{9,11},{10,... | collective-permute-start | bytes 7652 | tf_op jit(solution)/shard_map/ppermute | solution.py:576
  33.8 0.3 collective-permute-start.10
  34.1 0.7 %copy.12 = f32[637,128]{1,0:T(8,128)} copy(f32[637,128]{1,0:T(8,128)S(1)} %get-tuple-element.66) | data formatting | bytes 652288
  34.8 0.4 %collective-permute-done.12 = f32[1,637]{1,0:T(1,128)S(1)} collective-permute-done((f32[1,637]{1,0:T(1,128)S(1)}, f32[1,637]{1,0:T(1,128)S(1)}, u32[]{:S(2)}, u32[]{:S(2)}) %collective-permute-start.12) | collective-permute-done | bytes 2580 | tf_op jit(solution)/shard_map/ppermute | solution.py:576
  35.2 0.7 %collective-permute-done.11 = f32[1,637]{1,0:T(1,128)S(1)} collective-permute-done((f32[1,637]{1,0:T(1,128)S(1)}, f32[1,637]{1,0:T(1,128)S(1)}, u32[]{:S(2)}, u32[]{:S(2)}) %collective-permute-start.11) | collective-permute-done | bytes 2580 | tf_op jit(solution)/shard_map/ppermute | solution.py:576
  35.9 0.0 collective-permute-done.10
  35.9 0.6 %add_reduce_fusion = f32[637]{0:T(1024)} fusion(f32[1,637]{1,0:T(1,128)S(1)} %collective-permute-done.12, f32[1,637]{1,0:T(1,128)S(1)} %collective-permute-done.11, f32[1,637]{1,0:T(1,128)S(1)} %get-tuple-element.63, f32[1,637]{1,0:T(1,128)S(1)} %collective-permute-done.10), kind=kLoop, calls=%fused_computation.3 | loop fusion | flops 1911 | bytes 12740 | tf_op jit(solution)/shard_map/add | solution.py:579
Async XLA Ops:
  0.6 8.0 %copy-start = (bf16[8,343,343]{2,0,1:T(8,128)(2,1)S(1)}, bf16[8,343,343]{2,0,1:T(8,128)(2,1)}, u32[]{:S(2)}) copy-start(bf16[8,343,343]{2,0,1:T(8,128)(2,1)} %param.8) | copy-start | bytes 5647156
  2.1 9.1 %collective-permute-start = (bf16[560,128]{1,0:T(8,128)(2,1)S(1)}, bf16[560,128]{1,0:T(8,128)(2,1)S(1)}, u32[]{:S(2)}, u32[]{:S(2)}) collective-permute-start(bf16[560,128]{1,0:T(8,128)(2,1)S(1)} %get-tuple-element.33.refs_4_), channel_id=1, source_target_pairs={{0,4},{4,0},{8,12},{12,8},{16,20},{20,16},{24,28},{28,24},{1,5},{5... | collective-permute-start | bytes 430088 | tf_op jit(solution)/shard_map/ppermute | solution.py:473
  5.1 5.1 %copy-start.1 = (f32[16,16]{1,0:T(8,128)S(1)}, f32[16,16]{1,0:T(8,128)}, u32[]{:S(2)}) copy-start(f32[16,16]{1,0:T(8,128)} %refs_0_.3) | copy-start | bytes 3076
  5.1 7.9 %collective-permute-start.1 = (bf16[560,128]{1,0:T(8,128)(2,1)S(1)}, bf16[560,128]{1,0:T(8,128)(2,1)S(1)}, u32[]{:S(2)}, u32[]{:S(2)}) collective-permute-start(bf16[560,128]{1,0:T(8,128)(2,1)S(1)} %get-tuple-element.34.refs_5_), channel_id=1, source_target_pairs={{0,28},{4,8},{8,4},{12,16},{16,12},{20,24},{24,20},{28,0},{1,29},{... | collective-permute-start | bytes 430088 | tf_op jit(solution)/shard_map/ppermute | solution.py:473
  13.8 9.1 %collective-permute-start.3 = (bf16[224,128]{1,0:T(8,128)(2,1)S(1)}, bf16[224,128]{1,0:T(8,128)(2,1)S(1)}, u32[]{:S(2)}, u32[]{:S(2)}) collective-permute-start(bf16[224,128]{1,0:T(8,128)(2,1)S(1)} %get-tuple-element.43), channel_id=1, source_target_pairs={{0,4},{4,0},{8,12},{12,8},{16,20},{20,16},{24,28},{28,24},{1,5},{5... | collective-permute-start | bytes 172040 | tf_op jit(solution)/shard_map/ppermute | solution.py:473
  14.5 8.4 %collective-permute-start.4 = (bf16[208,128]{1,0:T(8,128)(2,1)S(1)}, bf16[208,128]{1,0:T(8,128)(2,1)S(1)}, u32[]{:S(2)}, u32[]{:S(2)}) collective-permute-start(bf16[208,128]{1,0:T(8,128)(2,1)S(1)} %get-tuple-element.44), channel_id=1, source_target_pairs={{0,8},{4,28},{8,16},{12,4},{16,24},{20,12},{24,0},{28,20},{1,9},{5... | collective-permute-start | bytes 159752 | tf_op jit(solution)/shard_map/ppermute | solution.py:473
  16.1 6.8 %collective-permute-start.2 = (bf16[192,128]{1,0:T(8,128)(2,1)S(1)}, bf16[192,128]{1,0:T(8,128)(2,1)S(1)}, u32[]{:S(2)}, u32[]{:S(2)}) collective-permute-start(bf16[192,128]{1,0:T(8,128)(2,1)S(1)} %get-tuple-element.42), channel_id=1, source_target_pairs={{0,28},{4,8},{8,4},{12,16},{16,12},{20,24},{24,20},{28,0},{1,29},{... | collective-permute-start | bytes 147464 | tf_op jit(solution)/shard_map/ppermute | solution.py:473
  18.5 3.8 %collective-permute-start.5 = (bf16[64,128]{1,0:T(8,128)(2,1)S(1)}, bf16[64,128]{1,0:T(8,128)(2,1)S(1)}, u32[]{:S(2)}, u32[]{:S(2)}) collective-permute-start(bf16[64,128]{1,0:T(8,128)(2,1)S(1)} %get-tuple-element.45), channel_id=1, source_target_pairs={{0,24},{4,12},{8,0},{12,20},{16,8},{20,28},{24,16},{28,4},{1,25},{... | collective-permute-start | bytes 49160 | tf_op jit(solution)/shard_map/ppermute | solution.py:473
  19.0 12.7 %copy-start.2 = (f32[128]{0:T(128)S(1)}, f32[128]{0:T(128)}, u32[]{:S(2)}) copy-start(f32[128]{0:T(128)} %param.13) | copy-start | bytes 1540
  23.5 8.2 %collective-permute-start.6 = (bf16[320,128]{1,0:T(8,128)(2,1)S(1)}, bf16[320,128]{1,0:T(8,128)(2,1)S(1)}, u32[]{:S(2)}, u32[]{:S(2)}) collective-permute-start(bf16[320,128]{1,0:T(8,128)(2,1)S(1)} %get-tuple-element.54), channel_id=1, source_target_pairs={{0,28},{4,8},{8,4},{12,16},{16,12},{20,24},{24,20},{28,0},{1,29},{... | collective-permute-start | bytes 245768 | tf_op jit(solution)/shard_map/ppermute | solution.py:473
  25.9 5.7 %collective-permute-start.7 = (bf16[320,128]{1,0:T(8,128)(2,1)S(1)}, bf16[320,128]{1,0:T(8,128)(2,1)S(1)}, u32[]{:S(2)}, u32[]{:S(2)}) collective-permute-start(bf16[320,128]{1,0:T(8,128)(2,1)S(1)} %get-tuple-element.55), channel_id=1, source_target_pairs={{0,4},{4,0},{8,12},{12,8},{16,20},{20,16},{24,28},{28,24},{1,5},{5... | collective-permute-start | bytes 245768 | tf_op jit(solution)/shard_map/ppermute | solution.py:473
  26.1 5.5 %collective-permute-start.8 = (bf16[64,128]{1,0:T(8,128)(2,1)S(1)}, bf16[64,128]{1,0:T(8,128)(2,1)S(1)}, u32[]{:S(2)}, u32[]{:S(2)}) collective-permute-start(bf16[64,128]{1,0:T(8,128)(2,1)S(1)} %get-tuple-element.56), channel_id=1, source_target_pairs={{0,8},{4,28},{8,16},{12,4},{16,24},{20,12},{24,0},{28,20},{1,9},{5... | collective-permute-start | bytes 49160 | tf_op jit(solution)/shard_map/ppermute | solution.py:473
  26.8 4.9 %collective-permute-start.9 = (bf16[64,128]{1,0:T(8,128)(2,1)S(1)}, bf16[64,128]{1,0:T(8,128)(2,1)S(1)}, u32[]{:S(2)}, u32[]{:S(2)}) collective-permute-start(bf16[64,128]{1,0:T(8,128)(2,1)S(1)} %get-tuple-element.57), channel_id=1, source_target_pairs={{0,24},{4,12},{8,0},{12,20},{16,8},{20,28},{24,16},{28,4},{1,25},{... | collective-permute-start | bytes 49160 | tf_op jit(solution)/shard_map/ppermute | solution.py:473
  32.2 3.0 %collective-permute-start.12 = (f32[1,637]{1,0:T(1,128)S(1)}, f32[1,637]{1,0:T(1,128)S(1)}, u32[]{:S(2)}, u32[]{:S(2)}) collective-permute-start(f32[1,637]{1,0:T(1,128)S(1)} %get-tuple-element.63), channel_id=1, source_target_pairs={{0,3},{1,2},{2,1},{3,0},{4,7},{5,6},{6,5},{7,4},{8,11},{9,10},{10,... | collective-permute-start | bytes 7652 | tf_op jit(solution)/shard_map/ppermute | solution.py:576
  32.2 3.7 %collective-permute-start.11 = (f32[1,637]{1,0:T(1,128)S(1)}, f32[1,637]{1,0:T(1,128)S(1)}, u32[]{:S(2)}, u32[]{:S(2)}) collective-permute-start(f32[1,637]{1,0:T(1,128)S(1)} %get-tuple-element.63), channel_id=1, source_target_pairs={{0,2},{1,3},{2,0},{3,1},{4,6},{5,7},{6,4},{7,5},{8,10},{9,11},{10,... | collective-permute-start | bytes 7652 | tf_op jit(solution)/shard_map/ppermute | solution.py:576
  33.8 2.1 %collective-permute-start.10 = (f32[1,637]{1,0:T(1,128)S(1)}, f32[1,637]{1,0:T(1,128)S(1)}, u32[]{:S(2)}, u32[]{:S(2)}) collective-permute-start(f32[1,637]{1,0:T(1,128)S(1)} %get-tuple-element.63), channel_id=1, source_target_pairs={{0,1},{1,0},{2,3},{3,2},{4,5},{5,4},{6,7},{7,6},{8,9},{9,8},{10,11... | collective-permute-start | bytes 7652 | tf_op jit(solution)/shard_map/ppermute | solution.py:576
